TPU v7x, 32 devices: a whole 2x2x4 slice. The times are simulated.
32 devices in a mesh: batch: 8 (over z, y), tier: 4 (over x, core).
Axes of the slice: x: 2, y: 2, z: 4, core: 2. Of those that a mesh axis runs over, the one named last changes fastest.
Arguments:
- segment: bfloat16 [32, 192, 1024], P('batch', 'tier'), may hold values from -6 to 6
- memory: bfloat16 [32, 192, 1024], P('batch', 'tier'), may hold values from -8 to 8
- compressed: bfloat16 [32, 192, 1024], P('batch', 'tier'), may hold values from -6 to 6
- evicted: int32 [32], P('batch'), may hold values from 48 to 192, as said below
- window_mask: int32 [32, 64], P('batch', 'tier'), may hold values 0 or 1
- cotangent: bfloat16 [32, 192, 1024], P('batch', 'tier'), may hold values from -6 to 6
- w_query: bfloat16 [1024, 1024], P(('batch', 'tier')), may hold values from -0.1875 to 0.1875
- w_key: bfloat16 [1024, 1024], P(('batch', 'tier')), may hold values from -0.1875 to 0.1875
- w_value: bfloat16 [1024, 1024], P(('batch', 'tier')), may hold values from -0.1875 to 0.1875
- w_output: bfloat16 [1024, 1024], P(('batch', 'tier')), may hold values from -0.375 to 0.375
- w_up: bfloat16 [1024, 4096], P(('batch', 'tier')), may hold values from -0.1875 to 0.1875
- b_up: bfloat16 [4096], P(('batch', 'tier')), may hold values from -3 to 3
- w_down: bfloat16 [4096, 1024], P(('batch', 'tier')), may hold values from -0.09375 to 0.09375
- b_down: bfloat16 [1024], P(('batch', 'tier')), may hold values from -3 to 3
- ln_gain: bfloat16 [1024], P(('batch', 'tier')), may hold values from 0.5 to 1.5
- ln_bias: bfloat16 [1024], P(('batch', 'tier')), may hold values from -3 to 3
- w_conv: bfloat16 [3, 1024, 1024], P(None, ('batch', 'tier')), may hold values from -0.109375 to 0.109375
- b_conv: bfloat16 [1024], P(('batch', 'tier')), may hold values from -3 to 3
- slopes: float32 [8], replicated, may hold values from 0.5 to 4
Outputs:
- output: bfloat16 [32, 192, 1024], P('batch', 'tier')
- input_grad: float32 [32, 192, 1024], P('batch', 'tier')
- new_memory: bfloat16 [32, 192, 1024], P('batch', 'tier')
- new_compressed: bfloat16 [32, 192, 1024], P('batch', 'tier')
- grad_query: float32 [1024, 1024], P(('batch', 'tier'))
- grad_key: float32 [1024, 1024], P(('batch', 'tier'))
- grad_value: float32 [1024, 1024], P(('batch', 'tier'))
- grad_output: float32 [1024, 1024], P(('batch', 'tier'))
- grad_up: float32 [1024, 4096], P(('batch', 'tier'))
- grad_up_bias: float32 [4096], P(('batch', 'tier'))
- grad_down: float32 [4096, 1024], P(('batch', 'tier'))
- grad_down_bias: float32 [1024], P(('batch', 'tier'))
- grad_gain: float32 [1024], P(('batch', 'tier'))
- grad_bias: float32 [1024], P(('batch', 'tier'))
- grad_conv: float32 [3, 1024, 1024], P(None, ('batch', 'tier'))
- grad_conv_bias: float32 [1024], P(('batch', 'tier'))
- grad_slopes: float32 [8], replicated
Inputs may be any that keep to these rules, and one draw needn't show every extreme that they name: In each aligned block of 4 sequences one has exactly 192 evicted slots.
All inputs are finite; a program needn't handle non-finite values. No bound on the sum of `window_mask` on one device may be relied on, other than what follows from the above.
Results may differ from a plain program's by a relative error of at most 0.015.
Values may be sent and summed in bfloat16 or wider, within the bound.
A program may use at most 192 MiB of HBM per device.

v0:
```python
import math

import jax
import jax.numpy as jnp
from jax import lax
from jax.sharding import PartitionSpec as P

masked_value = -1e30
norm_eps = 1e-05


def merged(part, axis, combine):
    gathered = jax.tree.map(lambda a: lax.all_gather(a, axis), part)

    def take(source):
        return jax.tree.map(lambda a: lax.dynamic_index_in_dim(a, source, 0, False), gathered)

    return lax.fori_loop(
        1, lax.axis_size(axis), lambda source, state: combine(state, take(source)), take(0)
    )


def layer_norm(resid, ln_gain, ln_bias):
    center = resid - jnp.mean(resid, axis=-1, keepdims=True)
    spread = lax.rsqrt(jnp.mean(center * center, axis=-1, keepdims=True) + norm_eps)
    return center * spread * ln_gain + ln_bias


def gelu_exact(inputs):
    return jax.nn.gelu(inputs, approximate=False)


def inner_rows(left, right):
    return lax.dot_general(
        left, right, (((0,), (0,)), ((), ())), preferred_element_type=jnp.float32
    )


def times_back(left, right):
    return lax.dot_general(
        left, right, (((1,), (1,)), ((), ())), preferred_element_type=jnp.float32
    )


def merge_stats(earlier, later):
    highest = jnp.maximum(earlier[0], later[0])
    summed = earlier[1] * jnp.exp(earlier[0] - highest) + later[1] * jnp.exp(later[0] - highest)
    return (highest, summed)


def dense_block(
    flat_segment,
    flat_mixed,
    cot_low,
    full_output,
    full_up,
    full_upbias,
    full_down,
    full_downbias,
    full_gain,
    full_bias,
):
    resid = flat_segment.astype(jnp.float32) + jnp.dot(
        flat_mixed, full_output, preferred_element_type=jnp.float32
    )
    normed, norm_back = jax.vjp(layer_norm, resid, full_gain, full_bias)
    normed_low = normed.astype(jnp.bfloat16)
    pre_act = jnp.dot(normed_low, full_up, preferred_element_type=jnp.float32) + full_upbias
    activ, gelu_back = jax.vjp(gelu_exact, pre_act)
    act_low = activ.astype(jnp.bfloat16)
    final = resid + jnp.dot(act_low, full_down, preferred_element_type=jnp.float32) + full_downbias
    output_low = final.astype(jnp.bfloat16)
    cot_float = cot_low.astype(jnp.float32)
    grad_down = inner_rows(act_low, cot_low)
    grad_downbias = jnp.sum(cot_float, axis=0)
    d_act = times_back(cot_low, full_down).astype(jnp.bfloat16)
    d_pre = gelu_back(d_act.astype(jnp.float32))[0]
    grad_upbias = jnp.sum(d_pre, axis=0)
    d_pre_low = d_pre.astype(jnp.bfloat16)
    grad_up = inner_rows(normed_low, d_pre_low)
    d_normed = times_back(d_pre_low, full_up).astype(jnp.bfloat16)
    d_resid_norm, grad_gain, grad_bias = norm_back(d_normed.astype(jnp.float32))
    d_resid = cot_float + d_resid_norm
    d_branch = d_resid.astype(jnp.bfloat16)
    grad_output = inner_rows(flat_mixed, d_branch)
    d_mixed = times_back(d_branch, full_output).astype(jnp.bfloat16)
    return (
        output_low,
        d_resid,
        d_mixed,
        (grad_output, grad_up, grad_upbias, grad_down, grad_downbias, grad_gain, grad_bias),
    )


def per_device(
    segment,
    memory,
    compressed,
    evicted,
    window_mask,
    cotangent,
    w_query,
    w_key,
    w_value,
    w_output,
    w_up,
    b_up,
    w_down,
    b_down,
    ln_gain,
    ln_bias,
    w_conv,
    b_conv,
    slopes,
):
    head_count = slopes.shape[0]
    seq_count, row_count, model_width = segment.shape
    head_dim = model_width // head_count
    tier_count = lax.axis_size("tier")
    tier_index = lax.axis_index("tier")
    seg_len = row_count * tier_count
    ctx_scale = 1.0 / (3 * seg_len)
    window_count = row_count // 3
    all_windows = seg_len // 3
    slot_offset = seg_len - all_windows
    score_scale = 1.0 / math.sqrt(head_dim)
    (
        full_query,
        full_key,
        full_value,
        full_output,
        full_up,
        full_upbias,
        full_down,
        full_downbias,
        full_gain,
        full_bias,
        full_conv,
        full_convbias,
    ) = (
        lax.all_gather(w_query, ("batch", "tier"), axis=0, tiled=True),
        lax.all_gather(w_key, ("batch", "tier"), axis=0, tiled=True),
        lax.all_gather(w_value, ("batch", "tier"), axis=0, tiled=True),
        lax.all_gather(w_output, ("batch", "tier"), axis=0, tiled=True),
        lax.all_gather(w_up, ("batch", "tier"), axis=0, tiled=True),
        lax.all_gather(b_up, ("batch", "tier"), axis=0, tiled=True),
        lax.all_gather(w_down, ("batch", "tier"), axis=0, tiled=True),
        lax.all_gather(b_down, ("batch", "tier"), axis=0, tiled=True),
        lax.all_gather(ln_gain, ("batch", "tier"), axis=0, tiled=True),
        lax.all_gather(ln_bias, ("batch", "tier"), axis=0, tiled=True),
        lax.all_gather(w_conv, ("batch", "tier"), axis=1, tiled=True),
        lax.all_gather(b_conv, ("batch", "tier"), axis=0, tiled=True),
    )
    full_upbias = full_upbias.astype(jnp.float32)
    full_downbias = full_downbias.astype(jnp.float32)
    full_gain = full_gain.astype(jnp.float32)
    full_bias = full_bias.astype(jnp.float32)
    full_convbias = full_convbias.astype(jnp.float32)
    dense_weights = (
        full_output,
        full_up,
        full_upbias,
        full_down,
        full_downbias,
        full_gain,
        full_bias,
    )
    local_rows = jnp.arange(row_count, dtype=jnp.int32) + tier_index * row_count
    group_count = seq_count // 2
    key_pos = jnp.concatenate([local_rows, local_rows + seg_len, local_rows + 2 * seg_len])
    query_pos = jnp.arange(seg_len, dtype=jnp.int32) + 2 * seg_len
    allowed = key_pos[None, :] <= query_pos[:, None]
    distance = (query_pos[:, None] - key_pos[None, :]).astype(jnp.float32) * ctx_scale
    bias_table = -slopes[:, None, None] * distance[None]
    context = jnp.concatenate([compressed, memory, segment], axis=1)
    flat_context = context.reshape(-1, model_width)
    flat_segment = segment.reshape(-1, model_width)
    key_rows = jnp.dot(flat_context, full_key, preferred_element_type=jnp.float32).astype(
        jnp.bfloat16
    )
    value_rows = jnp.dot(flat_context, full_value, preferred_element_type=jnp.float32).astype(
        jnp.bfloat16
    )
    query_rows = jnp.dot(flat_segment, full_query, preferred_element_type=jnp.float32).astype(
        jnp.bfloat16
    )
    all_queries = lax.all_gather(
        query_rows.reshape(seq_count, row_count, model_width), "tier", axis=1, tiled=True
    )
    q_groups = all_queries.reshape(group_count, 2, seg_len, head_count, head_dim)
    k_groups = key_rows.reshape(group_count, 2, 3 * row_count, head_count, head_dim)
    v_groups = value_rows.reshape(group_count, 2, 3 * row_count, head_count, head_dim)

    def fresh_scores(q_block, k_block):
        raw = jnp.einsum("sqhd,skhd->shqk", q_block, k_block, preferred_element_type=jnp.float32)
        return jnp.where(allowed, raw * score_scale + bias_table, masked_value)

    def row_stats_of(scores):
        highest = jnp.max(scores, axis=-1)
        return (highest, jnp.sum(jnp.exp(scores - highest[..., None]), axis=-1))

    def mix_of(scores, log_total, v_block):
        probs = jnp.exp(scores - log_total[..., None]).astype(jnp.bfloat16)
        return jnp.einsum("shqk,skhd->sqhd", probs, v_block, preferred_element_type=jnp.float32)

    def stats_only(items):
        return row_stats_of(fresh_scores(items[0], items[1]))

    highest, summed = lax.map(stats_only, (q_groups, k_groups))
    highest, summed = merged((highest, summed), "tier", merge_stats)
    log_total = highest + jnp.log(summed)

    def mix_again(items):
        return mix_of(fresh_scores(items[0], items[1]), items[2], items[3])

    mix_parts = lax.map(mix_again, (q_groups, k_groups, log_total, v_groups))
    mixed = lax.psum_scatter(
        mix_parts.reshape(seq_count, seg_len, model_width), "tier", scatter_dimension=1, tiled=True
    ).astype(jnp.bfloat16)
    flat_mixed = mixed.reshape(-1, model_width)
    output_low, d_resid, d_mixed_flat, dense_grads = dense_block(
        flat_segment, flat_mixed, cotangent.reshape(-1, model_width), *dense_weights
    )
    output = output_low.reshape(seq_count, row_count, model_width)
    d_mixed = d_mixed_flat.reshape(seq_count, row_count, model_width)
    all_dmixed = lax.all_gather(d_mixed, "tier", axis=1, tiled=True)
    dm_groups = all_dmixed.reshape(group_count, 2, seg_len, head_count, head_dim)

    def probs_and_grads(scores, log_total_block, dm_block, v_block):
        probs = jnp.exp(scores - log_total_block[..., None])
        d_probs = jnp.einsum(
            "sqhd,skhd->shqk", dm_block, v_block, preferred_element_type=jnp.float32
        )
        return (probs, d_probs)

    def grads_of(probs, d_probs, delta_block, q_block, k_block, dm_block):
        d_scores = probs * (d_probs - delta_block[..., None])
        slope_part = -jnp.sum(d_scores * distance[None, None], axis=(0, 2, 3))
        d_raw = (d_scores * score_scale).astype(jnp.bfloat16)
        d_query_part = jnp.einsum(
            "shqk,skhd->sqhd", d_raw, k_block, preferred_element_type=jnp.float32
        )
        d_key_part = jnp.einsum(
            "shqk,sqhd->skhd", d_raw, q_block, preferred_element_type=jnp.float32
        ).astype(jnp.bfloat16)
        d_value_part = jnp.einsum(
            "shqk,sqhd->skhd",
            probs.astype(jnp.bfloat16),
            dm_block,
            preferred_element_type=jnp.float32,
        ).astype(jnp.bfloat16)
        return (d_query_part, d_key_part, d_value_part, slope_part)

    def dots_again(items):
        probs, d_probs = probs_and_grads(
            fresh_scores(items[0], items[1]), items[2], items[3], items[4]
        )
        return jnp.sum(probs * d_probs, axis=-1)

    delta_part = lax.map(dots_again, (q_groups, k_groups, log_total, dm_groups, v_groups))
    delta = lax.psum(delta_part, "tier")

    def grads_again(items):
        probs, d_probs = probs_and_grads(
            fresh_scores(items[0], items[1]), items[2], items[3], items[4]
        )
        return grads_of(probs, d_probs, items[5], items[0], items[1], items[3])

    d_query_parts, d_keys, d_values, slope_parts = lax.map(
        grads_again, (q_groups, k_groups, log_total, dm_groups, v_groups, delta)
    )
    d_query = lax.psum_scatter(
        d_query_parts.reshape(seq_count, seg_len, model_width),
        "tier",
        scatter_dimension=1,
        tiled=True,
    ).astype(jnp.bfloat16)
    flat_dquery = d_query.reshape(-1, model_width)
    d_keys = d_keys.reshape(seq_count, 3 * row_count, model_width)
    d_values = d_values.reshape(seq_count, 3 * row_count, model_width)
    grad_query = inner_rows(flat_segment, flat_dquery)
    grad_key = inner_rows(flat_context, d_keys.reshape(-1, model_width))
    grad_value = inner_rows(flat_context, d_values.reshape(-1, model_width))
    seg_dkeys = d_keys[:, 2 * row_count :, :].reshape(-1, model_width)
    seg_dvalues = d_values[:, 2 * row_count :, :].reshape(-1, model_width)
    input_grad = (
        d_resid
        + times_back(flat_dquery, full_query)
        + times_back(seg_dkeys, full_key)
        + times_back(seg_dvalues, full_value)
    )
    input_grad = input_grad.reshape(seq_count, row_count, model_width)
    grad_output, grad_up, grad_upbias, grad_down, grad_downbias, grad_gain, grad_bias = dense_grads
    win_rows = memory.reshape(seq_count * window_count, 3 * model_width)
    conv_out = (
        jnp.dot(
            win_rows,
            full_conv.reshape(3 * model_width, model_width),
            preferred_element_type=jnp.float32,
        )
        + full_convbias
    )
    pooled = jnp.mean(
        memory.astype(jnp.float32).reshape(seq_count * window_count, 3, model_width), axis=1
    )
    window_index = jnp.arange(window_count, dtype=jnp.int32) + tier_index * window_count
    live = jnp.where(3 * window_index[None, :] + 3 <= evicted[:, None], window_mask, 0).astype(
        jnp.float32
    )
    d_conv = live.reshape(-1, 1) * (conv_out - pooled)
    grad_convbias = jnp.sum(d_conv, axis=0)
    grad_conv = inner_rows(win_rows, d_conv.astype(jnp.bfloat16)).reshape(
        3, model_width, model_width
    )
    new_rows = (
        (window_mask.astype(jnp.float32).reshape(-1, 1) * conv_out)
        .astype(jnp.bfloat16)
        .reshape(seq_count, window_count, model_width)
    )
    all_new = lax.all_gather(new_rows, "tier", axis=1, tiled=True)
    padded = jnp.concatenate(
        [jnp.zeros((seq_count, slot_offset, model_width), jnp.bfloat16), all_new], axis=1
    )
    slot_rows = lax.dynamic_slice_in_dim(padded, tier_index * row_count, row_count, 1)
    written = (local_rows[None, :] >= slot_offset) & (
        3 * (local_rows[None, :] - slot_offset) + 3 <= evicted[:, None]
    )
    new_compressed = jnp.where(written[..., None], slot_rows, compressed)
    new_memory = jnp.where((local_rows[None, :] < evicted[:, None])[..., None], segment, memory)
    summed_grads = (
        lax.psum_scatter(grad_query, ("batch", "tier"), scatter_dimension=0, tiled=True),
        lax.psum_scatter(grad_key, ("batch", "tier"), scatter_dimension=0, tiled=True),
        lax.psum_scatter(grad_value, ("batch", "tier"), scatter_dimension=0, tiled=True),
        lax.psum_scatter(grad_output, ("batch", "tier"), scatter_dimension=0, tiled=True),
        lax.psum_scatter(grad_up, ("batch", "tier"), scatter_dimension=0, tiled=True),
        lax.psum_scatter(grad_upbias, ("batch", "tier"), scatter_dimension=0, tiled=True),
        lax.psum_scatter(grad_down, ("batch", "tier"), scatter_dimension=0, tiled=True),
        lax.psum_scatter(grad_downbias, ("batch", "tier"), scatter_dimension=0, tiled=True),
        lax.psum_scatter(grad_gain, ("batch", "tier"), scatter_dimension=0, tiled=True),
        lax.psum_scatter(grad_bias, ("batch", "tier"), scatter_dimension=0, tiled=True),
        lax.psum_scatter(grad_conv, ("batch", "tier"), scatter_dimension=1, tiled=True),
        lax.psum_scatter(grad_convbias, ("batch", "tier"), scatter_dimension=0, tiled=True),
    )
    grad_slopes = lax.psum(jnp.sum(slope_parts, axis=0), ("batch", "tier"))
    return (
        output,
        input_grad,
        new_memory,
        new_compressed,
        summed_grads[0],
        summed_grads[1],
        summed_grads[2],
        summed_grads[3],
        summed_grads[4],
        summed_grads[5],
        summed_grads[6],
        summed_grads[7],
        summed_grads[8],
        summed_grads[9],
        summed_grads[10],
        summed_grads[11],
        grad_slopes,
    )


def solution(mesh):
    return jax.shard_map(
        per_device,
        mesh=mesh,
        in_specs=(
            P("batch", "tier", None),
            P("batch", "tier", None),
            P("batch", "tier", None),
            P("batch"),
            P("batch", "tier"),
            P("batch", "tier", None),
            P(("batch", "tier"), None),
            P(("batch", "tier"), None),
            P(("batch", "tier"), None),
            P(("batch", "tier"), None),
            P(("batch", "tier"), None),
            P(("batch", "tier")),
            P(("batch", "tier"), None),
            P(("batch", "tier")),
            P(("batch", "tier")),
            P(("batch", "tier")),
            P(None, ("batch", "tier"), None),
            P(("batch", "tier")),
            P(),
        ),
        out_specs=(
            P("batch", "tier", None),
            P("batch", "tier", None),
            P("batch", "tier", None),
            P("batch", "tier", None),
            P(("batch", "tier"), None),
            P(("batch", "tier"), None),
            P(("batch", "tier"), None),
            P(("batch", "tier"), None),
            P(("batch", "tier"), None),
            P(("batch", "tier")),
            P(("batch", "tier"), None),
            P(("batch", "tier")),
            P(("batch", "tier")),
            P(("batch", "tier")),
            P(None, ("batch", "tier"), None),
            P(("batch", "tier")),
            P(),
        ),
        check_vma=False,
    )
```

profile of v0, /device:TPU:11, one launch (start us, length us, event | category | flops | bytes accessed | tf_op | source)
XLA Modules:
  0.0 1794.6 jit_solution(13457536781898684183)
XLA Ops:
  9.5 58.5 %all-gather.15.cloned.1.call-done = bf16[1024,1024]{1,0:T(8,128)(2,1)} async-done(((bf16[32,1024]{1,0:T(8,128)(2,1)}), bf16[1024,1024]{1,0:T(8,128)(2,1)}) %all-gather.15.cloned.1.call-update) | async-done | bytes 2097168 | tf_op jit(solution)/shard_map/all_gather | solution.py:141
  71.9 54.1 %all-gather.19.cloned.1.call-done = bf16[1024,1024]{1,0:T(8,128)(2,1)} async-done(((bf16[32,1024]{1,0:T(8,128)(2,1)}), bf16[1024,1024]{1,0:T(8,128)(2,1)}) %all-gather.19.cloned.1.call-update) | async-done | bytes 2097168 | tf_op jit(solution)/shard_map/all_gather | solution.py:142
  129.6 54.6 %all-gather.13.cloned.1.call-done = bf16[1024,1024]{1,0:T(8,128)(2,1)} async-done(((bf16[32,1024]{1,0:T(8,128)(2,1)}), bf16[1024,1024]{1,0:T(8,128)(2,1)}) %all-gather.13.cloned.1.call-update) | async-done | bytes 2097168 | tf_op jit(solution)/shard_map/all_gather | solution.py:143
  188.7 16.1 all-gather.17.cloned.1.call-done
  210.4 5.5 all-gather
  226.3 17.4 while.72
  251.4 40.1 %all-reduce.11 = (bf16[1024]{0:T(1024)(128)(2,1)S(1)}, bf16[1024]{0:T(1024)(128)(2,1)S(1)}, bf16[1024]{0:T(1024)(128)(2,1)}, bf16[1024]{0:T(1024)(128)(2,1)S(1)}) all-reduce(bf16[1024]{0:T(1024)(128)(2,1)S(1)} %dynamic-update-slice.1, bf16[1024]{0:T(1024)(128)(2,1)S(1)} %dynamic-update-slice, ...), channel_id=1, replica_groups=mesh['batch'=8,'tier'=4] {'batch','tier'}, use_global_device_ids=true, to_apply=%add.2 | all-reduce | flops 4096 | bytes 16384
  291.5 31.2 %all-gather.2 = bf16[32,1,128]{2,1,0:T(2,128)(2,1)S(1)} all-gather(bf16[1,1,128]{2,1,0:T(2,128)(2,1)S(1)} %bitcast.281), channel_id=1, replica_groups=mesh['batch'=8,'tier'=4] {'batch','tier'}, dimensions={0}, use_global_device_ids=true | all-gather | bytes 8448 | tf_op jit(solution)/shard_map/all_gather | solution.py:146
  324.7 21.4 %all-gather.21.cloned.1.call-done = bf16[1024,1024]{1,0:T(8,128)(2,1)} async-done(((bf16[32,1024]{1,0:T(8,128)(2,1)}), bf16[1024,1024]{1,0:T(8,128)(2,1)}) %all-gather.21.cloned.1.call-update) | async-done | bytes 2097168 | tf_op jit(solution)/shard_map/all_gather | solution.py:144
  349.6 77.0 %all-gather.23.cloned.1.call-done = bf16[1024,4096]{1,0:T(8,128)(2,1)} async-done(((bf16[32,4096]{1,0:T(8,128)(2,1)}), bf16[1024,4096]{1,0:T(8,128)(2,1)}) %all-gather.23.cloned.1.call-update) | async-done | bytes 8388624 | tf_op jit(solution)/shard_map/all_gather | solution.py:145
  426.6 13.0 multiply_convert_fusion.3
  439.6 66.3 %all-gather.25.cloned.1.call-done = bf16[4096,1024]{1,0:T(8,128)(2,1)} async-done(((bf16[128,1024]{1,0:T(8,128)(2,1)}), bf16[4096,1024]{1,0:T(8,128)(2,1)}) %all-gather.25.cloned.1.call-update) | async-done | bytes 8388624 | tf_op jit(solution)/shard_map/all_gather | solution.py:147
  505.9 9.2 fusion.106
  523.2 17.2 all-gather.27.cloned.1.call-done
  543.8 5.6 while.73
  549.4 10.2 psum.14
  561.4 21.7 %while.74 = (s32[]{:T(128)}, f32[2,2,192,8,128]{4,3,2,1,0:T(8,128)}, bf16[2,2,144,8,128]{4,3,2,1,0:T(8,128)(2,1)}, bf16[2,2,144,8,128]{4,3,2,1,0:T(8,128)(2,1)},...) while((s32[]{:T(128)}, ...), condition=%wide.region_19.20_spmd.clone.clone, body=%wide.region_17.19_spmd.clone.clone.sunk | while | flops 572903424 | bytes 83783904 | solution.py:269
  602.5 24.1 %reduce-scatter.14.cloned.1.call-done = f32[4,48,1024]{2,1,0:T(8,128)} async-done(((f32[4,192,1024]{2,1,0:T(8,128)}), f32[4,48,1024]{2,1,0:T(8,128)}) %reduce-scatter.14.cloned.1.call-update) | async-done | bytes 786448 | tf_op jit(solution)/shard_map/reduce_scatter | solution.py:272
  638.5 61.9 %all-gather.29.cloned.1.call-done = bf16[3,1024,1024]{2,1,0:T(8,128)(2,1)} async-done(((bf16[3,32,1024]{2,1,0:T(8,128)(2,1)}), bf16[3,1024,1024]{2,1,0:T(8,128)(2,1)}) %all-gather.29.cloned.1.call-update) | async-done | bytes 6291472 | tf_op jit(solution)/shard_map/all_gather | solution.py:151
  704.4 6.5 convolution_bitcast_fusion.2
  710.9 12.7 copy.83
  725.2 8.3 fusion.94
  734.4 9.6 fusion.108
  745.7 9.2 all_gather.75
  755.8 6.6 fusion.87
  767.0 39.0 %all-reduce.10 = (f32[4096]{0:T(1024)S(1)}, f32[1024]{0:T(1024)S(1)}, f32[1024]{0:T(1024)S(1)}, f32[1024]{0:T(1024)S(1)}, f32[1024]{0:T(1024)S(1)}, /*index=5*/f32[8]{0:T(128)}) all-reduce(f32[4096]{0:T(1024)S(1)} %get-tuple-element.849, ...), channel_id=11, replica_groups=mesh['batch'=8,'tier'=4] {'batch','tier'}, use_global_device_ids=true, to_apply=%region_27.28.clone | all-reduce | flops 8200 | bytes 65600
  814.4 138.7 %reduce-scatter.16.cloned.1.call-done = f32[32,1024]{1,0:T(8,128)} async-done(((f32[1024,1024]{1,0:T(8,128)}), f32[32,1024]{1,0:T(8,128)}) %reduce-scatter.16.cloned.1.call-update) | async-done | bytes 131088 | tf_op jit(solution)/shard_map/reduce_scatter | solution.py:332
  953.1 139.0 %reduce-scatter.18.cloned.1.call-done = f32[32,1024]{1,0:T(8,128)} async-done(((f32[1024,1024]{1,0:T(8,128)}), f32[32,1024]{1,0:T(8,128)}) %reduce-scatter.18.cloned.1.call-update) | async-done | bytes 131088 | tf_op jit(solution)/shard_map/reduce_scatter | solution.py:333
  1092.1 139.6 %reduce-scatter.28.cloned.1.call-done = f32[32,1024]{1,0:T(8,128)} async-done(((f32[1024,1024]{1,0:T(8,128)}), f32[32,1024]{1,0:T(8,128)}) %reduce-scatter.28.cloned.1.call-update) | async-done | bytes 131088
  1231.7 167.8 %reduce-scatter.26.cloned.1.call-done = f32[3,32,1024]{2,1,0:T(8,128)} async-done(((f32[3,1024,1024]{2,1,0:T(8,128)}), f32[3,32,1024]{2,1,0:T(8,128)}) %reduce-scatter.26.cloned.1.call-update) | async-done | bytes 393232 | tf_op jit(solution)/shard_map/reduce_scatter | solution.py:341
  1399.5 200.6 %reduce-scatter.22.cloned.1.call-done = f32[32,4096]{1,0:T(8,128)} async-done(((f32[1024,4096]{1,0:T(8,128)}), f32[32,4096]{1,0:T(8,128)}) %reduce-scatter.22.cloned.1.call-update) | async-done | bytes 524304 | tf_op jit(solution)/shard_map/reduce_scatter | solution.py:335
  1600.1 187.2 %reduce-scatter.24.cloned.1.call-done = f32[128,1024]{1,0:T(8,128)} async-done(((f32[4096,1024]{1,0:T(8,128)}), f32[128,1024]{1,0:T(8,128)}) %reduce-scatter.24.cloned.1.call-update) | async-done | bytes 524304 | tf_op jit(solution)/shard_map/reduce_scatter | solution.py:337
  (317 shorter events, 159.5 us)
Async XLA Ops:
  7.2 64.5 %copy-start.15 = (bf16[4,48,1024]{2,1,0:T(8,128)(2,1)S(1)}, bf16[4,48,1024]{2,1,0:T(8,128)(2,1)}, u32[]{:S(2)}) copy-start(bf16[4,48,1024]{2,1,0:T(8,128)(2,1)} %param.29) | copy-start | bytes 1179652
  7.2 63.9 %copy-start.47 = (f32[8]{0:T(128)S(1)}, f32[8]{0:T(128)}, u32[]{:S(2)}) copy-start(f32[8]{0:T(128)} %param.47) | copy-start | bytes 100
  7.2 64.5 %copy-start.13 = (bf16[4,48,1024]{2,1,0:T(8,128)(2,1)S(1)}, bf16[4,48,1024]{2,1,0:T(8,128)(2,1)}, u32[]{:S(2)}) copy-start(bf16[4,48,1024]{2,1,0:T(8,128)(2,1)} %param.30) | copy-start | bytes 1179652
  7.2 64.5 %copy-start.24 = (bf16[4,48,1024]{2,1,0:T(8,128)(2,1)S(1)}, bf16[4,48,1024]{2,1,0:T(8,128)(2,1)}, u32[]{:S(2)}) copy-start(bf16[4,48,1024]{2,1,0:T(8,128)(2,1)} %param.31) | copy-start | bytes 1179652
  7.2 60.7 %all-gather.15.cloned.1.call-start = ((), (), s32[]{:S(2)}) async-start(), calls=%async_computation.10 | async-start | bytes 2162688 | tf_op jit(solution)/shard_map/all_gather | solution.py:141
  8.0 118.1 %all-gather.19.cloned.1.call-start = ((), (), s32[]{:S(2)}) async-start(), calls=%async_computation.12 | async-start | bytes 2162688 | tf_op jit(solution)/shard_map/all_gather | solution.py:142
  8.7 175.5 %all-gather.13.cloned.1.call-start = ((), (), s32[]{:S(2)}) async-start(), calls=%async_computation.9 | async-start | bytes 2162688 | tf_op jit(solution)/shard_map/all_gather | solution.py:143
  9.4 195.3 %all-gather.17.cloned.1.call-start = ((), (), s32[]{:S(2)}) async-start(), calls=%async_computation.11 | async-start | bytes 1966080 | tf_op jit(solution)/shard_map/all_gather | solution.py:187
  71.0 251.7 %reduce-scatter.12.cloned.1.call-start = ((), (), s32[]{:S(2)}) async-start(), calls=%async_computation.13 | async-start | bytes 3932160 | tf_op jit(solution)/shard_map/reduce_scatter | solution.py:217
  71.6 57.4 %copy-start.42 = (s32[48]{0:T(128)}, s32[48]{0:T(128)S(1)}, u32[]{:S(2)}) copy-start(s32[48]{0:T(128)S(1)} %get-tuple-element.852) | copy-start | bytes 580
  71.8 112.4 %copy-start.29 = (bf16[4,144,1024]{2,1,0:T(8,128)(2,1)}, bf16[4,144,1024]{2,1,0:T(8,128)(2,1)S(1)}, u32[]{:S(2)}) copy-start(bf16[4,144,1024]{2,1,0:T(8,128)(2,1)S(1)} %pad_maximum_fusion) | copy-start | bytes 3538948
  248.3 43.2 %copy-start.44 = (bf16[128]{0:T(256)(128)(2,1)S(1)}, bf16[128]{0:T(256)(128)(2,1)}, u32[]{:S(2)}) copy-start(bf16[128]{0:T(256)(128)(2,1)} %param.40) | copy-start | bytes 772
  248.3 97.8 %all-gather.21.cloned.1.call-start = ((), (), s32[]{:S(2)}) async-start(), calls=%async_computation.14 | async-start | bytes 2162688 | tf_op jit(solution)/shard_map/all_gather | solution.py:144
  248.9 177.7 %all-gather.23.cloned.1.call-start = ((), (), s32[]{:S(2)}) async-start(), calls=%async_computation.15 | async-start | bytes 8650752 | tf_op jit(solution)/shard_map/all_gather | solution.py:145
  249.6 256.3 %all-gather.25.cloned.1.call-start = ((), (), s32[]{:S(2)}) async-start(), calls=%async_computation.16 | async-start | bytes 8650752 | tf_op jit(solution)/shard_map/all_gather | solution.py:147
  250.4 290.0 %all-gather.27.cloned.1.call-start = ((), (), s32[]{:S(2)}) async-start(), calls=%async_computation.17 | async-start | bytes 1966080 | tf_op jit(solution)/shard_map/all_gather | solution.py:226
  505.9 10.4 copy-start.5
  505.9 10.4 copy-start.46
  522.9 103.7 %reduce-scatter.14.cloned.1.call-start = ((), (), s32[]{:S(2)}) async-start(), calls=%async_computation.18 | async-start | bytes 3932160 | tf_op jit(solution)/shard_map/reduce_scatter | solution.py:272
  587.6 112.7 %all-gather.29.cloned.1.call-start = ((), (), s32[]{:S(2)}) async-start(), calls=%async_computation.19 | async-start | bytes 6488064 | tf_op jit(solution)/shard_map/all_gather | solution.py:151
  588.4 226.0 %reduce-scatter.20.cloned.1.call-start = ((), (), s32[]{:S(2)}) async-start(), calls=%async_computation.22 | async-start | bytes 4325376 | tf_op jit(solution)/shard_map/reduce_scatter | solution.py:334
  591.5 361.6 %reduce-scatter.16.cloned.1.call-start = ((), (), s32[]{:S(2)}) async-start(), calls=%async_computation.20 | async-start | bytes 4325376 | tf_op jit(solution)/shard_map/reduce_scatter | solution.py:332
  597.0 495.2 %reduce-scatter.18.cloned.1.call-start = ((), (), s32[]{:S(2)}) async-start(), calls=%async_computation.21 | async-start | bytes 4325376 | tf_op jit(solution)/shard_map/reduce_scatter | solution.py:333
  602.2 629.5 %reduce-scatter.28.cloned.1.call-start = ((), (), s32[]{:S(2)}) async-start(), calls=%async_computation.26 | async-start | bytes 4325376
  636.0 763.5 %reduce-scatter.26.cloned.1.call-start = ((), (), s32[]{:S(2)}) async-start(), calls=%async_computation.25 | async-start | bytes 12976128 | tf_op jit(solution)/shard_map/reduce_scatter | solution.py:341
  723.6 876.5 %reduce-scatter.22.cloned.1.call-start = ((), (), s32[]{:S(2)}) async-start(), calls=%async_computation.23 | async-start | bytes 17301504 | tf_op jit(solution)/shard_map/reduce_scatter | solution.py:335
  733.5 1053.8 %reduce-scatter.24.cloned.1.call-start = ((), (), s32[]{:S(2)}) async-start(), calls=%async_computation.24 | async-start | bytes 17301504 | tf_op jit(solution)/shard_map/reduce_scatter | solution.py:337
  744.1 10.9 copy-start.25
  755.8 6.6 copy-start.34
  763.8 45.1 %copy-start.9 = (bf16[1024,1024]{1,0:T(8,128)(2,1)S(1)}, bf16[1024,1024]{1,0:T(8,128)(2,1)}, u32[]{:S(2)}) copy-start(bf16[1024,1024]{1,0:T(8,128)(2,1)} %all-gather.15.cloned.1.call-done) | copy-start | bytes 6291460
  763.8 45.1 %copy-start.12 = (f32[192,1024]{1,0:T(8,128)S(1)}, f32[192,1024]{1,0:T(8,128)}, u32[]{:S(2)}) copy-start(f32[192,1024]{1,0:T(8,128)} %copy-done.11) | copy-start | bytes 2359300
  763.8 45.1 %copy-start.18 = (bf16[4,48,1024]{2,1,0:T(8,128)(2,1)S(1)}, bf16[4,48,1024]{2,1,0:T(8,128)(2,1)}, u32[]{:S(2)}) copy-start(bf16[4,48,1024]{2,1,0:T(8,128)(2,1)} %param.34) | copy-start | bytes 1179652
  (50 other events, 92.9 us)
Sparse Core Ops, SparseCore 0:
  10.9 56.9 all-gather.14
  70.8 55.2 all-gather.18
  128.9 55.2 all-gather.12
  186.2 18.5 all-gather.16
  248.4 37.5 reduce-scatter.11
  289.1 56.9 all-gather.20
  349.3 77.2 all-gather.22
  429.9 76.0 all-gather.24
  523.0 17.3 all-gather.26
  587.8 38.8 reduce-scatter.13
  629.5 70.8 all-gather.28
  703.1 109.7 reduce-scatter.19
  815.7 137.3 reduce-scatter.15
  955.8 136.2 reduce-scatter.17
  1094.8 136.8 reduce-scatter.27
  1234.4 165.0 reduce-scatter.25
  1402.2 197.8 reduce-scatter.21
  1602.8 184.4 reduce-scatter.23
where the time goes:
time: 1800 us; the launch traced here: 1790 us
  waiting for transfers between devices  1430 us (79%)
  blocking collectives  141 us (8%)
  matrix products  111 us (6%)
  local copies, waits for them, and re-layouts  82.2 us (5%)
    reduce_scatter x1, waiting for transfers between devices, per_device(): lax.psum_scatter(grad_up, ('batch', 'tier'), scatter_dimension=0, tiled=T...  201 us
    reduce_scatter x1, waiting for transfers between devices, per_device(): lax.psum_scatter(grad_down, ('batch', 'tier'), scatter_dimension=0, tiled...  187 us
    reduce_scatter x1, waiting for transfers between devices, per_device(): lax.psum_scatter(grad_conv, ('batch', 'tier'), scatter_dimension=1, tiled...  168 us
    unnamed x19, waiting for transfers between devices  144 us
    reduce_scatter x1, waiting for transfers between devices, per_device(): lax.psum_scatter(grad_value, ('batch', 'tier'), scatter_dimension=0, tile...  139 us
    reduce_scatter x1, waiting for transfers between devices, per_device(): lax.psum_scatter(grad_key, ('batch', 'tier'), scatter_dimension=0, tiled=...  139 us
    unnamed x2, blocking collectives  79 us
    all_gather x1, waiting for transfers between devices, per_device(): lax.all_gather(w_up, ('batch', 'tier'), axis=0, tiled=True)  77 us
  transfers between devices with their start and end apart: 18, of which 16 were waited for; matrix products, arithmetic and copies ran while one was open for 6% of the time, Pallas kernels for 0%

commit v1 on v0

v1 whole, which is shorter than its diff:
```python
import functools
import math

import jax
import jax.numpy as jnp
from jax import lax
from jax.experimental import pallas as pl
from jax.experimental.pallas import tpu as pltpu
from jax.sharding import PartitionSpec as P

norm_eps = 1e-05
MESH = pl.DeviceIdType.MESH
ANY = pl.BlockSpec(memory_space=pl.ANY)
VM = pl.BlockSpec(memory_space=pltpu.VMEM)
f32 = jnp.float32
bf16 = jnp.bfloat16


def remote(src, dst, send, recv, device):
    return pltpu.make_async_remote_copy(
        src_ref=src,
        dst_ref=dst,
        send_sem=send,
        recv_sem=recv,
        device_id=device,
        device_id_type=MESH,
    )


def places(groups):
    b, t = lax.axis_index("batch"), lax.axis_index("tier")
    z, y = b // 2, lax.rem(b, 2)
    zs = [lax.rem(z + d, groups) for d in range(groups)]
    zback = [lax.rem(z + groups - d, groups) for d in range(groups)]
    return b, t, z, y, zs, zback


def greet(groups, tiers, columns):
    b, t, z, y, zs, _ = places(groups)
    barrier = pltpu.get_barrier_semaphore()
    peers = []
    if tiers:
        peers += [(b, t ^ d) for d in (1, 2, 3)]
    if columns:
        peers += [(2 * zz + y, t) for zz in zs[1:]] + [(b ^ 1, t)]
    for peer in peers:
        pl.semaphore_signal(barrier, inc=1, device_id=peer, device_id_type=MESH)
    pl.semaphore_wait(barrier, len(peers))


def gather_kernel(groups, nu, *refs):
    (wa, wu, wc, wd, sm, comp, mem, seg, cot, mk) = refs[:10]
    (WA, WU, WC, WD, SM, CTX, COT, MK) = refs[10:18]
    lsem, ts, tr, zsd, zr, ys, yr, acs, acr = refs[18:]
    G = groups
    b, t, z, y, zs, zback = places(G)
    greet(G, True, True)
    ypeer = (b ^ 1, t)
    local, sends = [], []

    def here(src, dst, i):
        cp = pltpu.make_async_copy(src, dst, lsem.at[i])
        cp.start()
        return cp

    kinds = [(sm, SM), (wa, WA), (wu, WU), (wc, WC)]
    own = []
    for k, (src, dst) in enumerate(kinds):
        mine = src if k == 0 else src.at[t]
        own.append(here(mine, dst.at[b, t], k))
        for d in (1, 2, 3):
            piece = src if k == 0 else src.at[t ^ d]
            cp = remote(piece, dst.at[b, t], ts.at[k, d - 1], tr.at[k, d - 1], (b, t ^ d))
            cp.start()
            sends.append(cp)
    own.append(here(wd, WD.at[b], 4))
    pieces = [
        (comp, lambda q: CTX.at[:, pl.ds(nu * q, nu)]),
        (mem.at[:, 0], lambda q: CTX.at[:, 4 * nu + q]),
        (mem.at[:, 1], lambda q: CTX.at[:, 4 * nu + 4 + q]),
        (mem.at[:, 2], lambda q: CTX.at[:, 4 * nu + 8 + q]),
        (seg, lambda q: CTX.at[:, pl.ds(8 * nu + nu * q, nu)]),
        (mk, lambda q: MK.at[:, q]),
        (cot, lambda q: COT.at[:, pl.ds(nu * q, nu)]),
    ]
    for i, (src, at) in enumerate(pieces):
        own.append(here(src, at(t), 5 + i))
        for j, d in enumerate((1, 2)):
            cp = remote(src, at(t), acs.at[i, j], acr.at[i, j], (b, t ^ d))
            cp.start()
            sends.append(cp)
    table = [SM, WA, WU, WD, WC]
    local_of = [0, 1, 2, 4, 3]
    for k, dst in enumerate(table):
        own[local_of[k]].wait()
        if k != 3:
            kk = local_of[k]
            for d in (1, 2, 3):
                remote(dst.at[b, t], dst.at[b, t ^ d], ts.at[kk, d - 1], tr.at[kk, d - 1], (b, t ^ d)).wait_recv()
        for d in range(1, G):
            cp = remote(dst.at[b], dst.at[b], zsd.at[k, d], zr.at[k, d], (2 * zs[d] + y, t))
            cp.start()
            sends.append(cp)
        cp = remote(dst.at[b], dst.at[b], ys.at[k, 0], yr.at[k, 0], ypeer)
        cp.start()
        sends.append(cp)
    for i, (src, at) in enumerate(pieces):
        remote(at(t ^ 2), at(t ^ 2), acs.at[i, 1], acr.at[i, 1], (b, t ^ 2)).wait_recv()
        cp = remote(at(t ^ 2), at(t ^ 2), acs.at[i, 2], acr.at[i, 2], (b, t ^ 1))
        cp.start()
        sends.append(cp)
    for k, dst in enumerate(table):
        for d in range(1, G):
            at = dst.at[2 * zback[d] + y]
            remote(at, at, zsd.at[k, d], zr.at[k, d], ypeer).wait_recv()
            cp = remote(at, at, ys.at[k, d], yr.at[k, d], ypeer)
            cp.start()
            sends.append(cp)
    for k, dst in enumerate(table):
        for d in range(G):
            at = dst.at[2 * zback[d] + (1 - y)]
            remote(at, at, ys.at[k, d], yr.at[k, d], ypeer).wait_recv()
    for i, (src, at) in enumerate(pieces):
        for j, q in ((0, t ^ 1), (2, t ^ 3)):
            remote(at(q), at(q), acs.at[i, j], acr.at[i, j], (b, t ^ 1)).wait_recv()
    for i in range(len(pieces)):
        own[5 + i].wait()
    for cp in sends:
        cp.wait_send()


def gather_all(nb, nu, wa, wu, wc, wd, sm, comp, mem, seg, cot, mk):
    G = nb // 2
    S, _, U, M = comp.shape
    out = [
        jax.ShapeDtypeStruct((nb,) + wa.shape, bf16),
        jax.ShapeDtypeStruct((nb,) + wu.shape, bf16),
        jax.ShapeDtypeStruct((nb,) + wc.shape, bf16),
        jax.ShapeDtypeStruct((nb,) + wd.shape, bf16),
        jax.ShapeDtypeStruct((nb, 4) + sm.shape, f32),
        jax.ShapeDtypeStruct((S, 12 * nu, U, M), bf16),
        jax.ShapeDtypeStruct((S, 4 * nu, U, M), bf16),
        jax.ShapeDtypeStruct((S, 4) + mk.shape[1:], f32),
    ]
    dma = pltpu.SemaphoreType.DMA
    return pl.pallas_call(
        functools.partial(gather_kernel, G, nu),
        out_shape=out,
        in_specs=[ANY] * 10,
        out_specs=[ANY] * 8,
        scratch_shapes=[
            dma((12,)),
            dma((4, 3)),
            dma((4, 3)),
            dma((5, G)),
            dma((5, G)),
            dma((5, G)),
            dma((5, G)),
            dma((7, 3)),
            dma((7, 3)),
        ],
        compiler_params=pltpu.CompilerParams(collective_id=0, has_side_effects=True),
        name="gather_all",
    )(wa, wu, wc, wd, sm, comp, mem, seg, cot, mk)


def spread_kernel(same, x, o, lsem, ss, rs):
    b, t = lax.axis_index("batch"), lax.axis_index("tier")
    greet(1, True, False)
    cps = []
    for d in (1, 2, 3):
        cp = remote(x if same else x.at[t ^ d], o.at[t], ss.at[d - 1], rs.at[d - 1], (b, t ^ d))
        cp.start()
        cps.append(cp)
    mine = pltpu.make_async_copy(x if same else x.at[t], o.at[t], lsem)
    mine.start()
    mine.wait()
    for d in (1, 2, 3):
        remote(o.at[t ^ d], o.at[t ^ d], ss.at[d - 1], rs.at[d - 1], (b, t ^ d)).wait_recv()
    for cp in cps:
        cp.wait_send()


def spread(x, same, cid):
    dma = pltpu.SemaphoreType.DMA
    shape = ((4,) + x.shape) if same else x.shape
    return pl.pallas_call(
        functools.partial(spread_kernel, same),
        out_shape=jax.ShapeDtypeStruct(shape, x.dtype),
        in_specs=[ANY],
        out_specs=ANY,
        scratch_shapes=[dma, dma((3,)), dma((3,))],
        compiler_params=pltpu.CompilerParams(collective_id=cid, has_side_effects=True),
        name="spread_%d" % cid,
    )(x)


def reduce_kernel(groups, *refs):
    GD, GU, GC, GA, SMG = refs[:5]
    OD, OU, OC, OA, OS = refs[5:10]
    YD, YU, YC, YA, YS, ZD, ZU, ZC, ZA, ZS, TU, TC, TA, MU, MC, MA, ys, yr, zsd, zr, ts, tr = refs[10:]
    G = groups
    b, t, z, y, zs, zback = places(G)
    greet(G, True, True)
    ypeer = (b ^ 1, t)
    sends = []
    kinds = [
        (GD, YD, ZD, OD, None, None),
        (GU, YU, ZU, OU, MU, TU),
        (GC, YC, ZC, OC, MC, TC),
        (GA, YA, ZA, OA, MA, TA),
    ]
    for k, (g, yb, *_) in enumerate(kinds):
        for d in range(G):
            zz = zs[(d + 1) % G]
            cp = remote(g.at[2 * zz + (1 - y)], yb.at[zz], ys.at[k, d], yr.at[k, d], ypeer)
            cp.start()
            sends.append(cp)
    cp = remote(SMG, YS, ys.at[4, 0], yr.at[4, 0], ypeer)
    cp.start()
    sends.append(cp)
    for k, (g, yb, zb, o, m, tb) in enumerate(kinds):
        for d in range(G):
            zz = zs[(d + 1) % G]
            at = yb.at[zz]
            remote(at, at, ys.at[k, d], yr.at[k, d], ypeer).wait_recv()

            def add(i, c, yb=yb, zz=zz, g=g):
                yb[zz, i] = (yb[zz, i].astype(f32) + g[2 * zz + y, i].astype(f32)).astype(bf16)
                return c

            lax.fori_loop(0, yb.shape[1], add, 0)
            if d < G - 1:
                cp = remote(at, zb.at[d], zsd.at[k, d], zr.at[k, d], (2 * zz + y, t))
                cp.start()
                sends.append(cp)
    remote(YS, YS, ys.at[4, 0], yr.at[4, 0], ypeer).wait_recv()
    ZS[z] = SMG[...] + YS[...]
    for d in range(G - 1):
        cp = remote(ZS.at[z], ZS.at[z], zsd.at[4, d], zr.at[4, d], (2 * zs[d + 1] + y, t))
        cp.start()
        sends.append(cp)
    for k, (g, yb, zb, o, m, tb) in enumerate(kinds):
        for d in range(G - 1):
            remote(zb.at[d], zb.at[d], zsd.at[k, d], zr.at[k, d], ypeer).wait_recv()

        def total(i, c, k=k, yb=yb, zb=zb, o=o, m=m):
            acc = yb[z, i].astype(f32)
            for d in range(G - 1):
                acc = acc + zb[d, i].astype(f32)
            if k == 0:
                o[i] = acc
            else:
                m[i] = acc.astype(bf16)
            return c

        lax.fori_loop(0, o.shape[0], total, 0)
        if k:
            for d in (1, 2, 3):
                cp = remote(m.at[t ^ d], tb.at[t], ts.at[k - 1, d - 1], tr.at[k - 1, d - 1], (b, t ^ d))
                cp.start()
                sends.append(cp)
    for d in range(G - 1):
        at = ZS.at[zback[d + 1]]
        remote(at, at, zsd.at[4, d], zr.at[4, d], ypeer).wait_recv()
    acc = ZS[0]
    for zz in range(1, G):
        acc = acc + ZS[zz]
    OS[t] = acc
    for d in (1, 2, 3):
        cp = remote(OS.at[t], OS.at[t], ts.at[3, d - 1], tr.at[3, d - 1], (b, t ^ d))
        cp.start()
        sends.append(cp)
    for k, (g, yb, zb, o, m, tb) in enumerate(kinds):
        if k:
            o[t] = m[t].astype(f32)
            for d in (1, 2, 3):
                at = tb.at[t ^ d]
                remote(at, at, ts.at[k - 1, d - 1], tr.at[k - 1, d - 1], (b, t ^ d)).wait_recv()
                o[t ^ d] = tb[t ^ d].astype(f32)
    for d in (1, 2, 3):
        at = OS.at[t ^ d]
        remote(at, at, ts.at[3, d - 1], tr.at[3, d - 1], (b, t ^ d)).wait_recv()
    for cp in sends:
        cp.wait_send()


def reduce_all(nb, gd, gu, gc, ga, sg):
    G = nb // 2
    dma = pltpu.SemaphoreType.DMA
    shapes = [x.shape[1:] for x in (gd, gu, gc, ga)]
    return pl.pallas_call(
        functools.partial(reduce_kernel, G),
        out_shape=[jax.ShapeDtypeStruct(s, f32) for s in shapes]
        + [jax.ShapeDtypeStruct((4,) + sg.shape, f32)],
        in_specs=[VM] * 5,
        out_specs=[VM] * 5,
        scratch_shapes=[pltpu.VMEM((G,) + s, bf16) for s in shapes]
        + [pltpu.VMEM(sg.shape, f32)]
        + [pltpu.VMEM((G - 1,) + s, bf16) for s in shapes]
        + [pltpu.VMEM((G,) + sg.shape, f32)]
        + [pltpu.VMEM(s, bf16) for s in shapes[1:]]
        + [pltpu.VMEM(s, bf16) for s in shapes[1:]]
        + [dma((5, G)), dma((5, G)), dma((5, G)), dma((5, G)), dma((4, 3)), dma((4, 3))],
        compiler_params=pltpu.CompilerParams(
            collective_id=1, has_side_effects=True, vmem_limit_bytes=48 * 2**20
        ),
        name="reduce_all",
    )(gd, gu, gc, ga, sg)


def dot(a, b):
    return jnp.dot(a, b, preferred_element_type=f32)


def dot_tn(a, b):
    return lax.dot_general(a, b, (((0,), (0,)), ((), ())), preferred_element_type=f32)


def dot_nt(a, b):
    return lax.dot_general(a, b, (((1,), (1,)), ((), ())), preferred_element_type=f32)


def per_device(
    nb,
    segment,
    memory,
    compressed,
    evicted,
    window_mask,
    cotangent,
    w_query,
    w_key,
    w_value,
    w_output,
    w_up,
    b_up,
    w_down,
    b_down,
    ln_gain,
    ln_bias,
    w_conv,
    b_conv,
    slopes,
):
    S, R, M = segment.shape
    heads = slopes.shape[0]
    hd = M // heads
    nt = 4
    rw, rd, rs = w_query.shape[0], w_down.shape[0], b_down.shape[0]
    b, t = lax.axis_index("batch"), lax.axis_index("tier")
    Cw, Fw = M // nt, nb * rd
    nu, W = R // 16, R // 3
    seg_len = nt * R
    T = S * seg_len
    ht = heads // nt
    index = 4 * b + t

    wa = jnp.stack([w_query, w_key, w_value, w_output]).reshape(4, rw, nt, Cw)
    wa = wa.transpose(2, 1, 0, 3).reshape(nt, rw, 4 * Cw)
    wu = w_up.reshape(rw, nb, nt, rd).transpose(2, 0, 1, 3).reshape(nt, rw, Fw)
    wc = w_conv.reshape(3, rw, nt, Cw).transpose(2, 1, 0, 3).reshape(nt, rw, 3 * Cw)
    row0 = jnp.concatenate([ln_gain, ln_bias, b_down, b_conv])
    sm = jnp.zeros((8, 128), f32).at[0, : 4 * rs].set(row0.astype(f32)).at[1, :rd].set(b_up.astype(f32))
    mem = memory.reshape(S, W, 3, M).transpose(0, 2, 1, 3)
    mk = jnp.broadcast_to(window_mask.astype(f32)[:, :, None], (S, W, 128))
    WA, WU, WC, WD, SM, CTX, COT, MK = gather_all(
        nb,
        nu,
        wa,
        wu,
        wc,
        w_down,
        sm,
        compressed.reshape(S, nu, 16, M),
        mem,
        segment.reshape(S, nu, 16, M),
        cotangent.reshape(S, nu, 16, M),
        mk,
    )
    WA = WA.reshape(M, 4 * Cw)
    Wqkv, Wo = WA[:, : 3 * Cw], WA[:, 3 * Cw :]
    WU, WC, WD = WU.reshape(M, Fw), WC.reshape(M, 3 * Cw), WD.reshape(Fw, M)
    gain, bias, bdown, bconv = [SM[:, :, 0, i * rs : (i + 1) * rs].reshape(M) for i in range(4)]
    bup = lax.dynamic_index_in_dim(SM, t, 1, False)[:, 1, :rd].reshape(Fw)
    cols = lambda v: lax.dynamic_slice_in_dim(v, t * Cw, Cw, v.ndim - 1)
    ctx = CTX.reshape(S, 3 * seg_len, M)
    cot = COT.reshape(T, M)
    seg = ctx[:, 2 * seg_len :].reshape(T, M)

    kpos = jnp.concatenate(
        [
            jnp.arange(seg_len),
            seg_len + (3 * jnp.arange(seg_len // 3)[None, :] + jnp.arange(3)[:, None]).reshape(-1),
            2 * seg_len + jnp.arange(seg_len),
        ]
    )
    qpos = 2 * seg_len + jnp.arange(seg_len)
    allowed = kpos[None, :] <= qpos[:, None]
    dist = (qpos[:, None] - kpos[None, :]).astype(f32) * (1.0 / (3 * seg_len))
    slope = lax.dynamic_slice_in_dim(slopes, t * ht, ht)
    scale = 1.0 / math.sqrt(hd)
    q = dot(seg, Wqkv[:, :Cw]).astype(bf16).reshape(S, seg_len, ht, hd)
    kv = dot(ctx.reshape(-1, M), Wqkv[:, Cw:]).astype(bf16).reshape(S, 3 * seg_len, 2, ht, hd)
    kk, vv = kv[:, :, 0], kv[:, :, 1]
    raw = jnp.einsum("sqhd,skhd->shqk", q, kk, preferred_element_type=f32)
    scores = jnp.where(allowed, raw * scale - slope[:, None, None] * dist, -1e30)
    high = jnp.max(scores, axis=-1, keepdims=True)
    e = jnp.exp(scores - high)
    probs = e / jnp.sum(e, axis=-1, keepdims=True)
    probs_low = probs.astype(bf16)
    mixed_t = jnp.einsum("shqk,skhd->sqhd", probs_low, vv, preferred_element_type=f32).astype(bf16)
    MIX = spread(mixed_t.reshape(T, Cw), True, 2)
    mixed = MIX.transpose(1, 0, 2).reshape(T, M)
    resid_t = cols(seg).astype(f32) + dot(mixed, Wo)
    RES = spread(resid_t.astype(bf16), True, 3)
    resid = RES.transpose(1, 0, 2).reshape(T, M).astype(f32)
    center = resid - jnp.mean(resid, axis=-1, keepdims=True)
    spread_ = lax.rsqrt(jnp.mean(center * center, axis=-1, keepdims=True) + norm_eps)
    xhat = center * spread_
    normed = (xhat * gain + bias).astype(bf16)
    pre = dot(normed, WU) + bup
    phi = 0.5 * (1.0 + lax.erf(pre * math.sqrt(0.5)))
    act = (pre * phi).astype(bf16)
    slope_act = phi + pre * jnp.exp(-0.5 * pre * pre) * (1.0 / math.sqrt(2 * math.pi))
    place = lambda v: lax.dynamic_update_slice_in_dim(jnp.zeros((T, M), f32), v, t * Cw, 1)
    out_part = dot(act, WD) + place(resid_t + cols(bdown))
    rows = lambda v: v.astype(bf16).reshape(S, nt, R, M).transpose(1, 0, 2, 3)
    output = jnp.sum(spread(rows(out_part), False, 4).astype(f32), axis=0).astype(bf16)
    gdown = dot_tn(act, cot)
    d_act = dot_nt(cot, WD).astype(bf16)
    d_pre = d_act.astype(f32) * slope_act
    gub = jnp.sum(d_pre, axis=0)
    d_pre_low = d_pre.astype(bf16)
    gup = dot_tn(normed, d_pre_low)
    dn_part = dot_nt(d_pre_low, WU)
    stats = jnp.stack([jnp.mean(dn_part * gain, axis=1), jnp.mean(dn_part * gain * xhat, axis=1)])
    stats = lax.psum(stats, "tier")
    cols_of = lambda v: v.astype(bf16).reshape(T, nt, Cw).transpose(1, 0, 2)
    dn = jnp.sum(spread(cols_of(dn_part), False, 5).astype(f32), axis=0)
    xhat_t = cols(xhat)
    ggain, gbias = jnp.sum(dn * xhat_t, axis=0), jnp.sum(dn, axis=0)
    g = dn * cols(gain)
    cot_t = cols(cot).astype(f32)
    gdb = jnp.sum(cot_t, axis=0)
    d_resid = cot_t + (g - stats[0][:, None] - xhat_t * stats[1][:, None]) * spread_
    d_branch = d_resid.astype(bf16)
    gout = dot_tn(mixed, d_branch)
    dm_part = dot_nt(d_branch, Wo)
    dm = jnp.sum(spread(cols_of(dm_part), False, 6).astype(f32), axis=0).astype(bf16)
    dm = dm.reshape(S, seg_len, ht, hd)
    d_probs = jnp.einsum("sqhd,skhd->shqk", dm, vv, preferred_element_type=f32)
    delta = jnp.sum(probs * d_probs, axis=-1, keepdims=True)
    d_scores = probs * (d_probs - delta)
    gslope = -jnp.sum(d_scores * dist, axis=(0, 2, 3))
    d_raw = (d_scores * scale).astype(bf16)
    dq = jnp.einsum("shqk,skhd->sqhd", d_raw, kk, preferred_element_type=f32).astype(bf16)
    dk = jnp.einsum("shqk,sqhd->skhd", d_raw, q, preferred_element_type=f32).astype(bf16)
    dv = jnp.einsum("shqk,sqhd->skhd", probs_low, dm, preferred_element_type=f32).astype(bf16)
    dq, dk, dv = dq.reshape(T, Cw), dk.reshape(S, -1, Cw), dv.reshape(S, -1, Cw)
    flat = ctx.reshape(-1, M)
    gq = dot_tn(seg, dq)
    gk, gv = dot_tn(flat, dk.reshape(-1, Cw)), dot_tn(flat, dv.reshape(-1, Cw))
    own = lambda v: v[:, 2 * seg_len :].reshape(T, Cw)
    ig_part = dot_nt(jnp.concatenate([dq, own(dk), own(dv)], axis=1), Wqkv) + place(d_resid)
    input_grad = jnp.sum(spread(rows(ig_part), False, 7).astype(f32), axis=0)

    nw = seg_len // 3
    win = ctx[:, seg_len : 2 * seg_len].reshape(S, 3, nw, M)
    win = [win[:, k].reshape(S * nw, M) for k in range(3)]
    conv = sum(dot(win[k], WC[:, k * Cw : (k + 1) * Cw]) for k in range(3)) + cols(bconv)
    pooled = sum(cols(win[k]).astype(f32) for k in range(3)) * (1.0 / 3.0)
    mask = MK.reshape(S, nw, 128)[:, :, :1]
    old = (3 * jnp.arange(nw) + 3)[None, :, None] <= evicted[:, None, None]
    live = jnp.where(old, mask, 0.0).reshape(-1, 1)
    d_conv = live * (conv - pooled)
    gcb = jnp.sum(d_conv, axis=0)
    d_low = d_conv.astype(bf16)
    gconv = jnp.concatenate([dot_tn(win[k], d_low) for k in range(3)], axis=1)
    new_t = (mask.reshape(-1, 1) * conv).astype(bf16)
    NEW = spread(new_t, True, 8).reshape(nt, S, nw, Cw).transpose(1, 2, 0, 3).reshape(S, nw, M)
    slot_offset = seg_len - nw
    local_rows = jnp.arange(R, dtype=jnp.int32) + t * R
    padded = jnp.concatenate([jnp.zeros((S, slot_offset, M), bf16), NEW], axis=1)
    slot_rows = lax.dynamic_slice_in_dim(padded, t * R, R, 1)
    written = (local_rows[None, :] >= slot_offset) & (
        3 * (local_rows[None, :] - slot_offset) + 3 <= evicted[:, None]
    )
    new_compressed = jnp.where(written[..., None], slot_rows, compressed)
    new_memory = jnp.where((local_rows[None, :] < evicted[:, None])[..., None], segment, memory)

    low = lambda v, *s: v.astype(bf16).reshape(s)
    gs = lax.dynamic_update_slice_in_dim(jnp.zeros((128,), f32), gslope, t * ht, 0)
    sg = jnp.concatenate([gub, gdb, ggain, gbias, gcb, gs])
    sg = jnp.concatenate([sg, jnp.zeros((24 * 128 - sg.shape[0],), f32)]).reshape(24, 128)
    OD, OU, OC, OA, OS = reduce_all(
        nb,
        low(gdown, nb, 4, rd // 4, M),
        low(gup, nb, 4, rw, Fw),
        low(gconv, nb, 4, rw, 3 * Cw),
        low(jnp.concatenate([gq, gk, gv, gout], axis=1), nb, 4, rw, 4 * Cw),
        sg,
    )
    OA = OA.reshape(nt, rw, 4, Cw).transpose(2, 1, 0, 3).reshape(4, rw, M)
    OU = OU.reshape(nt, rw, nb, rd).transpose(1, 2, 0, 3).reshape(rw, nb * nt * rd)
    OC = OC.reshape(nt, rw, 3, Cw).transpose(2, 1, 0, 3).reshape(3, rw, M)
    OS = OS.reshape(nt, -1)
    vec = lambda o: lax.dynamic_slice_in_dim(OS[:, o : o + Cw].reshape(M), index * rs, rs)
    gub_out = lax.dynamic_slice(OS, (t, b * rd), (1, rd)).reshape(rd)
    gslopes = jnp.sum(OS[:, Fw + 4 * Cw : Fw + 4 * Cw + heads], axis=0)
    return (
        output,
        input_grad,
        new_memory,
        new_compressed,
        OA[0],
        OA[1],
        OA[2],
        OA[3],
        OU,
        gub_out,
        OD.reshape(rd, M),
        vec(Fw),
        vec(Fw + Cw),
        vec(Fw + 2 * Cw),
        OC,
        vec(Fw + 3 * Cw),
        gslopes,
    )


def solution(mesh):
    both = ("batch", "tier")
    rows = P("batch", "tier", None)
    mat, vec = P(both, None), P(both)
    return jax.shard_map(
        functools.partial(per_device, mesh.shape["batch"]),
        mesh=mesh,
        in_specs=(
            (rows, rows, rows, P("batch"), P("batch", "tier"), rows)
            + (mat, mat, mat, mat, mat, vec, mat, vec, vec, vec)
            + (P(None, both, None), vec, P())
        ),
        out_specs=(
            (rows, rows, rows, rows, mat, mat, mat, mat, mat, vec, mat, vec, vec, vec)
            + (P(None, both, None), vec, P())
        ),
        check_vma=False,
    )
```

time: 1800 us -> 609 us (0.34)
  waiting for transfers between devices: 1430 us -> 0 us
  Pallas kernels: 0 us -> 347 us
  blocking collectives: 141 us -> 5.3 us
  other arithmetic: 15.2 us -> 47.8 us
    reduce_scatter x8 -> x0, waiting for transfers between devices: 857 us -> none  [the longest x1 201 us: per_device(): lax.psum_scatter(grad_up, ('batch', 'tier'), scatter_dimension=0, tiled=T...]
    all_gather x9 -> x0, waiting for transfers between devices: 427 us -> none  [the longest x1 77 us: per_device(): lax.all_gather(w_up, ('batch', 'tier'), axis=0, tiled=True)]
    pallas_call x0 -> x9, Pallas kernels: none -> 347 us  [the longest x7 129 us: spread(): pl.pallas_call(functools.partial(spread_kernel, same), out_shape=jax.Shap...]
    unnamed x19 -> x0, waiting for transfers between devices: 144 us -> none
    unnamed x2 -> x0, blocking collectives: 79 us -> none
    all_gather x4 -> x0, blocking collectives: 51.4 us -> none  [the longest x1 31.2 us: per_device(): lax.all_gather(b_up, ('batch', 'tier'), axis=0, tiled=True)]
    convert_element_type x0 -> x9, local copies, waits for them, and re-layouts: none -> 21.1 us  [the longest x2 7.32 us: per_device(): resid = RES.transpose(1, 0, 2).reshape(T, M).astype(f32)]
    dot_general x38 -> x26, matrix products: 111 us -> 96.7 us  [the longest x9 22.7 us: dot_tn(): lax.dot_general(a, b, (((0,), (0,)), ((), ())), preferred_element_type=f32)]
  transfers between devices with their start and end apart: 18 -> 0, of which waited for: 16 -> 0; matrix products, arithmetic and copies ran while one was open for 6% -> 0% of each run, Pallas kernels for 0% -> 0%
where the time goes in v1:
time: 609 us; the launch traced here: 601 us
  Pallas kernels  347 us (57%)
  matrix products  102 us (17%)
  local copies, waits for them, and re-layouts  96.6 us (16%)
  other arithmetic  47.8 us (8%)
    pallas_call x7, Pallas kernels, spread(): pl.pallas_call(functools.partial(spread_kernel, same), out_shape=jax.Shap...  129 us
    pallas_call x1, Pallas kernels, gather_all(): pl.pallas_call(functools.partial(gather_kernel, G, nu), out_shape=out, in...  114 us
    pallas_call x1, Pallas kernels, reduce_all(): pl.pallas_call(functools.partial(reduce_kernel, G), out_shape=[jax.ShapeD...  104 us
    dot_general x9, matrix products, dot_tn(): lax.dot_general(a, b, (((0,), (0,)), ((), ())), preferred_element_type=f32)  22.7 us
    dot_general x8, matrix products, dot(): return jnp.dot(a, b, preferred_element_type=f32)  22.5 us
    dot_general x1, matrix products, per_device(): jnp.einsum('shqk,sqhd->skhd', d_raw, q, preferred_element_type=f32)  15.6 us
    dot_general x1, matrix products, per_device(): jnp.einsum('shqk,skhd->sqhd', d_raw, kk, preferred_element_type=f32)  15.4 us
    sub x1, other arithmetic, per_device(): d_scores = probs * (d_probs - delta)  14.5 us

profile of v1, /device:TPU:11, one launch (start us, length us, event | category | flops | bytes accessed | tf_op | source)
XLA Modules:
  0.0 601.1 jit_solution(18006154522909875327)
XLA Ops:
  18.4 113.9 %gather_all.1 = (bf16[8,4,32,1024]{3,2,1,0:T(8,128)(2,1)}, bf16[8,4,32,1024]{3,2,1,0:T(8,128)(2,1)}, bf16[8,4,32,768]{3,2,1,0:T(8,128)(2,1)}, bf16[8,128,1024]{2...) custom-call(bf16[4,32,1024]{2,1,0:T(8,128)(2,1)} %reshape.590.refs_0, ...), custom_call_target="tpu_custom_call" | custom-call | tf_op jit(solution)/shard_map/gather_all/pallas_call | solution.py:146
  138.2 6.7 %convolution_convert_fusion = bf16[2304,512]{1,0:T(8,128)(2,1)} fusion(bf16[2304,1024]{1,0:T(8,128)(2,1)} %bitcast.231, bf16[1024,1024]{1,0:T(8,128)(2,1)} %bitcast.298), kind=kOutput, calls=%fused_computation.6 | convolution fusion | flops 2417098752 | bytes 8126464 | tf_op jit(solution)/shard_map/dot_general | solution.py:313
  144.9 5.2 reshape.603
  150.1 3.1 fusion.97
  160.4 8.7 %spread_8.1 = bf16[4,256,256]{2,1,0:T(8,128)(2,1)} custom-call(bf16[256,256]{1,0:T(8,128)(2,1)} %get-tuple-element.95.x), custom_call_target="tpu_custom_call" | custom-call | tf_op jit(solution)/shard_map/spread_8/pallas_call | solution.py:187
  179.8 5.3 fusion.100
  189.2 19.8 %spread_2.1 = bf16[4,768,256]{2,1,0:T(8,128)(2,1)} custom-call(bf16[768,256]{1,0:T(8,128)(2,1)} %bitcast.279), custom_call_target="tpu_custom_call" | custom-call | tf_op jit(solution)/shard_map/spread_2/pallas_call | solution.py:187
  210.7 3.4 fusion.103
  214.1 19.8 %spread_3.1 = bf16[4,768,256]{2,1,0:T(8,128)(2,1)} custom-call(bf16[768,256]{1,0:T(8,128)(2,1)} %get-tuple-element.106.x), custom_call_target="tpu_custom_call" | custom-call | tf_op jit(solution)/shard_map/spread_3/pallas_call | solution.py:187
  243.1 3.6 copy.118
  246.7 3.7 copy.119
  250.5 5.0 multiply_convert_fusion.1
  255.5 3.0 fusion.104
  258.6 4.3 multiply_reduce_fusion.3
  262.9 5.3 psum.7
  268.3 5.7 convolution_convert_fusion.1
  274.0 3.5 fusion.105
  277.5 3.2 convolution_convert_fusion.2
  284.2 21.7 %spread_5.1 = bf16[4,768,256]{2,1,0:T(8,128)(2,1)} custom-call(bf16[4,768,256]{2,1,0:T(8,128)(2,1)} %bitcast.236), custom_call_target="tpu_custom_call" | custom-call | tf_op jit(solution)/shard_map/spread_5/pallas_call | solution.py:187
  308.2 3.1 multiply_reduce_fusion.4
  316.2 19.8 %spread_4.1 = bf16[4,4,48,1024]{3,2,1,0:T(8,128)(2,1)} custom-call(bf16[4,4,48,1024]{3,2,1,0:T(8,128)(2,1)} %bitcast.237), custom_call_target="tpu_custom_call" | custom-call | tf_op jit(solution)/shard_map/spread_4/pallas_call | solution.py:187
  346.6 19.8 %spread_6.1 = bf16[4,768,256]{2,1,0:T(8,128)(2,1)} custom-call(bf16[4,768,256]{2,1,0:T(8,128)(2,1)} %bitcast.239), custom_call_target="tpu_custom_call" | custom-call | tf_op jit(solution)/shard_map/spread_6/pallas_call | solution.py:187
  369.0 3.5 convolution_convert_fusion.5
  374.7 4.1 reshape.645
  382.9 15.4 %fusion.27 = bf16[4,192,2,128]{3,1,2,0:T(8,128)(2,1)} fusion(bf16[4,576,1,2,128]{4,3,2,1,0:T(2,128)(2,1)} %get-tuple-element.85, f32[4,2,192,576]{3,2,1,0:T(8,128)} %fusion.38, f32[4,2,192,576]{3,2,1,0:T(8,128)} %get-tuple-element.105, f32[4,2,192]{2,1,0:T(2,128)S(1)} %copy-done.49), kind=kOutput, calls=%fused_computation.68 | convolution fusion | flops 232884288 | bytes 8656896 | tf_op jit(solution)/shard_map/shqk,skhd->sqhd/dot_general | solution.py:457
  398.3 14.5 %multiply_reduce_fusion = f32[2]{0:T(128)S(1)} fusion(f32[192,576]{1,0:T(8,128)S(1)} %copy-done.17, f32[4,2,192,576]{3,2,1,0:T(8,128)} %fusion.38, f32[4,2,192,576]{3,2,1,0:T(8,128)} %get-tuple-element.105, f32[4,2,192]{2,1,0:T(2,128)S(1)} %copy-done.49), kind=kOutput, calls=%fused_computation.7 | output fusion | flops 6195261 | bytes 7526408 | tf_op jit(solution)/shard_map/sub | solution.py:454
  412.8 15.6 %convolution_convert_fusion.6 = bf16[4,2,128,576]{2,3,1,0:T(8,128)(2,1)S(1)} fusion(f32[4,2,192,576]{3,2,1,0:T(8,128)} %fusion.38, bf16[4,192,2,128]{3,2,1,0:T(2,128)(2,1)} %reshape.604, f32[4,2,192,576]{3,2,1,0:T(8,128)} %get-tuple-element.105, f32[4,2,192]{2,1,0:T(2,128)} %copy-done.48), kind=kOutput, calls=%fused_computation.55 | convolution fusion | flops 233277504 | bytes 8656896 | tf_op jit(solution)/shard_map/shqk,sqhd->skhd/dot_general | solution.py:458
  438.6 4.1 reshape.644
  447.7 19.8 %spread_7.1 = bf16[4,4,48,1024]{3,2,1,0:T(8,128)(2,1)} custom-call(bf16[4,4,48,1024]{3,2,1,0:T(8,128)(2,1)} %bitcast.240), custom_call_target="tpu_custom_call" | custom-call | tf_op jit(solution)/shard_map/spread_7/pallas_call | solution.py:187
  470.2 6.9 %copy.135 = bf16[1024,2304]{1,0:T(8,128)(2,1)} copy(bf16[1024,2304]{0,1:T(8,128)(2,1)} %bitcast.232) | data formatting | bytes 9437184 | tf_op jit(solution)/shard_map/dot_general | solution.py:317
  477.1 3.9 convolution_convert_fusion.7
  484.9 104.1 %reduce_all.1 = (f32[4,32,1024]{2,1,0:T(8,128)S(1)}, f32[4,32,1024]{2,1,0:T(8,128)S(1)}, f32[4,32,768]{2,1,0:T(8,128)S(1)}, f32[4,32,1024]{2,1,0:T(8,128)S(1)}, f32[4,24,128]{2,1,0:T(8,128)S(1)}) custom-call(bf16[8,4,32,1024]{3,2,1,0:T(8,128)(2,1)S(1)} %bitcast.226, bf16[8,4,32,1024]{3,2,1,0:T(8,128)(2,1)} %bitcast.271, ...), custom_call_target="tpu_custom_call" | custom-call | tf_op jit(solution)/shard_map/reduce_all/pallas_call | solution.py:292
  (257 shorter events, 119.8 us)
Async XLA Ops:
  0.7 11.4 %copy-start.33 = (bf16[3,32,1024]{2,1,0:T(8,128)(2,1)S(1)}, bf16[3,32,1024]{2,1,0:T(8,128)(2,1)}, u32[]{:S(2)}) copy-start(bf16[3,32,1024]{2,1,0:T(8,128)(2,1)} %param.39) | copy-start | bytes 589828
  0.7 12.7 %copy-start.32 = (bf16[32,4096]{1,0:T(8,128)(2,1)S(1)}, bf16[32,4096]{1,0:T(8,128)(2,1)}, u32[]{:S(2)}) copy-start(bf16[32,4096]{1,0:T(8,128)(2,1)} %param.33) | copy-start | bytes 786436
  5.1 8.5 %copy-start.37 = (f32[8,128]{1,0:T(8,128)}, f32[8,128]{1,0:T(8,128)S(1)}, u32[]{:S(2)}) copy-start(f32[8,128]{1,0:T(8,128)S(1)} %scatter.14.refs_4_) | copy-start | bytes 12292
  8.7 5.6 copy-start.19
  8.7 5.6 copy-start.21
  16.4 117.0 %copy-start.41 = (s32[4]{0:T(128)S(1)}, s32[4]{0:T(128)}, u32[]{:S(2)}) copy-start(s32[4]{0:T(128)} %param.26) | copy-start | bytes 52
  150.0 3.1 copy-start.4
  153.5 24.7 %copy-start.7 = (bf16[4,192,1024]{2,1,0:T(8,128)(2,1)}, bf16[4,192,1024]{2,1,0:T(8,128)(2,1)S(1)}, u32[]{:S(2)}) copy-start(bf16[4,192,1024]{2,1,0:T(8,128)(2,1)S(1)} %get-tuple-element.81) | copy-start | bytes 4718596
  153.7 4.3 copy-start.13
  157.9 12.3 %copy-start.20 = (bf16[4,48,1024]{2,1,0:T(8,128)(2,1)S(1)}, bf16[4,48,1024]{2,1,0:T(8,128)(2,1)}, u32[]{:S(2)}) copy-start(bf16[4,48,1024]{2,1,0:T(8,128)(2,1)} %param.25) | copy-start | bytes 1179652
  172.0 4.5 copy-start.23
  179.8 5.3 copy-start.9
  185.1 2.9 copy-start.48
  210.7 3.4 copy-start.5
  246.7 3.7 copy-start.18
  246.7 3.7 copy-start.38
  250.4 5.0 copy-start.35
  250.5 5.0 copy-start.43
  255.5 3.1 copy-start.12
  255.5 3.1 copy-start.45
  258.5 4.4 copy-start.46
  268.3 5.7 copy-start.44
  268.3 5.7 copy-start.47
  274.0 3.5 copy-start.36
  284.2 24.0 %copy-start.26 = (f32[768,256]{1,0:T(8,128)S(1)}, f32[768,256]{1,0:T(8,128)}, u32[]{:S(2)}) copy-start(f32[768,256]{1,0:T(8,128)} %get-tuple-element.107) | copy-start | bytes 2359300
  284.2 24.0 %copy-start.39 = (f32[256]{0:T(256)S(1)}, f32[256]{0:T(256)}, u32[]{:S(2)}) copy-start(f32[256]{0:T(256)} %dynamic_slice.57) | copy-start | bytes 3076
  284.2 24.0 %copy-start.40 = (f32[256]{0:T(256)S(1)}, f32[256]{0:T(256)}, u32[]{:S(2)}) copy-start(f32[256]{0:T(256)} %dynamic_slice.55) | copy-start | bytes 3076
  308.2 3.1 copy-start.6
  382.9 15.4 %copy-start.17 = (f32[192,576]{1,0:T(8,128)S(1)}, f32[192,576]{1,0:T(8,128)}, u32[]{:S(2)}) copy-start(f32[192,576]{1,0:T(8,128)} %copy-done.16) | copy-start | bytes 1327108
  470.2 6.9 %copy-start.24 = (bf16[2304,256,1,1]{1,0,2,3:T(8,128)(2,1)S(1)}, bf16[2304,256,1,1]{1,0,2,3:T(8,128)(2,1)}, u32[]{:S(2)}) copy-start(bf16[2304,256,1,1]{1,0,2,3:T(8,128)(2,1)} %reshape.645) | copy-start | bytes 3538948
  477.1 3.9 copy-start.8
  477.1 4.1 copy-start.25
  (18 other events, 28.7 us)

commit v2 on v1

--- a/solution.py
+++ b/solution.py
@@ -529,12 +529,769 @@
     )
 
 
+class Names:
+    def __init__(self, names, refs):
+        for name, ref in zip(names, refs):
+            setattr(self, name, ref)
+
+
+def layer_kernel(names, shape, *refs):
+    r = Names(names, refs)
+    nb, nu, S, ht, hd, M, Cw, rw, rd = shape
+    G, bq = nb // 2, nb // 4
+    L = 16 * 4 * nu
+    C3 = 3 * L
+    nw = L // 3
+    Fw = nb * rd
+    scale = 1.0 / math.sqrt(hd)
+    b, t, z, y, zs, zback = places(G)
+    ypeer = (b ^ 1, t)
+    tc = pl.ds(pl.multiple_of(t * Cw, Cw), Cw)
+    sends = []
+
+    def put(cp):
+        cp.start()
+        sends.append(cp)
+
+    def each(n, body):
+        lax.fori_loop(0, n, lambda i, c: (body(i), c)[1], 0)
+
+    def ex_send(e, s, src, dst):
+        for d in (1, 2, 3):
+            remote(src(t ^ d), dst(d), r.es.at[e, s, d - 1], r.er.at[e, s, d - 1], (b, t ^ d)).start()
+
+    def ex_wait(e, s, dst):
+        for d in (1, 2, 3):
+            at = dst(d)
+            remote(at, at, r.es.at[e, s, d - 1], r.er.at[e, s, d - 1], (b, t ^ d)).wait_recv()
+
+    def ex_sent(e, src):
+        def one(s):
+            for d in (1, 2, 3):
+                at = src(t ^ d, s)
+                remote(at, at, r.es.at[e, s, d - 1], r.er.at[e, s, d - 1], (b, t ^ d)).wait_send()
+
+        each(S, one)
+
+    greet(G, True, True)
+
+    def here(src, dst, i):
+        cp = pltpu.make_async_copy(src, dst, r.lsem.at[i])
+        cp.start()
+        return cp
+
+    kinds = {"S": (r.sm, r.SM, 0), "A": (r.wa, r.WA, 1), "U": (r.wu, r.WU, 2), "C": (r.wc, r.WC, 3), "D": (r.wd, r.WD, 4)}
+    own = {}
+
+    def tier_start(n):
+        src, dst, k = kinds[n]
+        own[n] = here(src if n == "S" else src.at[t], dst.at[b, t], k)
+        for d in (1, 2, 3):
+            piece = src if n == "S" else src.at[t ^ d]
+            put(remote(piece, dst.at[b, t], r.ts.at[k, d - 1], r.tr.at[k, d - 1], (b, t ^ d)))
+
+    def tier_wait(n):
+        src, dst, k = kinds[n]
+        own[n].wait()
+        if n != "D":
+            for d in (1, 2, 3):
+                at = dst.at[b, t ^ d]
+                remote(at, at, r.ts.at[k, d - 1], r.tr.at[k, d - 1], (b, t ^ d)).wait_recv()
+
+    def z_send(n):
+        src, dst, k = kinds[n]
+        for d in range(1, G):
+            put(remote(dst.at[b], dst.at[b], r.zsd.at[k, d], r.zr.at[k, d], (2 * zs[d] + y, t)))
+
+    def y_send(n):
+        src, dst, k = kinds[n]
+        put(remote(dst.at[b], dst.at[b], r.ys.at[k, 0], r.yr.at[k, 0], ypeer))
+
+    def y_forward(n):
+        src, dst, k = kinds[n]
+        for d in range(1, G):
+            at = dst.at[2 * zback[d] + y]
+            remote(at, at, r.zsd.at[k, d], r.zr.at[k, d], ypeer).wait_recv()
+            put(remote(at, at, r.ys.at[k, d], r.yr.at[k, d], ypeer))
+
+    def y_wait(n):
+        src, dst, k = kinds[n]
+        for d in range(G):
+            at = dst.at[2 * zback[d] + (1 - y)]
+            remote(at, at, r.ys.at[k, d], r.yr.at[k, d], ypeer).wait_recv()
+
+    pieces = [
+        (r.seg, lambda q: r.CTX.at[:, pl.ds(8 * nu + nu * q, nu)]),
+        (r.comp, lambda q: r.CTX.at[:, pl.ds(nu * q, nu)]),
+        (r.mem.at[:, 0], lambda q: r.CTX.at[:, 4 * nu + q]),
+        (r.mem.at[:, 1], lambda q: r.CTX.at[:, 4 * nu + 4 + q]),
+        (r.mem.at[:, 2], lambda q: r.CTX.at[:, 4 * nu + 8 + q]),
+        (r.cot, lambda q: r.COT.at[:, pl.ds(nu * q, nu)]),
+        (r.mk, lambda q: r.MK.at[:, q]),
+    ]
+
+    tier_start("A")
+    own["D"] = here(r.wd, r.WD.at[b], 4)
+    tier_start("U")
+    acts = []
+    for i, (src, at) in enumerate(pieces):
+        acts.append(here(src, at(t), 5 + i))
+        for j, d in enumerate((1, 2)):
+            put(remote(src, at(t), r.acs.at[i, j], r.acr.at[i, j], (b, t ^ d)))
+    tier_start("C")
+    tier_start("S")
+    tier_wait("A")
+    z_send("A")
+    y_send("A")
+    tier_wait("D")
+    y_send("D")
+    tier_wait("U")
+    z_send("U")
+    y_send("U")
+
+    row = lax.broadcasted_iota(jnp.int32, (L, C3), 0) + 2 * L
+    col = lax.broadcasted_iota(jnp.int32, (L, C3), 1)
+    inner = col - L
+    k1 = (inner >= nw).astype(jnp.int32)
+    k2 = (inner >= 2 * nw).astype(jnp.int32)
+    win = inner - nw * (k1 + k2)
+    pos = jnp.where((col >= L) & (col < 2 * L), L + 3 * win + k1 + k2, col)
+    r.DIST[...] = jnp.where(pos <= row, (row - pos).astype(f32) * (1.0 / C3), 1e30)
+    r.SMG[...] = jnp.zeros_like(r.SMG)
+
+    y_forward("A")
+    z_send("D")
+    for i, (src, at) in enumerate(pieces):
+        remote(at(t ^ 2), at(t ^ 2), r.acs.at[i, 1], r.acr.at[i, 1], (b, t ^ 2)).wait_recv()
+        put(remote(at(t ^ 2), at(t ^ 2), r.acs.at[i, 2], r.acr.at[i, 2], (b, t ^ 1)))
+    for i, (src, at) in enumerate(pieces):
+        for j, q in ((0, t ^ 1), (2, t ^ 3)):
+            remote(at(q), at(q), r.acs.at[i, j], r.acr.at[i, j], (b, t ^ 1)).wait_recv()
+        acts[i].wait()
+    y_wait("A")
+
+    def seg_rows(s):
+        return r.CTX[s, 8 * nu : 12 * nu].reshape(L, M)
+
+    def project(s):
+        rows = r.CTX[s].reshape(C3, M)
+        kv = jnp.dot(rows, r.WA[:, :, :, Cw : 3 * Cw].reshape(M, 2 * Cw), preferred_element_type=f32)
+        r.KV[s] = kv.astype(bf16)
+        q = jnp.dot(seg_rows(s), r.WA[:, :, :, :Cw].reshape(M, Cw), preferred_element_type=f32)
+        r.Q[s] = q.astype(bf16)
+
+    each(S, project)
+    tier_wait("S")
+    z_send("S")
+    y_send("S")
+
+    def attend(s):
+        for h in range(ht):
+            c = slice(h * hd, (h + 1) * hd)
+            raw = dot_nt(r.Q[s, :, c], r.KV[s, :, c])
+            slope = r.sl[pl.ds(t * ht + h, 1), :][:, :1]
+            scores = raw * scale - slope * r.DIST[...]
+            e = jnp.exp(scores - jnp.max(scores, axis=1, keepdims=True))
+            p = e * (1.0 / jnp.sum(e, axis=1, keepdims=True))
+            r.PR[s, h] = p
+            v = r.KV[s, :, Cw + h * hd : Cw + (h + 1) * hd]
+            r.MIX[t, s, :, c] = jnp.dot(p.astype(bf16), v, preferred_element_type=f32).astype(bf16)
+        ex_send(0, s, lambda q: r.MIX.at[t, s], lambda d: r.MIX.at[t, s])
+
+    each(S, attend)
+    y_forward("U")
+    tier_wait("C")
+    z_send("C")
+
+    def wo(q):
+        return r.WA[bq * q : bq * (q + 1), :, :, 3 * Cw :].reshape(Cw, Cw)
+
+    def residual(s):
+        ex_wait(0, s, lambda d: r.MIX.at[t ^ d, s])
+        acc = r.CTX[s, 8 * nu : 12 * nu, :, tc].reshape(L, Cw).astype(f32)
+        for q in range(4):
+            acc = acc + jnp.dot(r.MIX[q, s], wo(q), preferred_element_type=f32)
+        r.RT[s] = acc
+        r.RES[t, s] = acc.astype(bf16)
+        ex_send(1, s, lambda q: r.RES.at[t, s], lambda d: r.RES.at[t, s])
+
+    each(S, residual)
+    y_forward("S")
+    y_wait("S")
+    for q in range(4):
+        block = r.SM[bq * q, 0, 0:8]
+        for bb in range(bq * q, bq * (q + 1)):
+            for tt in range(4):
+                if bb != bq * q or tt:
+                    block = block + r.SM[bb, tt, 0:8]
+        for i in range(8):
+            at = q * Cw + 128 * (i % 2)
+            r.VV[i // 2 : i // 2 + 1, at : at + 128] = block[i : i + 1]
+    for bb in range(nb):
+        r.VV[4:5, bb * rd : (bb + 1) * rd] = r.SM[bb, t, 8:9, :rd]
+    y_wait("U")
+
+    def xhat_of(s, q):
+        return (r.RES[q, s].astype(f32) - r.MU[s, :, :1]) * r.INV[s, :, :1]
+
+    def feed(s):
+        ex_wait(1, s, lambda d: r.RES.at[t ^ d, s])
+        parts = [r.RES[q, s].astype(f32) for q in range(4)]
+        mu = sum(jnp.sum(x, axis=1, keepdims=True) for x in parts) * (1.0 / M)
+        var = sum(jnp.sum((x - mu) * (x - mu), axis=1, keepdims=True) for x in parts) * (1.0 / M)
+        inv = lax.rsqrt(var + norm_eps)
+        r.MU[s] = jnp.broadcast_to(mu, (L, 128))
+        r.INV[s] = jnp.broadcast_to(inv, (L, 128))
+        for q in range(4):
+            c = slice(q * Cw, (q + 1) * Cw)
+            r.NRM[s, :, c] = (((parts[q] - mu) * inv) * r.VV[0:1, c] + r.VV[1:2, c]).astype(bf16)
+        fb = Fw // 4
+        for j in range(4):
+            c = slice(j * fb, (j + 1) * fb)
+            pre = jnp.dot(r.NRM[s], r.WU[:, :, :, c].reshape(M, fb), preferred_element_type=f32) + r.VV[4:5, c]
+            phi = 0.5 + 0.5 * lax.erf(pre * math.sqrt(0.5))
+            r.ACT[s, :, c] = (pre * phi).astype(bf16)
+            r.GP[s, :, c] = (phi + pre * (jnp.exp(-0.5 * pre * pre) * (1.0 / math.sqrt(2 * math.pi)))).astype(bf16)
+
+    each(S, feed)
+
+    grads = [(r.GD, r.YD, r.ZD), (r.GU, r.YU, r.ZU), (r.GC, r.YC, r.ZC), (r.GA, r.YA, r.ZA)]
+
+    def to_y(k, zz):
+        g, yb, zb = grads[k]
+        remote(g.at[2 * zz + (1 - y)], yb.at[zz], r.gys.at[k, zz], r.gyr.at[k, zz], ypeer).start()
+
+    def mid(k):
+        g, yb, zb = grads[k]
+        for d in range(G):
+            zz = zs[(d + 1) % G]
+            at = yb.at[zz]
+            remote(at, at, r.gys.at[k, zz], r.gyr.at[k, zz], ypeer).wait_recv()
+
+            def add(i, zz=zz):
+                yb[zz, i] = (yb[zz, i].astype(f32) + g[2 * zz + y, i].astype(f32)).astype(bf16)
+
+            each(yb.shape[1], add)
+            if d < G - 1:
+                put(remote(at, zb.at[d], r.gzs.at[k, d], r.gzr.at[k, d], (2 * zz + y, t)))
+
+    def fin(k, store):
+        g, yb, zb = grads[k]
+        for d in range(G - 1):
+            remote(zb.at[d], zb.at[d], r.gzs.at[k, d], r.gzr.at[k, d], ypeer).wait_recv()
+
+        def total(i):
+            acc = yb[z, i].astype(f32)
+            for d in range(G - 1):
+                acc = acc + zb[d, i].astype(f32)
+            store(i, acc)
+
+        each(4, total)
+
+    fb = Fw // 4
+
+    def grad_down(j):
+        c = pl.ds(pl.multiple_of(j * fb, fb), fb)
+        rows = r.ACT[:, :, c].reshape(S * L, fb)
+        g = dot_tn(rows, r.COT[...].reshape(S * L, M)).astype(bf16)
+        r.GD[pl.ds(j * bq, bq)] = g.reshape(bq, 4, rd // 4, M)
+        for i in range(bq // 2):
+            to_y(0, j * (bq // 2) + i)
+
+    each(4, grad_down)
+    y_forward("D")
+    y_send("C")
+    y_wait("D")
+
+    def back_feed(s):
+        cot = r.COT[s].reshape(L, M)
+        for j in range(4):
+            c = slice(j * fb, (j + 1) * fb)
+            wd = r.WD[bq * j : bq * (j + 1)].reshape(fb, M)
+            d_act = dot_nt(cot, wd).astype(bf16).astype(f32)
+            d_pre = d_act * r.GP[s, :, c].astype(f32)
+            total = jnp.sum(d_pre, axis=0, keepdims=True)
+            for i in range(fb // 128):
+                at = j * (fb // 128) + i
+                r.SMG[at : at + 1] += total[:, 128 * i : 128 * (i + 1)]
+            r.GP[s, :, c] = d_pre.astype(bf16)
+        m1 = jnp.zeros((L, 1), f32)
+        m2 = jnp.zeros((L, 1), f32)
+        for q in range(4):
+            c = slice(q * Cw, (q + 1) * Cw)
+            dn = dot_nt(r.GP[s], r.WU[bq * q : bq * (q + 1)].reshape(Cw, Fw))
+            g = dn * r.VV[0:1, c]
+            m1 = m1 + jnp.sum(g, axis=1, keepdims=True)
+            m2 = m2 + jnp.sum(g * xhat_of(s, q), axis=1, keepdims=True)
+            r.DNP[q, s] = dn.astype(bf16)
+        lane = lax.broadcasted_iota(jnp.int32, (L, 128), 1)
+        both = jnp.where(lane == 0, m1, jnp.where(lane == 1, m2, 0.0)) * (1.0 / M)
+        pick = (
+            lax.broadcasted_iota(jnp.int32, (8, 128), 0) == lax.broadcasted_iota(jnp.int32, (8, 128), 1)
+        ).astype(f32)
+        r.ST[t, s] = lax.dot_general(
+            pick, both, (((1,), (1,)), ((), ())), precision=lax.Precision.HIGHEST, preferred_element_type=f32
+        )
+        ex_send(2, s, lambda q: r.DNP.at[q, s], lambda d: r.DNR.at[d - 1, s])
+        ex_send(3, s, lambda q: r.ST.at[t, s], lambda d: r.ST.at[t, s])
+
+    each(S, back_feed)
+
+    def grad_up(j):
+        c = pl.ds(pl.multiple_of(j * Cw, Cw), Cw)
+        rows = r.NRM[:, :, c].reshape(S * L, Cw)
+        g = dot_tn(rows, r.GP[...].reshape(S * L, Fw)).astype(bf16)
+        r.GU[pl.ds(j * bq, bq)] = g.reshape(bq, 4, rw, Fw)
+        for i in range(bq // 2):
+            to_y(1, j * (bq // 2) + i)
+
+    each(4, grad_up)
+    mid(0)
+
+    def back_norm(s):
+        ex_wait(2, s, lambda d: r.DNR.at[d - 1, s])
+        ex_wait(3, s, lambda d: r.ST.at[t ^ d, s])
+        dn = r.DNP[t, s].astype(f32)
+        for d in range(3):
+            dn = dn + r.DNR[d, s].astype(f32)
+        st = r.ST[0, s] + r.ST[1, s] + r.ST[2, s] + r.ST[3, s]
+        side = lax.broadcasted_iota(jnp.int32, (8, 128), 0)
+        col_of = lambda i: lax.dot_general(
+            st,
+            (side == i).astype(f32),
+            (((0,), (0,)), ((), ())),
+            precision=lax.Precision.HIGHEST,
+            preferred_element_type=f32,
+        )[:, :1]
+        m1, m2 = col_of(0), col_of(1)
+        inv = r.INV[s, :, :1]
+        xhat = (r.RES[t, s].astype(f32) - r.MU[s, :, :1]) * inv
+        cot = r.COT[s, :, :, tc].reshape(L, Cw).astype(f32)
+        for i, v in enumerate((cot, dn * xhat, dn)):
+            total = jnp.sum(v, axis=0, keepdims=True)
+            for k in range(Cw // 128):
+                at = Fw // 128 + i * (Cw // 128) + k
+                r.SMG[at : at + 1] += total[:, 128 * k : 128 * (k + 1)]
+        d_resid = cot + (dn * r.VV[0:1, tc] - m1 - xhat * m2) * inv
+        r.DR[s] = d_resid
+        db = d_resid.astype(bf16)
+        r.DB[s] = db
+        for q in range(4):
+            r.DMP[q, s] = dot_nt(db, wo(q)).astype(bf16)
+        ex_send(4, s, lambda q: r.DMP.at[q, s], lambda d: r.DMR.at[d - 1, s])
+
+    each(S, back_norm)
+    for q in range(4):
+        g = dot_tn(r.MIX[q].reshape(S * L, Cw), r.DB[...].reshape(S * L, Cw))
+        r.GA[bq * q : bq * (q + 1), :, :, 3 * Cw :] = g.astype(bf16).reshape(bq, 4, rw, Cw)
+
+    def out_rows(s):
+        for q in range(4):
+            c = slice(q * Cw, (q + 1) * Cw)
+            o = jnp.dot(r.ACT[s], r.WD[:, :, c].reshape(Fw, Cw), preferred_element_type=f32)
+            mine = (t == q).astype(f32)
+            o = o + mine * (r.RT[s] + r.VV[2:3, c])
+            r.OP[s, :, :, c] = o.astype(bf16).reshape(4 * nu, 16, Cw)
+        ex_send(5, s, lambda q: r.OP.at[s, pl.ds(nu * q, nu)], lambda d: r.OR.at[d - 1, s])
+
+    each(S, out_rows)
+
+    y_forward("C")
+    y_wait("C")
+
+    def windows(k):
+        return r.CTX[:, 4 * nu + 4 * k : 4 * nu + 4 * (k + 1)].reshape(S * nw, M)
+
+    conv = r.VV[3:4, tc]
+    pooled = 0.0
+    for k in range(3):
+        wk = r.WC[:, :, :, k * Cw : (k + 1) * Cw].reshape(M, Cw)
+        conv = conv + jnp.dot(windows(k), wk, preferred_element_type=f32)
+        pooled = pooled + r.CTX[:, 4 * nu + 4 * k : 4 * nu + 4 * (k + 1), :, tc].reshape(S * nw, Cw).astype(f32)
+    mask = r.MK[...].reshape(S * nw, 128)[:, :1]
+    done = 3 * lax.broadcasted_iota(jnp.int32, (nw, 128), 0) + 3
+    live = jnp.concatenate(
+        [(done.astype(f32) <= r.ev[s, 0:1, :]).astype(f32)[:, :1] for s in range(S)], axis=0
+    ) * mask
+    r.NEW[t] = (mask * conv).astype(bf16)
+    for d in (1, 2, 3):
+        put(remote(r.NEW.at[t], r.NEW.at[t], r.ts.at[5, d - 1], r.tr.at[5, d - 1], (b, t ^ d)))
+    d_conv = live * (conv - pooled * (1.0 / 3.0))
+    total = jnp.sum(d_conv, axis=0, keepdims=True)
+    for k in range(Cw // 128):
+        at = Fw // 128 + 3 * (Cw // 128) + k
+        r.SMG[at : at + 1] = total[:, 128 * k : 128 * (k + 1)]
+    r.DC[...] = d_conv.astype(bf16)
+    for k in range(3):
+        g = dot_tn(windows(k), r.DC[...])
+        r.GC[:, :, :, k * Cw : (k + 1) * Cw] = g.astype(bf16).reshape(nb, 4, rw, Cw)
+    for zz in range(G):
+        to_y(2, zz)
+    mid(1)
+
+    slope_row = Fw // 128 + 4 * (Cw // 128)
+
+    def back_attend(s):
+        ex_wait(4, s, lambda d: r.DMR.at[d - 1, s])
+        dm = r.DMP[t, s].astype(f32)
+        for d in range(3):
+            dm = dm + r.DMR[d, s].astype(f32)
+        dm = dm.astype(bf16)
+        lane = lax.broadcasted_iota(jnp.int32, (1, 128), 1)
+        for h in range(ht):
+            c = slice(h * hd, (h + 1) * hd)
+            cv = slice(Cw + h * hd, Cw + (h + 1) * hd)
+            p = r.PR[s, h]
+            dp = dot_nt(dm[:, c], r.KV[s, :, cv])
+            delta = jnp.sum(p * dp, axis=1, keepdims=True)
+            ds = p * (dp - delta)
+            part = jnp.sum(jnp.sum(ds * r.DIST[...], axis=0, keepdims=True), axis=1, keepdims=True)
+            r.SMG[slope_row : slope_row + 1] -= jnp.where(lane == t * ht + h, part, 0.0)
+            dr = (ds * scale).astype(bf16)
+            dq = jnp.dot(dr, r.KV[s, :, c], preferred_element_type=f32).astype(bf16)
+            dk = dot_tn(dr, r.Q[s, :, c]).astype(bf16)
+            dv = dot_tn(p.astype(bf16), dm[:, c]).astype(bf16)
+            r.Q[s, :, c] = dq
+            r.KV[s, :, c] = dk
+            r.KV[s, :, cv] = dv
+
+    each(S, back_attend)
+
+    def grad_proj(j):
+        c = pl.ds(pl.multiple_of(j * Cw, Cw), Cw)
+        gq = jnp.zeros((Cw, Cw), f32)
+        gkv = jnp.zeros((Cw, 2 * Cw), f32)
+        for s in range(S):
+            gq = gq + dot_tn(r.CTX[s, 8 * nu : 12 * nu, :, c].reshape(L, Cw), r.Q[s])
+            gkv = gkv + dot_tn(r.CTX[s, :, :, c].reshape(C3, Cw), r.KV[s])
+        rows = pl.ds(j * bq, bq)
+        r.GA[rows, :, :, :Cw] = gq.astype(bf16).reshape(bq, 4, rw, Cw)
+        r.GA[rows, :, :, Cw : 3 * Cw] = gkv.astype(bf16).reshape(bq, 4, rw, 2 * Cw)
+        for i in range(bq // 2):
+            to_y(3, j * (bq // 2) + i)
+
+    each(4, grad_proj)
+    put(remote(r.SMG, r.YS, r.gys.at[4, 0], r.gyr.at[4, 0], ypeer))
+    ex_sent(5, lambda q, s: r.OP.at[s, pl.ds(nu * q, nu)])
+
+    def own_out(s):
+        ex_wait(5, s, lambda d: r.OR.at[d - 1, s])
+        acc = r.OP[s, pl.ds(nu * t, nu)].astype(f32)
+        for d in range(3):
+            acc = acc + r.OR[d, s].astype(f32)
+        r.out[s] = acc.astype(bf16)
+
+    each(S, own_out)
+
+    def input_rows(s):
+        x = jnp.concatenate([r.Q[s], r.KV[s, 2 * L :]], axis=1)
+        for q in range(4):
+            c = slice(q * Cw, (q + 1) * Cw)
+            w = r.WA[bq * q : bq * (q + 1), :, :, : 3 * Cw].reshape(Cw, 3 * Cw)
+            o = dot_nt(x, w) + (t == q).astype(f32) * r.DR[s]
+            r.OP[s, :, :, c] = o.astype(bf16).reshape(4 * nu, 16, Cw)
+        ex_send(6, s, lambda q: r.OP.at[s, pl.ds(nu * q, nu)], lambda d: r.IR.at[d - 1, s])
+
+    each(S, input_rows)
+
+    mid(2)
+
+    def keep(o):
+        def store(i, acc):
+            o[i] = acc
+
+        return store
+
+    def hold(m):
+        def store(i, acc):
+            m[i] = acc.astype(bf16)
+
+        return store
+
+    def tier_back(k, m, tb):
+        for d in (1, 2, 3):
+            put(remote(m.at[t ^ d], tb.at[t], r.gts.at[k, d - 1], r.gtr.at[k, d - 1], (b, t ^ d)))
+
+    fin(0, keep(r.od))
+    fin(1, hold(r.MU_))
+    tier_back(0, r.MU_, r.TU)
+    remote(r.YS, r.YS, r.gys.at[4, 0], r.gyr.at[4, 0], ypeer).wait_recv()
+    r.ZS[z] = r.SMG[...] + r.YS[...]
+    for d in range(G - 1):
+        put(remote(r.ZS.at[z], r.ZS.at[z], r.gzs.at[4, d], r.gzr.at[4, d], (2 * zs[d + 1] + y, t)))
+    mid(3)
+    fin(2, hold(r.MC_))
+    tier_back(1, r.MC_, r.TC)
+    for d in range(G - 1):
+        at = r.ZS.at[zback[d + 1]]
+        remote(at, at, r.gzs.at[4, d], r.gzr.at[4, d], ypeer).wait_recv()
+    acc = r.ZS[0]
+    for zz in range(1, G):
+        acc = acc + r.ZS[zz]
+    r.os[t] = acc
+    for d in (1, 2, 3):
+        put(remote(r.os.at[t], r.os.at[t], r.gts.at[3, d - 1], r.gtr.at[3, d - 1], (b, t ^ d)))
+
+    def own_input(s):
+        ex_wait(6, s, lambda d: r.IR.at[d - 1, s])
+        acc = r.OP[s, pl.ds(nu * t, nu)].astype(f32)
+        for d in range(3):
+            acc = acc + r.IR[d, s].astype(f32)
+        r.ig[s] = acc
+
+    each(S, own_input)
+    fin(3, hold(r.MA_))
+    tier_back(2, r.MA_, r.TA)
+    for k, (m, tb, o) in enumerate(((r.MU_, r.TU, r.ou), (r.MC_, r.TC, r.oc), (r.MA_, r.TA, r.oa))):
+        o[t] = m[t].astype(f32)
+        for d in (1, 2, 3):
+            at = tb.at[t ^ d]
+            remote(at, at, r.gts.at[k, d - 1], r.gtr.at[k, d - 1], (b, t ^ d)).wait_recv()
+            o[t ^ d] = tb[t ^ d].astype(f32)
+    for d in (1, 2, 3):
+        at = r.os.at[t ^ d]
+        remote(at, at, r.gts.at[3, d - 1], r.gtr.at[3, d - 1], (b, t ^ d)).wait_recv()
+        at = r.NEW.at[t ^ d]
+        remote(at, at, r.ts.at[5, d - 1], r.tr.at[5, d - 1], (b, t ^ d)).wait_recv()
+    r.new[...] = r.NEW[...]
+
+    for cp in sends:
+        cp.wait_send()
+    for k, (g, yb, zb) in enumerate(grads):
+        for zz in range(G):
+            remote(yb.at[zz], yb.at[zz], r.gys.at[k, zz], r.gyr.at[k, zz], ypeer).wait_send()
+    ex_sent(0, lambda q, s: r.MIX.at[t, s])
+    ex_sent(1, lambda q, s: r.RES.at[t, s])
+    ex_sent(2, lambda q, s: r.DNP.at[q, s])
+    ex_sent(3, lambda q, s: r.ST.at[t, s])
+    ex_sent(4, lambda q, s: r.DMP.at[q, s])
+    ex_sent(6, lambda q, s: r.OP.at[s, pl.ds(nu * q, nu)])
+
+
+def whole_layer(nb, nu, ht, hd, wa, wu, wc, wd, sm, comp, mem, seg, cot, mk, ev, sl):
+    S, _, _, M = comp.shape
+    _, rw, _ = wa.shape
+    rd = wd.shape[0]
+    G, Cw, Fw, L = nb // 2, M // 4, nb * rd, 64 * nu
+    dma = pltpu.SemaphoreType.DMA
+    V = lambda shape, dtype=bf16: pltpu.VMEM(shape, dtype)
+    D4, A4, U4, C4 = (4, rd // 4, M), (4, rw, 4 * Cw), (4, rw, Fw), (4, rw, 3 * Cw)
+    ins = dict(wa=wa, wu=wu, wc=wc, wd=wd, sm=sm, comp=comp, mem=mem, seg=seg, cot=cot, mk=mk, ev=ev, sl=sl)
+    outs = dict(
+        out=((S, nu, 16, M), bf16),
+        ig=((S, nu, 16, M), f32),
+        new=((4, S * L // 3, Cw), bf16),
+        od=(D4, f32),
+        ou=(U4, f32),
+        oc=(C4, f32),
+        oa=(A4, f32),
+        os=((4, 24, 128), f32),
+    )
+    scratch = dict(
+        WA=V((nb,) + A4),
+        WU=V((nb,) + U4),
+        WC=V((nb,) + C4),
+        WD=V((nb, rd, M)),
+        SM=V((nb, 4, 16, 128), f32),
+        CTX=V((S, 12 * nu, 16, M)),
+        COT=V((S, 4 * nu, 16, M)),
+        MK=V((S, 4, L // 12, 128), f32),
+        DIST=V((L, 3 * L), f32),
+        VV=V((8, max(M, Fw)), f32),
+        SMG=V((24, 128), f32),
+        Q=V((S, L, Cw)),
+        KV=V((S, 3 * L, 2 * Cw)),
+        PR=V((S, ht, L, 3 * L), f32),
+        MIX=V((4, S, L, Cw)),
+        RT=V((S, L, Cw), f32),
+        RES=V((4, S, L, Cw)),
+        MU=V((S, L, 128), f32),
+        INV=V((S, L, 128), f32),
+        NRM=V((S, L, M)),
+        ACT=V((S, L, Fw)),
+        GP=V((S, L, Fw)),
+        DNP=V((4, S, L, Cw)),
+        DNR=V((3, S, L, Cw)),
+        ST=V((4, S, 8, L), f32),
+        DR=V((S, L, Cw), f32),
+        DB=V((S, L, Cw)),
+        DMP=V((4, S, L, Cw)),
+        DMR=V((3, S, L, Cw)),
+        OP=V((S, 4 * nu, 16, M)),
+        OR=V((3, S, nu, 16, M)),
+        IR=V((3, S, nu, 16, M)),
+        NEW=V((4, S * L // 3, Cw)),
+        DC=V((S * L // 3, Cw)),
+        GD=V((nb,) + D4),
+        GU=V((nb,) + U4),
+        GC=V((nb,) + C4),
+        GA=V((nb,) + A4),
+        YD=V((G,) + D4),
+        YU=V((G,) + U4),
+        YC=V((G,) + C4),
+        YA=V((G,) + A4),
+        ZD=V((G - 1,) + D4),
+        ZU=V((G - 1,) + U4),
+        ZC=V((G - 1,) + C4),
+        ZA=V((G - 1,) + A4),
+        YS=V((24, 128), f32),
+        ZS=V((G, 24, 128), f32),
+        MU_=V(U4),
+        MC_=V(C4),
+        MA_=V(A4),
+        TU=V(U4),
+        TC=V(C4),
+        TA=V(A4),
+        lsem=dma((12,)),
+        ts=dma((6, 3)),
+        tr=dma((6, 3)),
+        zsd=dma((5, G)),
+        zr=dma((5, G)),
+        ys=dma((5, G)),
+        yr=dma((5, G)),
+        acs=dma((7, 3)),
+        acr=dma((7, 3)),
+        es=dma((7, S, 3)),
+        er=dma((7, S, 3)),
+        gys=dma((5, G)),
+        gyr=dma((5, G)),
+        gzs=dma((5, G)),
+        gzr=dma((5, G)),
+        gts=dma((4, 3)),
+        gtr=dma((4, 3)),
+    )
+    names = list(ins) + list(outs) + list(scratch)
+    near = ("ev", "sl")
+    return pl.pallas_call(
+        functools.partial(layer_kernel, names, (nb, nu, S, ht, hd, M, Cw, rw, rd)),
+        out_shape=[jax.ShapeDtypeStruct(s, d) for s, d in outs.values()],
+        in_specs=[VM if n in near else ANY for n in ins],
+        out_specs=[VM] * len(outs),
+        scratch_shapes=list(scratch.values()),
+        compiler_params=pltpu.CompilerParams(
+            collective_id=9, has_side_effects=True, vmem_limit_bytes=63 * 2**20
+        ),
+        name="whole_layer",
+    )(*ins.values())
+
+
+def prepared(nb, segment, memory, compressed, evicted, window_mask, cotangent, w, b_up, vectors, w_up, w_conv, slopes):
+    S, R, M = segment.shape
+    rw, rd, rs = w[0].shape[0], b_up.shape[0], vectors[0].shape[0]
+    b, t = lax.axis_index("batch"), lax.axis_index("tier")
+    Cw, nu, W = M // 4, R // 16, R // 3
+    wa = jnp.stack(w).reshape(4, rw, 4, Cw).transpose(2, 1, 0, 3).reshape(4, rw, 4 * Cw)
+    wu = w_up.reshape(rw, nb, 4, rd).transpose(2, 0, 1, 3).reshape(4, rw, nb * rd)
+    wc = w_conv.reshape(3, rw, 4, Cw).transpose(2, 1, 0, 3).reshape(4, rw, 3 * Cw)
+    four = jnp.stack(vectors).astype(f32)
+    four = lax.dynamic_update_slice(jnp.zeros((4, Cw), f32), four, (0, lax.rem(rs * (4 * b + t), Cw)))
+    low = jnp.zeros((8, 128), f32).at[0, :rd].set(b_up.astype(f32))
+    sm = jnp.concatenate([four.reshape(8, 128), low], axis=0)
+    mem = memory.reshape(S, W, 3, M).transpose(0, 2, 1, 3)
+    mk = jnp.broadcast_to(window_mask.astype(f32)[:, :, None], (S, W, 128))
+    ev = jnp.broadcast_to(evicted.astype(f32)[:, None, None], (S, 8, 128))
+    sl = jnp.broadcast_to(slopes[:, None], (slopes.shape[0], 128))
+    cut = lambda v: v.reshape(S, nu, 16, M)
+    return wa, wu, wc, sm, cut(compressed), mem, cut(segment), cut(cotangent), mk, ev, sl
+
+
+def per_device_fused(
+    nb,
+    segment,
+    memory,
+    compressed,
+    evicted,
+    window_mask,
+    cotangent,
+    w_query,
+    w_key,
+    w_value,
+    w_output,
+    w_up,
+    b_up,
+    w_down,
+    b_down,
+    ln_gain,
+    ln_bias,
+    w_conv,
+    b_conv,
+    slopes,
+):
+    S, R, M = segment.shape
+    heads = slopes.shape[0]
+    rw, rd, rs = w_query.shape[0], w_down.shape[0], b_down.shape[0]
+    b, t = lax.axis_index("batch"), lax.axis_index("tier")
+    Cw, Fw, seg_len = M // 4, nb * rd, 4 * R
+    index = 4 * b + t
+    wa, wu, wc, sm, comp, mem, seg, cot, mk, ev, sl = prepared(
+        nb,
+        segment,
+        memory,
+        compressed,
+        evicted,
+        window_mask,
+        cotangent,
+        (w_query, w_key, w_value, w_output),
+        b_up,
+        (ln_gain, ln_bias, b_down, b_conv),
+        w_up,
+        w_conv,
+        slopes,
+    )
+    out, ig, NEW, OD, OU, OC, OA, OS = whole_layer(
+        nb, R // 16, heads // 4, M // heads, wa, wu, wc, w_down, sm, comp, mem, seg, cot, mk, ev, sl
+    )
+    nw = seg_len // 3
+    NEW = NEW.reshape(4, S, nw, Cw).transpose(1, 2, 0, 3).reshape(S, nw, M)
+    slot_offset = seg_len - nw
+    local_rows = jnp.arange(R, dtype=jnp.int32) + t * R
+    padded = jnp.concatenate([jnp.zeros((S, slot_offset, M), bf16), NEW], axis=1)
+    slot_rows = lax.dynamic_slice_in_dim(padded, t * R, R, 1)
+    written = (local_rows[None, :] >= slot_offset) & (
+        3 * (local_rows[None, :] - slot_offset) + 3 <= evicted[:, None]
+    )
+    new_compressed = jnp.where(written[..., None], slot_rows, compressed)
+    new_memory = jnp.where((local_rows[None, :] < evicted[:, None])[..., None], segment, memory)
+    OA = OA.reshape(4, rw, 4, Cw).transpose(2, 1, 0, 3).reshape(4, rw, M)
+    OU = OU.reshape(4, rw, nb, rd).transpose(1, 2, 0, 3).reshape(rw, nb * 4 * rd)
+    OC = OC.reshape(4, rw, 3, Cw).transpose(2, 1, 0, 3).reshape(3, rw, M)
+    OS = OS.reshape(4, -1)
+    vec = lambda o: lax.dynamic_slice_in_dim(OS[:, o : o + Cw].reshape(M), index * rs, rs)
+    gub_out = lax.dynamic_slice(OS, (t, b * rd), (1, rd)).reshape(rd)
+    gslopes = jnp.sum(OS[:, Fw + 4 * Cw : Fw + 4 * Cw + heads], axis=0)
+    return (
+        out.reshape(S, R, M),
+        ig.reshape(S, R, M),
+        new_memory,
+        new_compressed,
+        OA[0],
+        OA[1],
+        OA[2],
+        OA[3],
+        OU,
+        gub_out,
+        OD.reshape(rd, M),
+        vec(Fw),
+        vec(Fw + Cw),
+        vec(Fw + 2 * Cw),
+        OC,
+        vec(Fw + 3 * Cw),
+        gslopes,
+    )
+
+
 def solution(mesh):
     both = ("batch", "tier")
     rows = P("batch", "tier", None)
     mat, vec = P(both, None), P(both)
+    nb = mesh.shape["batch"]
+
+    def body(*args):
+        fused = args[6].shape[0] % 16 == 0 and args[12].shape[0] == 128
+        return (per_device_fused if fused else per_device)(nb, *args)
+
     return jax.shard_map(
-        functools.partial(per_device, mesh.shape["batch"]),
+        body,
         mesh=mesh,
         in_specs=(
             (rows, rows, rows, P("batch"), P("batch", "tier"), rows)

time: 609 us -> 292 us (0.48); the launches traced: 601 us -> 291 us
  matrix products: 102 us -> 0 us
  Pallas kernels: 347 us -> 263 us
  local copies, waits for them, and re-layouts: 96.6 us -> 22.4 us
  other arithmetic: 47.8 us -> 5 us
    dot_general x26 -> x0, matrix products: 96.7 us -> none  [the longest x9 22.7 us: dot_tn(): lax.dot_general(a, b, (((0,), (0,)), ((), ())), preferred_element_type=f32)]
    pallas_call x9 -> x1, Pallas kernels: 347 us -> 263 us  [whole_layer(): pl.pallas_call(functools.partial(layer_kernel, names, (nb, nu, S, ht, hd,...]
    convert_element_type x9 -> x0, local copies, waits for them, and re-layouts: 21.1 us -> none  [the longest x2 7.32 us: per_device(): resid = RES.transpose(1, 0, 2).reshape(T, M).astype(f32)]
    reshape x24 -> x15, local copies, waits for them, and re-layouts: 23.9 us -> 7.03 us  [the longest x3 1.2 us: prepared(): w_conv.reshape(3, rw, 4, Cw).transpose(2, 1, 0, 3).reshape(4, rw, 3 * Cw)]
    reduce_sum x8 -> x1, other arithmetic: 15.3 us -> 0.53 us  [per_device_fused(): gslopes = jnp.sum(OS[:, Fw + 4 * Cw:Fw + 4 * Cw + heads], axis=0)]
    sub x1 -> x0, other arithmetic: 14.5 us -> none  [per_device(): d_scores = probs * (d_probs - delta)]
    another operation x14 -> x8, local copies, waits for them, and re-layouts: 12.4 us -> 2.22 us  [prepared(): jnp.stack(w).reshape(4, rw, 4, Cw).transpose(2, 1, 0, 3)]
    dot_general x5 -> x0, local copies, waits for them, and re-layouts: 9.08 us -> none  [dot_tn(): lax.dot_general(a, b, (((0,), (0,)), ((), ())), preferred_element_type=f32)]
where the time goes in v2:
time: 292 us; the launch traced here: 291 us
  Pallas kernels  263 us (90%)
  local copies, waits for them, and re-layouts  22.4 us (8%)
  other arithmetic  5 us (2%)
    pallas_call x1, Pallas kernels, whole_layer(): pl.pallas_call(functools.partial(layer_kernel, names, (nb, nu, S, ht, hd,...  263 us
    unnamed x49, local copies, waits for them, and re-layouts  7.15 us

profile of v2, /device:TPU:11, one launch (start us, length us, event | category | flops | bytes accessed | tf_op | source)
XLA Modules:
  0.0 291.2 jit_solution(7845925689269699832)
XLA Ops:
  0.7 0.7 maximum_convert_fusion
  1.7 0.7 pad_convert_fusion
  2.4 0.6 pad_maximum_fusion.refs_4_
  3.0 0.9 stack.30
  4.0 0.9 stack.31
  5.3 0.6 maximum_bitcast_fusion
  5.9 0.9 reshape.245.refs_0_
  7.1 0.9 copy.93
  8.2 0.8 reshape.247.refs_1_
  9.3 0.9 reshape.249.refs_2_
  10.3 0.7 broadcast_in_dim.19.refs_9_
  11.0 0.7 broadcast_in_dim.20.refs_10_
  11.6 0.7 broadcast_in_dim.21.refs_11_
  12.3 262.8 %whole_layer.1 = (bf16[4,3,16,1024]{3,2,1,0:T(8,128)(2,1)}, f32[4,3,16,1024]{3,2,1,0:T(8,128)}, bf16[4,256,256]{2,1,0:T(8,128)(2,1)}, f32[4,32,1024]{2,1,0:T(8,1...) custom-call(bf16[4,32,1024]{2,1,0:T(8,128)(2,1)} %reshape.245.refs_0_, ...), custom_call_target="tpu_custom_call" | custom-call | tf_op jit(solution)/shard_map/whole_layer/pallas_call | solution.py:1165
  275.1 1.1 copy.83
  276.6 1.0 reshape.262
  278.4 0.7 copy.79
  279.2 0.7 copy.80
  280.0 0.7 copy.81
  280.7 0.7 copy.82
  281.9 0.9 reshape.270
  283.1 0.9 fusion
  284.0 0.6 dynamic_slice.20
  284.6 0.6 dynamic_slice.21
  285.2 0.6 dynamic_slice.22
  285.8 0.6 dynamic_slice.23
  286.3 0.6 dynamic-slice_bitcast_fusion
  286.9 0.5 slice_reduce_fusion
  287.5 0.9 broadcast_select_fusion
  288.3 0.7 copy.101
  289.1 0.9 copy.102
  290.4 0.8 copy.103
  (70 shorter events, 4.1 us)
Async XLA Ops:
  0.7 4.3 %copy-start.11 = (bf16[32,1024]{1,0:T(8,128)(2,1)S(1)}, bf16[32,1024]{1,0:T(8,128)(2,1)}, u32[]{:S(2)}) copy-start(bf16[32,1024]{1,0:T(8,128)(2,1)} %param.29) | copy-start | bytes 196612
  0.7 4.5 %copy-start.12 = (bf16[32,1024]{1,0:T(8,128)(2,1)S(1)}, bf16[32,1024]{1,0:T(8,128)(2,1)}, u32[]{:S(2)}) copy-start(bf16[32,1024]{1,0:T(8,128)(2,1)} %param.30) | copy-start | bytes 196612
  5.1 1.7 copy-start.2
  6.8 1.2 copy-start.9
  8.0 1.0 copy-start.10
  9.0 1.2 copy-start.14
  9.0 1.9 copy-start.16
  9.0 2.6 copy-start.15
  276.6 1.0 copy-start.6
  279.1 2.3 copy-start.7
  281.6 1.2 copy-start.5
  281.9 1.2 copy-start
  282.9 1.0 copy-start.13
  282.9 4.5 %copy-start.1 = (bf16[4,48,1024]{2,1,0:T(8,128)(2,1)S(1)}, bf16[4,48,1024]{2,1,0:T(8,128)(2,1)}, u32[]{:S(2)}) copy-start(bf16[4,48,1024]{2,1,0:T(8,128)(2,1)} %param.21) | copy-start | bytes 1179652
  283.9 4.4 %copy-start.8 = (bf16[4,3,16,1024]{3,2,1,0:T(8,128)(2,1)S(1)}, bf16[4,3,16,1024]{3,2,1,0:T(8,128)(2,1)}, u32[]{:S(2)}) copy-start(bf16[4,3,16,1024]{3,2,1,0:T(8,128)(2,1)} %get-tuple-element.37) | copy-start | bytes 1179652
  287.5 1.6 copy-start.3
  289.1 1.3 copy-start.4

commit v3 on v1

--- a/solution.py
+++ b/solution.py
@@ -12,6 +12,7 @@
 MESH = pl.DeviceIdType.MESH
 ANY = pl.BlockSpec(memory_space=pl.ANY)
 VM = pl.BlockSpec(memory_space=pltpu.VMEM)
+SM = pl.BlockSpec(memory_space=pltpu.SMEM)
 f32 = jnp.float32
 bf16 = jnp.bfloat16
 
@@ -529,12 +530,1100 @@
     )
 
 
+class Names:
+    def __init__(self, names, refs):
+        for name, ref in zip(names, refs):
+            setattr(self, name, ref)
+
+
+def layer_kernel(names, shape, *refs):
+    r = Names(names, refs)
+    nb, nu, S, ht, hd, M, Cw, rw, rd, rs = shape
+    R = 16 * nu
+    G, bq = nb // 2, nb // 4
+    L = 16 * 4 * nu
+    C3 = 3 * L
+    nw = L // 3
+    Fw = nb * rd
+    scale = 1.0 / math.sqrt(hd)
+    b, t, z, y, zs, zback = places(G)
+    mate, ends = z ^ 1, (z == 0) | (z == G - 1)
+    ypeer = (b ^ 1, t)
+    tc = pl.ds(pl.multiple_of(t * Cw, Cw), Cw)
+    sends = []
+
+    def got(ref, sem):
+        pltpu.make_async_copy(ref, ref, sem).wait()
+
+    def left_all(ref, sem):
+        sends.append((ref, sem))
+
+    def each(n, body, between=None):
+        def step(i, c):
+            body(i)
+            for at, then in (between or {}).items():
+                pl.when(i == at)(then)
+            return c
+
+        lax.fori_loop(0, n, step, 0)
+
+    def ex_send(e, sem, src, dst):
+        for d in (1, 2, 3):
+            remote(src(t ^ d), dst(d), r.es.at[e], sem, (b, t ^ d)).start()
+
+    def spread_send(e, s, arr):
+        at = arr.at[t, s]
+        for d in (1, 2):
+            remote(at, at, r.es.at[e], r.er.at[e, s, d - 1], (b, t ^ d)).start()
+
+    def spread_pass(e, s, arr):
+        at = arr.at[t ^ 2, s]
+        got(at, r.er.at[e, s, 1])
+        remote(at, at, r.es.at[e], r.er.at[e, s, 0], (b, t ^ 1)).start()
+
+    def spread_wait(e, s, arr):
+        @pl.when(s < S - 1)
+        def _():
+            spread_pass(e, s + 1, arr)
+
+        got(arr.at[0:2, s], r.er.at[e, s, 0])
+
+    def fold_send(e, s, out, into):
+        for i, d in enumerate((1, 3)):
+            remote(out.at[t ^ d, s], into.at[i, s], r.es.at[e], r.er.at[e, s, i], (b, t ^ 1)).start()
+
+    def fold_pass(e, s, out, into):
+        at = into.at[1, s]
+        got(at, r.er.at[e, s, 1])
+        out[t ^ 2, s] = (out[t ^ 2, s].astype(f32) + at[...].astype(f32)).astype(bf16)
+        remote(out.at[t ^ 2, s], into.at[2, s], r.es.at[e], r.er.at[e, s, 0], (b, t ^ 2)).start()
+
+    def fold_late(e, s, out, into):
+        @pl.when(s > 0)
+        def _():
+            fold_pass(e, s - 1, out, into)
+
+    def folded(e, s, out, into):
+        got(into.at[0:2, s], r.er.at[e, s, 0])
+        return out[t, s].astype(f32) + into[0, s].astype(f32) + into[2, s].astype(f32)
+
+    def here(src, dst, i):
+        cp = pltpu.make_async_copy(src, dst, r.lsem.at[i])
+        cp.start()
+        return cp
+
+    wide = lambda at, size: pl.ds(pl.multiple_of(at, 128), size)
+    mats = (r.w_query, r.w_key, r.w_value, r.w_output)
+    whole = {"S": r.SM, "A": r.WA, "U": r.WU, "C": r.WC}
+    index = {"S": 0, "A": 1, "U": 2, "C": 3}
+
+    def cuts(n, q):
+        if n == "S":
+            return [(r.SM.at[b, t], r.SM.at[b, t])]
+        if n == "A":
+            return [(w.at[:, wide(Cw * q, Cw)], r.WA.at[b, t, :, i * Cw : (i + 1) * Cw]) for i, w in enumerate(mats)]
+        if n == "U":
+            return [
+                (r.w_up.at[:, wide((4 * i + q) * rd, rd)], r.WU.at[b, t, :, i * rd : (i + 1) * rd]) for i in range(nb)
+            ]
+        return [(r.w_conv.at[i, :, wide(Cw * q, Cw)], r.WC.at[b, t, :, i * Cw : (i + 1) * Cw]) for i in range(3)]
+
+    def tier_start(n):
+        i = index[n]
+        if n != "S":
+            for src, dst in cuts(n, t):
+                here(src, dst, i)
+        for d in (1, 2, 3):
+            for src, dst in cuts(n, t ^ d):
+                remote(src, dst, r.ts.at[i], r.tr.at[i], (b, t ^ d)).start()
+        left_all(whole[n].at[b, 0:3], r.ts.at[i])
+
+    def tier_wait(n):
+        i = index[n]
+        if n != "S":
+            got(whole[n].at[b, t], r.lsem.at[i])
+        got(whole[n].at[b, 0:3], r.tr.at[i])
+
+    def if_(cond, body):
+        pl.when(cond)(body)
+
+    right, left = (2 * z + 2 + y, t), (2 * z - 2 + y, t)
+    parts = {"S": [(r.SM, 0, 0, 4, 0)], "C": [(r.WC, 1, 0, 4, 1)], "X": [(r.WC, 2, 0, 4, 2)]}
+    for i, (n, w, size) in enumerate((("A", r.WA, 2), ("U", r.WU, 2), ("D", r.WD, rd // 2))):
+        parts[n] = [(w, 3 + 2 * i + h, h * size, size, 3 + i) for h in (0, 1)]
+
+    def chunk_of(n, part, zz, col=None):
+        w, k, at, size, _ = part
+        col = ((1 - y) if n == "X" else y) if col is None else col
+        return w.at[2 * zz + col, pl.ds(at, size)]
+
+    def hop(part, at, j, way):
+        k = part[1]
+        peer, past = (right, z < G - 1) if way == 0 else (left, z > 0)
+        return past, remote(at, at, r.zs.at[part[4]], r.zr.at[way, k, j], peer)
+
+    def own_z(n):
+        for part in parts[n]:
+            for way in (0, 1):
+                past, cp = hop(part, chunk_of(n, part, z), 0, way)
+                if_(past, cp.start)
+
+    def own_y(n):
+        for part in parts[n]:
+            at, k = chunk_of(n, part, z), part[4]
+            remote(at, at, r.ys.at[k], r.yr.at[k], ypeer).start()
+
+    def arrivals(n, step, js):
+        for j in js:
+            for part in parts[n]:
+                for way in (0, 1):
+                    zz = z - j if way == 0 else z + j
+                    step(part, j, way, zz, chunk_of(n, part, zz), zz >= 0 if way == 0 else zz < G)
+
+    def onward(n, *js):
+        def step(part, j, way, zz, at, there):
+            k = part[1]
+
+            def body():
+                got(at, r.zr.at[way, k, j - 1])
+                if j < G - 1:
+                    past, cp = hop(part, at, j, way)
+                    if_(past, cp.start)
+                if n not in "CX":
+                    remote(at, at, r.ys.at[part[4]], r.yr.at[part[4]], ypeer).start()
+
+            if_(there, body)
+
+        arrivals(n, step, js or range(1, G))
+
+    def all_sent(n):
+        w, k = parts[n][0][0], parts[n][0][4]
+        if_(ends, lambda: got(w.at[0:1], r.zs.at[k]))
+        if_(~ends, lambda: got(w.at[0:5], r.zs.at[k]))
+        if n != "X":
+            got(w.at[0 : 1 if n == "C" else G], r.ys.at[k])
+
+    def y_wait(n):
+        w, k = parts[n][0][0], parts[n][0][4]
+        got(w.at[0 : 1 if n == "C" else G], r.yr.at[k])
+
+    def small_start():
+        lane = lax.broadcasted_iota(jnp.int32, (8, 128), 1)
+        side = lax.broadcasted_iota(jnp.int32, (8, 128), 0)
+        spot = lax.rem(4 * b + t, Cw // rs)
+        half, group = spot // (128 // rs), lax.rem(spot, 128 // rs)
+        for q, v in enumerate((r.gain, r.bias, r.bdown, r.bconv)):
+            r.SMG[q : q + 1, :rs] = v[...].astype(f32)
+        r.SMG[4:5, :rd] = r.bup[...].astype(f32)
+        acc = jnp.zeros((8, 128), f32)
+        for q in range(4):
+            turned = pltpu.roll(jnp.broadcast_to(r.SMG[q : q + 1], (8, 128)), rs * group, 1)
+            mine = (side == 2 * q + half) & (lane >= rs * group) & (lane < rs * (group + 1))
+            acc = jnp.where(mine, turned, acc)
+        r.SM[b, t, 0:8] = acc
+        r.SM[b, t, 8:16] = jnp.broadcast_to(r.SMG[4:5], (8, 128))
+        tier_start("S")
+
+    def memory_rows():
+        W = R // 3
+        to, frm = (lax.broadcasted_iota(jnp.int32, (R, R), axis) for axis in (0, 1))
+        tap = (to >= W).astype(jnp.int32) + (to >= 2 * W).astype(jnp.int32)
+        order = (frm == 3 * (to - W * tap) + tap).astype(bf16)
+        for s in range(S):
+            rows = jnp.dot(order, r.mem[s], preferred_element_type=f32).astype(bf16)
+            for i in range(3):
+                r.CTX[s, 4 * nu + 4 * i + t] = rows[W * i : W * (i + 1)]
+            square = lambda axis: lax.broadcasted_iota(jnp.int32, (R // 3, R // 3), axis)
+            line = jnp.broadcast_to(r.mask[s : s + 1].astype(f32), (R // 3, R // 3))
+            col = jnp.sum(jnp.where(square(0) == square(1), line, 0.0), axis=1, keepdims=True)
+            r.MK[s, t] = jnp.broadcast_to(col, (R // 3, 128))
+
+    def rows_of(src, buf, first):
+        at = lambda q: buf.at[:, pl.ds(first + nu * q, nu)]
+        parts = [(src.at[:, 16 * i : 16 * i + 16], buf.at[:, first + nu * t + i]) for i in range(nu)]
+        return parts, at, True
+
+    def held(at):
+        return [(at(t), at(t))], at, False
+
+    pieces = [
+        rows_of(r.seg, r.CTX, 8 * nu),
+        rows_of(r.comp, r.CTX, 0),
+        held(lambda q: r.CTX.at[:, 4 * nu + q]),
+        held(lambda q: r.CTX.at[:, 4 * nu + 4 + q]),
+        held(lambda q: r.CTX.at[:, 4 * nu + 8 + q]),
+        rows_of(r.cot, r.COT, 0),
+        held(lambda q: r.MK.at[:, q]),
+    ]
+
+    group = lambda i: 0 if i < 5 else i - 4
+    grouped = [(r.CTX, 3 * nu), (r.COT, nu), (r.MK, 1)]
+
+    def act_start(*which):
+        for i in which:
+            cut, at, far = pieces[i]
+            g = group(i)
+            for src, dst in cut:
+                if far:
+                    here(src, dst, 4 + g)
+                remote(src, dst, r.acs.at[g], r.acc.at[g], (b, t ^ 1)).start()
+                remote(src, dst, r.acs.at[g], r.acx.at[i], (b, t ^ 2)).start()
+
+    def act_forward(*which):
+        for i in which:
+            at = pieces[i][1](t ^ 2)
+            got(at, r.acx.at[i])
+            remote(at, at, r.acs.at[group(i)], r.acf.at[group(i)], (b, t ^ 1)).start()
+
+    def act_wait(g):
+        buf, n = grouped[g]
+        got(buf.at[:, 0:n], r.acc.at[g])
+        got(buf.at[:, 0:n], r.acf.at[g])
+        if g < 2:
+            got(buf.at[:, 0 : n if g else 2 * nu], r.lsem.at[4 + g])
+
+    def act_sent():
+        for g, (buf, n) in enumerate(grouped):
+            got(buf.at[:, 0 : 3 * n], r.acs.at[g])
+
+    def table():
+        row = lax.broadcasted_iota(jnp.int32, (L, C3), 0) + 2 * L
+        col = lax.broadcasted_iota(jnp.int32, (L, C3), 1)
+        inner = col - L
+        k1 = (inner >= nw).astype(jnp.int32)
+        k2 = (inner >= 2 * nw).astype(jnp.int32)
+        win = inner - nw * (k1 + k2)
+        pos = jnp.where((col >= L) & (col < 2 * L), L + 3 * win + k1 + k2, col)
+        r.DIST[...] = jnp.where(pos <= row, (row - pos).astype(f32) * (1.0 / C3), 1e30)
+        r.SMG[...] = jnp.zeros_like(r.SMG)
+
+    def seg_rows(s):
+        return r.CTX[s, 8 * nu : 12 * nu].reshape(L, M)
+
+    def project(s):
+        rows = r.CTX[s].reshape(C3, M)
+        kv = jnp.dot(rows, r.WA[:, :, :, Cw : 3 * Cw].reshape(M, 2 * Cw), preferred_element_type=f32)
+        r.KV[s] = kv.astype(bf16)
+        q = jnp.dot(seg_rows(s), r.WA[:, :, :, :Cw].reshape(M, Cw), preferred_element_type=f32)
+        r.Q[s] = q.astype(bf16)
+
+
+    def attend(s):
+        for h in range(ht):
+            c = slice(h * hd, (h + 1) * hd)
+            raw = dot_nt(r.Q[s, :, c], r.KV[s, :, c])
+            scores = raw * scale - r.slopes[t * ht + h] * r.DIST[...]
+            e = jnp.exp(scores - jnp.max(scores, axis=1, keepdims=True))
+            p = e * (1.0 / jnp.sum(e, axis=1, keepdims=True))
+            r.PR[s, h] = p
+            v = r.KV[s, :, Cw + h * hd : Cw + (h + 1) * hd]
+            r.MIX[t, s, :, c] = jnp.dot(p.astype(bf16), v, preferred_element_type=f32).astype(bf16)
+        spread_send(0, s, r.MIX)
+
+
+    def wo(q):
+        return r.WA[bq * q : bq * (q + 1), :, :, 3 * Cw :].reshape(Cw, Cw)
+
+    def residual(s):
+        spread_wait(0, s, r.MIX)
+        acc = r.CTX[s, 8 * nu : 12 * nu, :, tc].reshape(L, Cw).astype(f32)
+        for q in range(4):
+            acc = acc + jnp.dot(r.MIX[q, s], wo(q), preferred_element_type=f32)
+        r.RT[s] = acc
+        r.RES[t, s] = acc.astype(bf16)
+        spread_send(1, s, r.RES)
+
+    def vectors():
+        for q in range(4):
+            block = r.SM[bq * q, 0, 0:8]
+            for bb in range(bq * q, bq * (q + 1)):
+                for tt in range(4):
+                    if bb != bq * q or tt:
+                        block = block + r.SM[bb, tt, 0:8]
+            for i in range(8):
+                at = q * Cw + 128 * (i % 2)
+                r.VV[i // 2 : i // 2 + 1, at : at + 128] = block[i : i + 1]
+        for bb in range(nb):
+            r.VV[4:5, bb * rd : (bb + 1) * rd] = r.SM[bb, t, 8:9, :rd]
+
+    def xhat_of(s, q):
+        return (r.RES[q, s].astype(f32) - r.MU[s, :, :1]) * r.MU[s, :, 1:2]
+
+    def feed(s):
+        spread_wait(1, s, r.RES)
+        parts = [r.RES[q, s].astype(f32) for q in range(4)]
+        mu = sum(jnp.sum(x, axis=1, keepdims=True) for x in parts) * (1.0 / M)
+        var = sum(jnp.sum((x - mu) * (x - mu), axis=1, keepdims=True) for x in parts) * (1.0 / M)
+        inv = lax.rsqrt(var + norm_eps)
+        lane = lax.broadcasted_iota(jnp.int32, (L, 128), 1)
+        r.MU[s] = jnp.where(lane == 0, mu, inv)
+        for q in range(4):
+            c = slice(q * Cw, (q + 1) * Cw)
+            rows = ((parts[q] - mu) * inv) * r.VV[0:1, c] + r.VV[1:2, c]
+            r.NRM[s, :, :, c] = rows.astype(bf16).reshape(4 * nu, 16, Cw)
+        fb = Fw // 4
+        for j in range(4):
+            c = slice(j * fb, (j + 1) * fb)
+            pre = jnp.dot(r.NRM[s].reshape(L, M), r.WU[:, :, :, c].reshape(M, fb), preferred_element_type=f32) + r.VV[4:5, c]
+            phi = 0.5 + 0.5 * lax.erf(pre * math.sqrt(0.5))
+            r.ACT[s, :, c] = (pre * phi).astype(bf16)
+            r.GP[s, :, c] = (phi + pre * (jnp.exp(-0.5 * pre * pre) * (1.0 / math.sqrt(2 * math.pi)))).astype(bf16)
+
+
+    def turn(j):
+        low = lax.rem(G - j, G)
+        inner = jnp.where(z == 1, low, G - 1 - low)
+        return jnp.where(z == 0, G - 1 - j, jnp.where(z == G - 1, j, inner))
+
+    grads = [(r.GD, r.YD, r.ZD), (r.GU, r.YU, r.ZU), (r.GC, r.YC, r.ZC), (r.GA, r.YA, r.ZA)]
+
+    def to_y(k, zz):
+        g, yb, zb = grads[k]
+        remote(g.at[2 * zz + (1 - y)], yb.at[zz], r.gys.at[k], r.gyr.at[k, zz], ypeer).start()
+
+    def plus(into, *others):
+        def add(i):
+            acc = into[i].astype(f32)
+            for o in others:
+                acc = acc + o[i].astype(f32)
+            into[i] = acc.astype(bf16)
+
+        each(into.shape[0], add)
+
+    def pass_on(i, at, zb, o, sem):
+        @pl.when((o != mate) & ~ends)
+        def _():
+            slot = lax.rem(o, 2)
+            got(zb.at[slot], r.gzr.at[sem, slot])
+            plus(at, zb.at[slot])
+
+        to = jnp.where(ends, mate, o)
+        slot = jnp.where(o == mate, 2, jnp.where(ends, lax.rem(o, 2), 3))
+        remote(at, zb.at[slot], r.gzs.at[sem], r.gzr.at[sem, jnp.minimum(slot, 2)], (2 * to + y, t)).start()
+
+    def mid(k, *steps):
+        g, yb, zb = grads[k]
+        for i in steps or range(G - 1):
+            o = turn(i)
+            at = yb.at[o]
+            got(at, r.gyr.at[k, o])
+            plus(at, g.at[2 * o + y])
+            pass_on(i, at, zb, o, k)
+
+    def mid_c(*steps):
+        for i in steps or range(G - 1):
+            o = turn(i)
+            for c, col in enumerate((1 - y, y)):
+                pass_on(i, r.GC.at[2 * o + col], r.ZC.at[c], o, (2, 4)[c])
+
+    def arrived(zb, sem):
+        got(zb.at[2:4], r.gzr.at[sem, 2])
+
+    def summed(at, zb, more, store):
+        def total(i):
+            acc = at[i].astype(f32)
+            for o in [zb.at[2], zb.at[3]] + more:
+                acc = acc + o[i].astype(f32)
+            store(i, acc)
+
+        each(4, total)
+
+    def fin(k, store):
+        g, yb, zb = grads[k]
+        at = yb.at[z]
+        got(at, r.gyr.at[k, z])
+        arrived(zb, k)
+        summed(at, zb, [g.at[2 * z + y]], store)
+
+    def cross_c():
+        arrived(r.ZC.at[0], 2)
+        other = r.GC.at[2 * z + 1 - y]
+
+        def store(i, acc):
+            other[i] = acc.astype(bf16)
+
+        summed(other, r.ZC.at[0], [], store)
+        remote(other, r.YC, r.gys.at[2], r.gyr.at[2, 0], ypeer).start()
+
+    def fin_c(store):
+        got(r.YC, r.gyr.at[2, 0])
+        arrived(r.ZC.at[1], 4)
+        summed(r.GC.at[2 * z + y], r.ZC.at[1], [r.YC], store)
+
+    def reduced_sent():
+        for k, (g, yb, zb) in enumerate(grads):
+            got(g.at[0 : 1 if k == 2 else G], r.gys.at[k])
+            for sem in (2, 4) if k == 2 else (k,):
+                got(g.at[0:3], r.gzs.at[sem])
+
+    fb = Fw // 4
+
+    def grad_down(i):
+        j = turn(i)
+        c = pl.ds(pl.multiple_of(j * fb, fb), fb)
+        rows = r.ACT[:, :, c].reshape(S * L, fb)
+        g = dot_tn(rows, r.COT[...].reshape(S * L, M)).astype(bf16)
+        r.GD[pl.ds(j * bq, bq)] = g.reshape(bq, 4, rd // 4, M)
+        to_y(0, j)
+
+
+    def back_feed(s):
+        cot = r.COT[s].reshape(L, M)
+        for j in range(4):
+            c = slice(j * fb, (j + 1) * fb)
+            wd = r.WD[bq * j : bq * (j + 1)].reshape(fb, M)
+            d_act = dot_nt(cot, wd).astype(bf16).astype(f32)
+            d_pre = d_act * r.GP[s, :, c].astype(f32)
+            total = jnp.sum(d_pre, axis=0, keepdims=True)
+            for i in range(fb // 128):
+                at = j * (fb // 128) + i
+                r.SMG[at : at + 1] += total[:, 128 * i : 128 * (i + 1)]
+            r.GP[s, :, c] = d_pre.astype(bf16)
+        m1 = jnp.zeros((L, 1), f32)
+        m2 = jnp.zeros((L, 1), f32)
+        for q in range(4):
+            c = slice(q * Cw, (q + 1) * Cw)
+            dn = dot_nt(r.GP[s], r.WU[bq * q : bq * (q + 1)].reshape(Cw, Fw))
+            g = dn * r.VV[0:1, c]
+            m1 = m1 + jnp.sum(g, axis=1, keepdims=True)
+            m2 = m2 + jnp.sum(g * xhat_of(s, q), axis=1, keepdims=True)
+            r.DNP[q, s] = dn.astype(bf16)
+        lane = lax.broadcasted_iota(jnp.int32, (L, 128), 1)
+        both = jnp.where(lane == 0, m1, jnp.where(lane == 1, m2, 0.0)) * (1.0 / M)
+        pick = (
+            lax.broadcasted_iota(jnp.int32, (8, 128), 0) == lax.broadcasted_iota(jnp.int32, (8, 128), 1)
+        ).astype(f32)
+        r.ST[t, s] = lax.dot_general(
+            pick, both, (((1,), (1,)), ((), ())), precision=lax.Precision.HIGHEST, preferred_element_type=f32
+        )
+        fold_send(2, s, r.DNP, r.DNR)
+        ex_send(3, r.er.at[3, s, 0], lambda q: r.ST.at[t, s], lambda d: r.ST.at[t, s])
+        fold_late(2, s, r.DNP, r.DNR)
+
+
+    def grad_up(i):
+        j = turn(i)
+        c = pl.ds(pl.multiple_of(j * Cw, Cw), Cw)
+        rows = r.NRM[:, :, :, c].reshape(S * L, Cw)
+        g = dot_tn(rows, r.GP[...].reshape(S * L, Fw)).astype(bf16)
+        r.GU[pl.ds(j * bq, bq)] = g.reshape(bq, 4, rw, Fw)
+        to_y(1, j)
+
+
+    def back_norm(s):
+        dn = folded(2, s, r.DNP, r.DNR)
+        got(r.ST.at[0:3, s], r.er.at[3, s, 0])
+        st = r.ST[0, s] + r.ST[1, s] + r.ST[2, s] + r.ST[3, s]
+        side = lax.broadcasted_iota(jnp.int32, (8, 128), 0)
+        col_of = lambda i: lax.dot_general(
+            st,
+            (side == i).astype(f32),
+            (((0,), (0,)), ((), ())),
+            precision=lax.Precision.HIGHEST,
+            preferred_element_type=f32,
+        )[:, :1]
+        m1, m2 = col_of(0), col_of(1)
+        inv = r.MU[s, :, 1:2]
+        xhat = (r.RES[t, s].astype(f32) - r.MU[s, :, :1]) * inv
+        cot = r.COT[s, :, :, tc].reshape(L, Cw).astype(f32)
+        for i, v in enumerate((cot, dn * xhat, dn)):
+            total = jnp.sum(v, axis=0, keepdims=True)
+            for k in range(Cw // 128):
+                at = Fw // 128 + i * (Cw // 128) + k
+                r.SMG[at : at + 1] += total[:, 128 * k : 128 * (k + 1)]
+        d_resid = cot + (dn * r.VV[0:1, tc] - m1 - xhat * m2) * inv
+        r.DR[s] = d_resid
+        db = d_resid.astype(bf16)
+        r.DB[s] = db
+        for q in range(4):
+            r.DMP[q, s] = dot_nt(db, wo(q)).astype(bf16)
+        fold_send(4, s, r.DMP, r.DMR)
+        fold_late(4, s, r.DMP, r.DMR)
+
+    def grad_out():
+        for q in range(4):
+            g = dot_tn(r.MIX[q].reshape(S * L, Cw), r.DB[...].reshape(S * L, Cw))
+            r.GA[bq * q : bq * (q + 1), :, :, 3 * Cw :] = g.astype(bf16).reshape(bq, 4, rw, Cw)
+
+    def out_rows(s):
+        for q in range(4):
+            c = slice(q * Cw, (q + 1) * Cw)
+            o = jnp.dot(r.ACT[s], r.WD[:, :, c].reshape(Fw, Cw), preferred_element_type=f32)
+            mine = (t == q).astype(f32)
+            o = o + mine * (r.RT[s] + r.VV[2:3, c])
+            r.OP[s, :, :, c] = o.astype(bf16).reshape(4 * nu, 16, Cw)
+        ex_send(5, r.eo.at[0], lambda q: r.OP.at[s, pl.ds(nu * q, nu)], lambda d: r.OR.at[d - 1, s])
+
+
+    def windows(k):
+        return r.CTX[:, 4 * nu + 4 * k : 4 * nu + 4 * (k + 1)].reshape(S * nw, M)
+
+    def compress():
+        conv = r.VV[3:4, tc]
+        pooled = 0.0
+        for k in range(3):
+            wk = r.WC[:, :, :, k * Cw : (k + 1) * Cw].reshape(M, Cw)
+            conv = conv + jnp.dot(windows(k), wk, preferred_element_type=f32)
+            pooled = pooled + r.CTX[:, 4 * nu + 4 * k : 4 * nu + 4 * (k + 1), :, tc].reshape(S * nw, Cw).astype(f32)
+        mask = r.MK[...].reshape(S * nw, 128)[:, :1]
+        done = 3 * lax.broadcasted_iota(jnp.int32, (nw, 128), 0) + 3
+        live = jnp.concatenate(
+            [(done <= r.evicted[s]).astype(f32)[:, :1] for s in range(S)], axis=0
+        ) * mask
+        r.NEW[t] = (mask * conv).astype(bf16)
+        d_conv = live * (conv - pooled * (1.0 / 3.0))
+        total = jnp.sum(d_conv, axis=0, keepdims=True)
+        for k in range(Cw // 128):
+            at = Fw // 128 + 3 * (Cw // 128) + k
+            r.SMG[at : at + 1] = total[:, 128 * k : 128 * (k + 1)]
+        r.DC[...] = d_conv.astype(bf16)
+        for k in range(3):
+            g = dot_tn(windows(k), r.DC[...])
+            r.GC[:, :, :, k * Cw : (k + 1) * Cw] = g.astype(bf16).reshape(nb, 4, rw, Cw)
+
+    slope_row = Fw // 128 + 4 * (Cw // 128)
+
+    def back_attend(s):
+        dm = folded(4, s, r.DMP, r.DMR).astype(bf16)
+        lane = lax.broadcasted_iota(jnp.int32, (1, 128), 1)
+        for h in range(ht):
+            c = slice(h * hd, (h + 1) * hd)
+            cv = slice(Cw + h * hd, Cw + (h + 1) * hd)
+            p = r.PR[s, h]
+            dp = dot_nt(dm[:, c], r.KV[s, :, cv])
+            delta = jnp.sum(p * dp, axis=1, keepdims=True)
+            ds = p * (dp - delta)
+            part = jnp.sum(jnp.sum(ds * r.DIST[...], axis=0, keepdims=True), axis=1, keepdims=True)
+            r.SMG[slope_row : slope_row + 1] -= jnp.where(lane == t * ht + h, part, 0.0)
+            dr = (ds * scale).astype(bf16)
+            dq = jnp.dot(dr, r.KV[s, :, c], preferred_element_type=f32).astype(bf16)
+            dk = dot_tn(dr, r.Q[s, :, c]).astype(bf16)
+            dv = dot_tn(p.astype(bf16), dm[:, c]).astype(bf16)
+            r.Q[s, :, c] = dq
+            r.KV[s, :, c] = dk
+            r.KV[s, :, cv] = dv
+
+
+    def grad_proj(i):
+        j = turn(i)
+        c = pl.ds(pl.multiple_of(j * Cw, Cw), Cw)
+        gq = jnp.zeros((Cw, Cw), f32)
+        gkv = jnp.zeros((Cw, 2 * Cw), f32)
+        for s in range(S):
+            gq = gq + dot_tn(r.CTX[s, 8 * nu : 12 * nu, :, c].reshape(L, Cw), r.Q[s])
+            gkv = gkv + dot_tn(r.CTX[s, :, :, c].reshape(C3, Cw), r.KV[s])
+        rows = pl.ds(j * bq, bq)
+        r.GA[rows, :, :, :Cw] = gq.astype(bf16).reshape(bq, 4, rw, Cw)
+        r.GA[rows, :, :, Cw : 3 * Cw] = gkv.astype(bf16).reshape(bq, 4, rw, 2 * Cw)
+        to_y(3, j)
+
+    def own_out(s):
+        acc = r.OP[s, pl.ds(nu * t, nu)].astype(f32)
+        for d in range(3):
+            acc = acc + r.OR[d, s].astype(f32)
+        r.OR[0, s] = acc.astype(bf16)
+
+
+    def input_rows(s):
+        x = jnp.concatenate([r.Q[s], r.KV[s, 2 * L :]], axis=1)
+        for q in range(4):
+            c = slice(q * Cw, (q + 1) * Cw)
+            w = r.WA[bq * q : bq * (q + 1), :, :, : 3 * Cw].reshape(Cw, 3 * Cw)
+            o = dot_nt(x, w) + (t == q).astype(f32) * r.DR[s]
+            r.NRM[s, :, :, c] = o.astype(bf16).reshape(4 * nu, 16, Cw)
+        ex_send(6, r.eo.at[1], lambda q: r.NRM.at[s, pl.ds(nu * q, nu)], lambda d: r.IR.at[d - 1, s])
+
+
+    def keep(o):
+        def store(i, acc):
+            o[pl.ds(i * (rd // 4), rd // 4)] = acc
+
+        return store
+
+    def hold(m):
+        def store(i, acc):
+            m[i] = acc.astype(bf16)
+
+        return store
+
+    def tier_back(k, m, tb):
+        for d in (1, 2, 3):
+            remote(m.at[t ^ d], tb.at[t], r.gts.at[k], r.gtr.at[k], (b, t ^ d)).start()
+        left_all(tb.at[0:3], r.gts.at[k])
+
+    def small_y():
+        remote(r.SMG, r.YS, r.ss.at[0], r.sr.at[0], ypeer).start()
+        left_all(r.SMG, r.ss.at[0])
+
+    def small_z():
+        got(r.YS, r.sr.at[0])
+        r.ZS[z] = r.SMG[...] + r.YS[...]
+        for d in range(1, G):
+            remote(r.ZS.at[z], r.ZS.at[z], r.ss.at[1], r.sr.at[1], (2 * zs[d] + y, t)).start()
+        left_all(r.ZS.at[0 : G - 1], r.ss.at[1])
+
+    def small_tier():
+        got(r.ZS.at[0 : G - 1], r.sr.at[1])
+        acc = r.ZS[0]
+        for zz in range(1, G):
+            acc = acc + r.ZS[zz]
+        r.os[t] = acc
+        for d in (1, 2, 3):
+            remote(r.os.at[t], r.os.at[t], r.gts.at[3], r.gtr.at[3], (b, t ^ d)).start()
+        left_all(r.os.at[0:3], r.gts.at[3])
+
+    def own_input(s):
+        acc = r.NRM[s, pl.ds(nu * t, nu)].astype(f32)
+        for d in range(3):
+            acc = acc + r.IR[d, s].astype(f32)
+        r.IG[s] = acc
+
+    mineU, mineC, mineA = (g.at[2 * z + y] for g in (r.GU, r.GC, r.GA))
+    def give(i, src, dst):
+        pltpu.make_async_copy(src, dst, r.osem.at[i]).start()
+
+    def rows_out(i, src, dst):
+        for j in range(nu):
+            give(i, src.at[:, j], dst.at[:, 16 * j : 16 * j + 16])
+
+    backs = ((mineU, r.TU, r.OU, r.ou), (mineC, r.TC, r.OC, r.oc), (mineA, r.TA, r.OA, r.oa))
+
+    def lay(k, o, q, rows):
+        if k == 0:
+            for i in range(nb):
+                o[:, wide((4 * i + q) * rd, rd)] = rows[:, i * rd : (i + 1) * rd].astype(f32)
+        else:
+            for i in range(o.shape[0]):
+                o[i, :, wide(q * Cw, Cw)] = rows[:, i * Cw : (i + 1) * Cw].astype(f32)
+
+    def tier_out(k):
+        m, tb, o, far = backs[k]
+        lay(k, o, t, m[t])
+        got(tb.at[0:3], r.gtr.at[k])
+        for d in (1, 2, 3):
+            lay(k, o, t ^ d, tb[t ^ d])
+        give(k, o, far)
+
+    def given():
+        for i, (src, dst) in enumerate(((r.OU, r.ou), (r.OC, r.oc), (r.OA, r.oa), (r.OD, r.od), (r.NEW, r.new))):
+            pltpu.make_async_copy(src, dst, r.osem.at[i]).wait()
+        for i, (src, dst) in ((5, (r.OR.at[0], r.out)), (6, (r.IG, r.ig))):
+            for j in range(nu):
+                pltpu.make_async_copy(src.at[:, j], dst.at[:, 16 * j : 16 * j + 16], r.osem.at[i]).wait()
+
+    def small_out():
+        got(r.os.at[0:3], r.gtr.at[3])
+
+    def new_send():
+        for d in (1, 2, 3):
+            remote(r.NEW.at[t], r.NEW.at[t], r.ts.at[4], r.tr.at[4], (b, t ^ d)).start()
+        left_all(r.NEW.at[0:3], r.ts.at[4])
+
+    def new_out():
+        got(r.NEW.at[0:3], r.tr.at[4])
+        give(4, r.NEW, r.new)
+
+    def drain():
+        for n in parts:
+            all_sent(n)
+        for ref, sem in sends:
+            got(ref, sem)
+        act_sent()
+        reduced_sent()
+        for e, ref in enumerate((r.MIX, r.RES, r.DNP, r.ST, r.DMP, r.OR, r.IR)):
+            got(ref.at[0:3], r.es.at[e])
+        given()
+
+    def out_come():
+        got(r.OR, r.eo.at[0])
+
+    def in_come():
+        got(r.IR, r.eo.at[1])
+
+    greet(G, True, True)
+    here(r.wd, r.WD.at[b], 0)
+    tier_start("A")
+    tier_start("C")
+    small_start()
+    tier_start("U")
+    act_start(0, 1)
+    memory_rows()
+    act_start(2, 3, 4, 5, 6)
+    got(r.WD.at[b], r.lsem.at[0])
+    own_z("D")
+    own_y("D")
+    tier_wait("A")
+    own_z("A")
+    own_y("A")
+    tier_wait("C")
+    own_y("C")
+    tier_wait("S")
+    own_z("S")
+    own_y("S")
+    table()
+    onward("A", 1)
+    onward("S", 1)
+    onward("A", 2)
+    onward("S", 2)
+    tier_wait("U")
+    own_z("U")
+    onward("A", 3)
+    own_y("U")
+    onward("S", 3)
+    y_wait("C")
+    onward("U", 1)
+    act_forward(0, 1, 2, 3, 4)
+    act_wait(0)
+    y_wait("A")
+    each(S, project, {0: lambda: onward("U", 2), 1: lambda: onward("D", 1)})
+    own_z("C")
+    own_z("X")
+    each(S, attend, {1: lambda: onward("U", 3)})
+    spread_pass(0, 0, r.MIX)
+    each(S, residual)
+    onward("D", 2)
+    y_wait("S")
+    vectors()
+    onward("C", 1)
+    act_forward(5, 6)
+    y_wait("U")
+    spread_pass(1, 0, r.RES)
+    each(S, feed, {1: lambda: onward("X", 1), 3: lambda: onward("D", 3)})
+    act_wait(1)
+    act_wait(2)
+    each(4, grad_down, {1: lambda: onward("C", 2)})
+    onward("X", 2)
+    y_wait("D")
+    each(S, back_feed, {0: lambda: onward("C", 3), 1: lambda: mid(0, 0), 2: lambda: onward("X", 3)})
+    fold_pass(2, S - 1, r.DNP, r.DNR)
+    compress()
+    mid_c(0)
+    mid(0, 1)
+    each(4, grad_up)
+    each(S, back_norm)
+    fold_pass(4, S - 1, r.DMP, r.DMR)
+    mid_c(1)
+    mid(0, 2)
+    grad_out()
+    each(S, back_attend, {1: lambda: mid_c(2)})
+    small_y()
+    mid(1, 0)
+    each(4, grad_proj)
+    each(S, out_rows)
+    mid(1, 1)
+    each(S, input_rows)
+    new_send()
+    mid(1, 2)
+    mid(3, 0)
+    cross_c()
+    fin(0, keep(r.OD))
+    give(3, r.OD, r.od)
+    small_z()
+    mid(3, 1)
+    fin(1, hold(mineU))
+    tier_back(0, mineU, r.TU)
+    mid(3, 2)
+    small_tier()
+    fin_c(hold(mineC))
+    tier_back(1, mineC, r.TC)
+    out_come()
+    each(S, own_out)
+    rows_out(5, r.OR.at[0], r.out)
+    in_come()
+    each(S, own_input)
+    rows_out(6, r.IG, r.ig)
+    new_out()
+    tier_out(0)
+    tier_out(1)
+    small_out()
+    fin(3, hold(mineA))
+    tier_back(2, mineA, r.TA)
+    tier_out(2)
+    drain()
+
+def whole_layer(nb, ht, hd, arrays):
+    S, R, M = arrays["seg"].shape
+    rw, rd, rs = arrays["w_query"].shape[0], arrays["wd"].shape[0], M // (4 * nb)
+    nu = R // 16
+    G, Cw, Fw, L = nb // 2, M // 4, nb * rd, 64 * nu
+    dma = pltpu.SemaphoreType.DMA
+    V = lambda shape, dtype=bf16: pltpu.VMEM(shape, dtype)
+    D4, A4, U4, C4 = (4, rd // 4, M), (4, rw, 4 * Cw), (4, rw, Fw), (4, rw, 3 * Cw)
+    ins = arrays
+    outs = dict(
+        out=((S, R, M), bf16),
+        ig=((S, R, M), f32),
+        new=((4, S * L // 3, Cw), bf16),
+        od=((rd, M), f32),
+        ou=((rw, 4 * Fw), f32),
+        oc=((3, rw, M), f32),
+        oa=((4, rw, M), f32),
+        os=((4, 24, 128), f32),
+    )
+    scratch = dict(
+        WA=V((nb,) + A4),
+        WU=V((nb,) + U4),
+        WC=V((nb,) + C4),
+        WD=V((nb, rd, M)),
+        SM=V((nb, 4, 16, 128), f32),
+        CTX=V((S, 12 * nu, 16, M)),
+        COT=V((S, 4 * nu, 16, M)),
+        MK=V((S, 4, L // 12, 128), f32),
+        DIST=V((L, 3 * L), f32),
+        VV=V((8, max(M, Fw)), f32),
+        SMG=V((24, 128), f32),
+        Q=V((S, L, Cw)),
+        KV=V((S, 3 * L, 2 * Cw)),
+        PR=V((S, ht, L, 3 * L), f32),
+        MIX=V((4, S, L, Cw)),
+        RT=V((S, L, Cw), f32),
+        RES=V((4, S, L, Cw)),
+        MU=V((S, L, 128), f32),
+        NRM=V((S, 4 * nu, 16, M)),
+        ACT=V((S, L, Fw)),
+        GP=V((S, L, Fw)),
+        DNP=V((4, S, L, Cw)),
+        DNR=V((3, S, L, Cw)),
+        ST=V((4, S, 8, L), f32),
+        DR=V((S, L, Cw), f32),
+        DB=V((S, L, Cw)),
+        DMP=V((4, S, L, Cw)),
+        DMR=V((3, S, L, Cw)),
+        OP=V((S, 4 * nu, 16, M)),
+        OR=V((3, S, nu, 16, M)),
+        IR=V((3, S, nu, 16, M)),
+        DC=V((S * L // 3, Cw)),
+        GD=V((nb,) + D4),
+        GU=V((nb,) + U4),
+        GC=V((nb,) + C4),
+        GA=V((nb,) + A4),
+        YD=V((G,) + D4),
+        YU=V((G,) + U4),
+        YC=V(C4),
+        YA=V((G,) + A4),
+        ZD=V((4,) + D4),
+        ZU=V((4,) + U4),
+        ZC=V((2, 4) + C4),
+        ZA=V((4,) + A4),
+        YS=V((24, 128), f32),
+        ZS=V((G, 24, 128), f32),
+        TU=V(U4),
+        TC=V(C4),
+        TA=V(A4),
+        NEW=V((4, S * L // 3, Cw)),
+        IG=V((S, nu, 16, M), f32),
+        OD=V((rd, M), f32),
+        OU=V((rw, 4 * Fw), f32),
+        OC=V((3, rw, M), f32),
+        OA=V((4, rw, M), f32),
+        osem=dma((7,)),
+        lsem=dma((6,)),
+        ts=dma((5,)),
+        tr=dma((5,)),
+        zs=dma((6,)),
+        zr=dma((2, 9, G - 1)),
+        ys=dma((6,)),
+        yr=dma((6,)),
+        acs=dma((3,)),
+        acc=dma((3,)),
+        acf=dma((3,)),
+        acx=dma((7,)),
+        es=dma((7,)),
+        er=dma((5, S, 2)),
+        eo=dma((2,)),
+        gys=dma((4,)),
+        gyr=dma((4, G)),
+        gzs=dma((5,)),
+        gzr=dma((5, 3)),
+        ss=dma((2,)),
+        sr=dma((2,)),
+        gts=dma((4,)),
+        gtr=dma((4,)),
+    )
+    names = list(ins) + list(outs) + list(scratch)
+    near = dict(gain=VM, bias=VM, bdown=VM, bconv=VM, bup=VM, mem=VM, mask=VM, evicted=SM, slopes=SM)
+    return pl.pallas_call(
+        functools.partial(layer_kernel, names, (nb, nu, S, ht, hd, M, Cw, rw, rd, rs)),
+        out_shape=[jax.ShapeDtypeStruct(s, d) for s, d in outs.values()],
+        in_specs=[near.get(n, ANY) for n in ins],
+        out_specs=[VM if n == "os" else ANY for n in outs],
+        scratch_shapes=list(scratch.values()),
+        compiler_params=pltpu.CompilerParams(
+            collective_id=9, has_side_effects=True, vmem_limit_bytes=63 * 2**20
+        ),
+        name="whole_layer",
+    )(*ins.values())
+
+
+def finish_kernel(names, shape, *refs):
+    r = Names(names, refs)
+    r.bufs = refs[len(names) :]
+    nb, rs, rd, Fw, Cw, heads = shape
+    S, R, M = r.seg.shape
+    b, t = lax.axis_index("batch"), lax.axis_index("tier")
+    moves = [(r.out, r.o_out), (r.ig, r.o_ig), (r.od, r.o_od), (r.ou, r.o_ou), (r.oc, r.o_oc)]
+    moves += [(r.oa.at[i], o) for i, o in enumerate((r.o_q, r.o_k, r.o_v, r.o_o))]
+    into, onto = [], []
+    for i, (src, dst) in enumerate(moves):
+        n = src.shape[0]
+        cut = 4 if n % 4 == 0 else 1
+        for j in range(cut):
+            rows = pl.ds(j * (n // cut), n // cut)
+            buf = r.bufs[i].at[rows]
+            into.append(pltpu.make_async_copy(src.at[rows], buf, r.sem.at[len(into)]))
+            onto.append(pltpu.make_async_copy(buf, dst.at[rows], r.sem.at[64 + len(onto)]))
+    for cp in into:
+        cp.start()
+    nw = 4 * R // 3
+    slots = 4 * R - nw
+    place = lax.broadcasted_iota(jnp.int32, (R, 1), 0) + R * t
+    for s in range(S):
+        r.o_mem[s] = jnp.where(place < r.evicted[s], r.seg[s], r.mem[s])
+        r.o_comp[s] = r.comp[s]
+    for tier in range(4):
+        first = max(slots - R * tier, 0)
+        if first < R:
+
+            @pl.when(t == tier)
+            def _(tier=tier, first=first):
+                w = R * tier + first - slots
+                side = lax.broadcasted_iota(jnp.int32, (R - first, 1), 0)
+                for s in range(S):
+                    written = 3 * (side + w) + 3 <= r.evicted[s]
+                    for q in range(4):
+                        c = slice(q * Cw, (q + 1) * Cw)
+                        rows = r.new[q, s * nw + w : s * nw + w + R - first]
+                        r.o_comp[s, first:, c] = jnp.where(written, rows, r.comp[s, first:, c])
+    spot = 4 * b + t
+    block, inner = spot // (Cw // rs), lax.rem(spot, Cw // rs)
+    half, group = inner // (128 // rs), lax.rem(inner, 128 // rs)
+    for i, o in enumerate((r.o_down, r.o_gain, r.o_bias, r.o_conv)):
+        row = r.os[block, pl.ds(Fw // 128 + (Cw // 128) * i + half, 1), :]
+        turned = pltpu.roll(jnp.broadcast_to(row, (8, 128)), lax.rem(128 - rs * group, 128), 1)
+        o[...] = turned[0:1, :rs]
+    r.o_up[...] = r.os[t, pl.ds(b, 1), :rd]
+    at = Fw // 128 + 4 * (Cw // 128)
+    total = r.os[0, at : at + 1]
+    for q in range(1, 4):
+        total = total + r.os[q, at : at + 1]
+    r.o_slopes[...] = total[:, :heads]
+    for cp, then in zip(into, onto):
+        cp.wait()
+        then.start()
+    for cp in onto:
+        cp.wait()
+
+
+def finish(nb, heads, arrays):
+    S, R, M = arrays["seg"].shape
+    rw, rd, rs = arrays["oa"].shape[1], arrays["od"].shape[0], M // (4 * nb)
+    Cw, Fw = M // 4, nb * rd
+    rows, mat, vec = (S, R, M), (rw, M), (1, rs)
+    outs = dict(
+        o_out=(rows, bf16, ANY),
+        o_ig=(rows, f32, ANY),
+        o_mem=(rows, bf16, VM),
+        o_comp=(rows, bf16, VM),
+        o_q=(mat, f32, ANY),
+        o_k=(mat, f32, ANY),
+        o_v=(mat, f32, ANY),
+        o_o=(mat, f32, ANY),
+        o_ou=((rw, 4 * Fw), f32, ANY),
+        o_up=((1, rd), f32, VM),
+        o_od=((rd, M), f32, ANY),
+        o_down=(vec, f32, VM),
+        o_gain=(vec, f32, VM),
+        o_bias=(vec, f32, VM),
+        o_oc=((3, rw, M), f32, ANY),
+        o_conv=(vec, f32, VM),
+        o_slopes=((1, heads), f32, VM),
+    )
+    moved = ("o_out", "o_ig", "o_od", "o_ou", "o_oc", "o_q", "o_k", "o_v", "o_o")
+    near = dict(seg=VM, mem=VM, comp=VM, new=VM, os=VM, evicted=SM)
+    return pl.pallas_call(
+        functools.partial(
+            finish_kernel, list(arrays) + list(outs) + ["sem"], (nb, rs, rd, Fw, Cw, heads)
+        ),
+        out_shape=[jax.ShapeDtypeStruct(s, d) for s, d, _ in outs.values()],
+        in_specs=[near.get(n, ANY) for n in arrays],
+        out_specs=[o[2] for o in outs.values()],
+        scratch_shapes=[pltpu.SemaphoreType.DMA((128,))]
+        + [pltpu.VMEM(outs[n][0], outs[n][1]) for n in moved],
+        compiler_params=pltpu.CompilerParams(vmem_limit_bytes=63 * 2**20),
+        name="finish",
+    )(*arrays.values())
+
+
+def per_device_fused(
+    nb,
+    segment,
+    memory,
+    compressed,
+    evicted,
+    window_mask,
+    cotangent,
+    w_query,
+    w_key,
+    w_value,
+    w_output,
+    w_up,
+    b_up,
+    w_down,
+    b_down,
+    ln_gain,
+    ln_bias,
+    w_conv,
+    b_conv,
+    slopes,
+):
+    S, R, M = segment.shape
+    heads = slopes.shape[0]
+    line = lambda v: v.reshape(1, -1)
+    names = ("out", "ig", "new", "od", "ou", "oc", "oa", "os")
+    made = whole_layer(
+        nb,
+        heads // 4,
+        M // heads,
+        dict(
+            w_query=w_query,
+            w_key=w_key,
+            w_value=w_value,
+            w_output=w_output,
+            w_up=w_up,
+            w_conv=w_conv,
+            wd=w_down,
+            comp=compressed,
+            seg=segment,
+            cot=cotangent,
+            mem=memory,
+            gain=line(ln_gain),
+            bias=line(ln_bias),
+            bdown=line(b_down),
+            bconv=line(b_conv),
+            bup=line(b_up),
+            mask=window_mask,
+            evicted=evicted,
+            slopes=slopes,
+        ),
+    )
+    arrays = dict(zip(names, made), seg=segment, mem=memory, comp=compressed, evicted=evicted)
+    outs = finish(nb, heads, arrays)
+    flat = (9, 11, 12, 13, 15, 16)
+    return tuple(o.reshape(-1) if i in flat else o for i, o in enumerate(outs))
+
+
 def solution(mesh):
     both = ("batch", "tier")
     rows = P("batch", "tier", None)
     mat, vec = P(both, None), P(both)
+    nb = mesh.shape["batch"]
+
+    def body(*args):
+        fused = args[6].shape[0] % 16 == 0 and args[12].shape[0] == 128
+        return (per_device_fused if fused else per_device)(nb, *args)
+
     return jax.shard_map(
-        functools.partial(per_device, mesh.shape["batch"]),
+        body,
         mesh=mesh,
         in_specs=(
             (rows, rows, rows, P("batch"), P("batch", "tier"), rows)

time: 609 us -> 192 us (0.32); the launches traced: 601 us -> 192 us
  Pallas kernels: 347 us -> 191 us
  matrix products: 102 us -> 0 us
  local copies, waits for them, and re-layouts: 96.6 us -> 0 us
  other arithmetic: 47.8 us -> 0 us
    pallas_call x9 -> x2, Pallas kernels: 347 us -> 191 us  [the longest x1 185 us: whole_layer(): pl.pallas_call(functools.partial(layer_kernel, names, (nb, nu, S, ht, hd,...]
    dot_general x26 -> x0, matrix products: 96.7 us -> none  [the longest x9 22.7 us: dot_tn(): lax.dot_general(a, b, (((0,), (0,)), ((), ())), preferred_element_type=f32)]
    reshape x24 -> x0, local copies, waits for them, and re-layouts: 23.9 us -> none  [the longest x1 5.16 us: per_device(): dot(ctx.reshape(-1, M), Wqkv[:, Cw:]).astype(bf16)]
    convert_element_type x9 -> x0, local copies, waits for them, and re-layouts: 21.1 us -> none  [the longest x2 7.32 us: per_device(): resid = RES.transpose(1, 0, 2).reshape(T, M).astype(f32)]
    reduce_sum x8 -> x0, other arithmetic: 15.3 us -> none  [the longest x2 5.39 us: per_device(): ggain, gbias = (jnp.sum(dn * xhat_t, axis=0), jnp.sum(dn, axis=0))]
    sub x1 -> x0, other arithmetic: 14.5 us -> none  [per_device(): d_scores = probs * (d_probs - delta)]
    unnamed x122 -> x0, local copies, waits for them, and re-layouts: 14.1 us -> none
    another operation x14 -> x0, local copies, waits for them, and re-layouts: 12.4 us -> none  [the longest x1 4.13 us: per_device(): dk.reshape(-1, Cw)]
where the time goes in v3:
time: 192 us
  Pallas kernels  191 us (99%)
    pallas_call x1, Pallas kernels, whole_layer(): pl.pallas_call(functools.partial(layer_kernel, names, (nb, nu, S, ht, hd,...  185 us
    pallas_call x1, Pallas kernels, finish(): pl.pallas_call(functools.partial(finish_kernel, list(arrays) + list(outs)...  6.17 us

profile of v3, /device:TPU:11, one launch (start us, length us, event | category | flops | bytes accessed | tf_op | source)
XLA Modules:
  0.0 191.6 jit_solution(5316899321991929705)
XLA Ops:
  0.7 184.7 %whole_layer.1 = (bf16[4,48,1024]{2,1,0:T(8,128)(2,1)}, f32[4,48,1024]{2,1,0:T(8,128)}, bf16[4,256,256]{2,1,0:T(8,128)(2,1)}, f32[128,1024]{1,0:T(8,128)}, f32[3...) custom-call(bf16[32,1024]{1,0:T(8,128)(2,1)} %refs_0_.1, ...), custom_call_target="tpu_custom_call" | custom-call | tf_op jit(solution)/shard_map/whole_layer/pallas_call | solution.py:1445
  185.4 6.2 %finish.1 = (bf16[4,48,1024]{2,1,0:T(8,128)(2,1)}, f32[4,48,1024]{2,1,0:T(8,128)}, bf16[4,48,1024]{2,1,0:T(8,128)(2,1)}, bf16[4,48,1024]{2,1,0:T(8,128)(2,1)}, f...) custom-call(bf16[4,48,1024]{2,1,0:T(8,128)(2,1)} %get-tuple-element., ...), custom_call_target="tpu_custom_call" | custom-call | tf_op jit(solution)/shard_map/finish/pallas_call | solution.py:1543

commit v4 on v3

--- a/solution.py
+++ b/solution.py
@@ -540,6 +540,7 @@
     r = Names(names, refs)
     nb, nu, S, ht, hd, M, Cw, rw, rd, rs = shape
     R = 16 * nu
+    ct = r.OC.shape[0] - r.GB.shape[-1] // Cw
     G, bq = nb // 2, nb // 4
     L = 16 * 4 * nu
     C3 = 3 * L
@@ -588,24 +589,34 @@
 
         got(arr.at[0:2, s], r.er.at[e, s, 0])
 
-    def fold_send(e, s, out, into):
+    folds = {
+        2: (lambda q, s: r.DNP.at[q, s], r.DNR),
+        4: (lambda q, s: r.DMP.at[q, s], r.DMR),
+        5: (lambda q, s: r.OP.at[s, pl.ds(nu * q, nu)], r.OR),
+        6: (lambda q, s: r.NRM.at[s, pl.ds(nu * q, nu)], r.IR),
+    }
+
+    def fold_send(e, s):
+        out, into = folds[e]
         for i, d in enumerate((1, 3)):
-            remote(out.at[t ^ d, s], into.at[i, s], r.es.at[e], r.er.at[e, s, i], (b, t ^ 1)).start()
-
-    def fold_pass(e, s, out, into):
-        at = into.at[1, s]
+            remote(out(t ^ d, s), into.at[i, s], r.es.at[e], r.er.at[e, s, i], (b, t ^ 1)).start()
+
+    def fold_pass(e, s):
+        out, into = folds[e]
+        at, far = into.at[1, s], out(t ^ 2, s)
         got(at, r.er.at[e, s, 1])
-        out[t ^ 2, s] = (out[t ^ 2, s].astype(f32) + at[...].astype(f32)).astype(bf16)
-        remote(out.at[t ^ 2, s], into.at[2, s], r.es.at[e], r.er.at[e, s, 0], (b, t ^ 2)).start()
-
-    def fold_late(e, s, out, into):
+        far[...] = (far[...].astype(f32) + at[...].astype(f32)).astype(bf16)
+        remote(far, into.at[2, s], r.es.at[e], r.er.at[e, s, 0], (b, t ^ 2)).start()
+
+    def fold_late(e, s):
         @pl.when(s > 0)
         def _():
-            fold_pass(e, s - 1, out, into)
-
-    def folded(e, s, out, into):
+            fold_pass(e, s - 1)
+
+    def folded(e, s):
+        out, into = folds[e]
         got(into.at[0:2, s], r.er.at[e, s, 0])
-        return out[t, s].astype(f32) + into[0, s].astype(f32) + into[2, s].astype(f32)
+        return out(t, s)[...].astype(f32) + into[0, s].astype(f32) + into[2, s].astype(f32)
 
     def here(src, dst, i):
         cp = pltpu.make_async_copy(src, dst, r.lsem.at[i])
@@ -628,11 +639,12 @@
             ]
         return [(r.w_conv.at[i, :, wide(Cw * q, Cw)], r.WC.at[b, t, :, i * Cw : (i + 1) * Cw]) for i in range(3)]
 
+    def tier_own(n):
+        for src, dst in cuts(n, t):
+            here(src, dst, index[n])
+
     def tier_start(n):
         i = index[n]
-        if n != "S":
-            for src, dst in cuts(n, t):
-                here(src, dst, i)
         for d in (1, 2, 3):
             for src, dst in cuts(n, t ^ d):
                 remote(src, dst, r.ts.at[i], r.tr.at[i], (b, t ^ d)).start()
@@ -730,7 +742,7 @@
         tap = (to >= W).astype(jnp.int32) + (to >= 2 * W).astype(jnp.int32)
         order = (frm == 3 * (to - W * tap) + tap).astype(bf16)
         for s in range(S):
-            rows = jnp.dot(order, r.mem[s], preferred_element_type=f32).astype(bf16)
+            rows = jnp.dot(order, r.MEMV[s], preferred_element_type=f32).astype(bf16)
             for i in range(3):
                 r.CTX[s, 4 * nu + 4 * i + t] = rows[W * i : W * (i + 1)]
             square = lambda axis: lax.broadcasted_iota(jnp.int32, (R // 3, R // 3), axis)
@@ -759,13 +771,17 @@
     group = lambda i: 0 if i < 5 else i - 4
     grouped = [(r.CTX, 3 * nu), (r.COT, nu), (r.MK, 1)]
 
+    def act_own():
+        for i, (cut, at, far) in enumerate(pieces):
+            if far:
+                for src, dst in cut:
+                    here(src, dst, 4 + group(i))
+
     def act_start(*which):
         for i in which:
             cut, at, far = pieces[i]
             g = group(i)
             for src, dst in cut:
-                if far:
-                    here(src, dst, 4 + g)
                 remote(src, dst, r.acs.at[g], r.acc.at[g], (b, t ^ 1)).start()
                 remote(src, dst, r.acs.at[g], r.acx.at[i], (b, t ^ 2)).start()
 
@@ -875,7 +891,7 @@
         inner = jnp.where(z == 1, low, G - 1 - low)
         return jnp.where(z == 0, G - 1 - j, jnp.where(z == G - 1, j, inner))
 
-    grads = [(r.GD, r.YD, r.ZD), (r.GU, r.YU, r.ZU), (r.GC, r.YC, r.ZC), (r.GA, r.YA, r.ZA)]
+    grads = [(r.GD, r.YD, r.ZD), (r.GU, r.YU, r.ZU), (r.GB, r.YB, r.ZB), (r.WU, r.YA, r.ZA)]
 
     def to_y(k, zz):
         g, yb, zb = grads[k]
@@ -914,7 +930,7 @@
         for i in steps or range(G - 1):
             o = turn(i)
             for c, col in enumerate((1 - y, y)):
-                pass_on(i, r.GC.at[2 * o + col], r.ZC.at[c], o, (2, 4)[c])
+                pass_on(i, r.GC.at[2 * o + col], r.ZC.at[c], o, 4 + c)
 
     def arrived(zb, sem):
         got(zb.at[2:4], r.gzr.at[sem, 2])
@@ -936,25 +952,27 @@
         summed(at, zb, [g.at[2 * z + y]], store)
 
     def cross_c():
-        arrived(r.ZC.at[0], 2)
+        arrived(r.ZC.at[0], 4)
         other = r.GC.at[2 * z + 1 - y]
 
         def store(i, acc):
             other[i] = acc.astype(bf16)
 
         summed(other, r.ZC.at[0], [], store)
-        remote(other, r.YC, r.gys.at[2], r.gyr.at[2, 0], ypeer).start()
+        remote(other, r.YC, r.gys.at[4], r.gyr.at[4, 0], ypeer).start()
 
     def fin_c(store):
-        got(r.YC, r.gyr.at[2, 0])
-        arrived(r.ZC.at[1], 4)
+        got(r.YC, r.gyr.at[4, 0])
+        arrived(r.ZC.at[1], 5)
         summed(r.GC.at[2 * z + y], r.ZC.at[1], [r.YC], store)
 
     def reduced_sent():
         for k, (g, yb, zb) in enumerate(grads):
-            got(g.at[0 : 1 if k == 2 else G], r.gys.at[k])
-            for sem in (2, 4) if k == 2 else (k,):
-                got(g.at[0:3], r.gzs.at[sem])
+            got(g.at[0:G], r.gys.at[k])
+            got(g.at[0:3], r.gzs.at[k])
+        got(r.YC, r.gys.at[4])
+        for sem in (4, 5):
+            got(r.GC.at[0:3], r.gzs.at[sem])
 
     fb = Fw // 4
 
@@ -996,9 +1014,9 @@
         r.ST[t, s] = lax.dot_general(
             pick, both, (((1,), (1,)), ((), ())), precision=lax.Precision.HIGHEST, preferred_element_type=f32
         )
-        fold_send(2, s, r.DNP, r.DNR)
+        fold_send(2, s)
         ex_send(3, r.er.at[3, s, 0], lambda q: r.ST.at[t, s], lambda d: r.ST.at[t, s])
-        fold_late(2, s, r.DNP, r.DNR)
+        fold_late(2, s)
 
 
     def grad_up(i):
@@ -1011,7 +1029,7 @@
 
 
     def back_norm(s):
-        dn = folded(2, s, r.DNP, r.DNR)
+        dn = folded(2, s)
         got(r.ST.at[0:3, s], r.er.at[3, s, 0])
         st = r.ST[0, s] + r.ST[1, s] + r.ST[2, s] + r.ST[3, s]
         side = lax.broadcasted_iota(jnp.int32, (8, 128), 0)
@@ -1037,8 +1055,8 @@
         r.DB[s] = db
         for q in range(4):
             r.DMP[q, s] = dot_nt(db, wo(q)).astype(bf16)
-        fold_send(4, s, r.DMP, r.DMR)
-        fold_late(4, s, r.DMP, r.DMR)
+        fold_send(4, s)
+        fold_late(4, s)
 
     def grad_out():
         for q in range(4):
@@ -1052,7 +1070,8 @@
             mine = (t == q).astype(f32)
             o = o + mine * (r.RT[s] + r.VV[2:3, c])
             r.OP[s, :, :, c] = o.astype(bf16).reshape(4 * nu, 16, Cw)
-        ex_send(5, r.eo.at[0], lambda q: r.OP.at[s, pl.ds(nu * q, nu)], lambda d: r.OR.at[d - 1, s])
+        fold_send(5, s)
+        fold_late(5, s)
 
 
     def windows(k):
@@ -1070,7 +1089,7 @@
         live = jnp.concatenate(
             [(done <= r.evicted[s]).astype(f32)[:, :1] for s in range(S)], axis=0
         ) * mask
-        r.NEW[t] = (mask * conv).astype(bf16)
+        r.NEW[t] = (mask * conv).astype(bf16).reshape(S, nw, Cw)
         d_conv = live * (conv - pooled * (1.0 / 3.0))
         total = jnp.sum(d_conv, axis=0, keepdims=True)
         for k in range(Cw // 128):
@@ -1079,12 +1098,13 @@
         r.DC[...] = d_conv.astype(bf16)
         for k in range(3):
             g = dot_tn(windows(k), r.DC[...])
-            r.GC[:, :, :, k * Cw : (k + 1) * Cw] = g.astype(bf16).reshape(nb, 4, rw, Cw)
+            far, at = (r.GC, k) if k < ct else (r.GB, k - ct)
+            far[:, :, :, at * Cw : (at + 1) * Cw] = g.astype(bf16).reshape(nb, 4, rw, Cw)
 
     slope_row = Fw // 128 + 4 * (Cw // 128)
 
     def back_attend(s):
-        dm = folded(4, s, r.DMP, r.DMR).astype(bf16)
+        dm = folded(4, s).astype(bf16)
         lane = lax.broadcasted_iota(jnp.int32, (1, 128), 1)
         for h in range(ht):
             c = slice(h * hd, (h + 1) * hd)
@@ -1115,14 +1135,18 @@
         rows = pl.ds(j * bq, bq)
         r.GA[rows, :, :, :Cw] = gq.astype(bf16).reshape(bq, 4, rw, Cw)
         r.GA[rows, :, :, Cw : 3 * Cw] = gkv.astype(bf16).reshape(bq, 4, rw, 2 * Cw)
-        to_y(3, j)
+        for d in (1, 2, 3):
+            remote(r.GA.at[rows, t ^ d], r.WU.at[rows, t], r.xs.at[0], r.xr.at[j], (b, t ^ d)).start()
+        r.WU[rows, t] = r.GA[rows, t]
+
+    def proj_y(*steps):
+        for i in steps:
+            j = turn(i)
+            got(r.WU.at[pl.ds(j * bq, bq), 0:3], r.xr.at[j])
+            to_y(3, j)
 
     def own_out(s):
-        acc = r.OP[s, pl.ds(nu * t, nu)].astype(f32)
-        for d in range(3):
-            acc = acc + r.OR[d, s].astype(f32)
-        r.OR[0, s] = acc.astype(bf16)
-
+        r.OR[1, s] = folded(5, s).astype(bf16)
 
     def input_rows(s):
         x = jnp.concatenate([r.Q[s], r.KV[s, 2 * L :]], axis=1)
@@ -1131,7 +1155,8 @@
             w = r.WA[bq * q : bq * (q + 1), :, :, : 3 * Cw].reshape(Cw, 3 * Cw)
             o = dot_nt(x, w) + (t == q).astype(f32) * r.DR[s]
             r.NRM[s, :, :, c] = o.astype(bf16).reshape(4 * nu, 16, Cw)
-        ex_send(6, r.eo.at[1], lambda q: r.NRM.at[s, pl.ds(nu * q, nu)], lambda d: r.IR.at[d - 1, s])
+        fold_send(6, s)
+        fold_late(6, s)
 
 
     def keep(o):
@@ -1139,6 +1164,10 @@
             o[pl.ds(i * (rd // 4), rd // 4)] = acc
 
         return store
+
+    def across(q, acc):
+        for i in range(4):
+            r.OA[i, :, wide(q * Cw, Cw)] = acc[:, i * Cw : (i + 1) * Cw]
 
     def hold(m):
         def store(i, acc):
@@ -1173,12 +1202,9 @@
         left_all(r.os.at[0:3], r.gts.at[3])
 
     def own_input(s):
-        acc = r.NRM[s, pl.ds(nu * t, nu)].astype(f32)
-        for d in range(3):
-            acc = acc + r.IR[d, s].astype(f32)
-        r.IG[s] = acc
-
-    mineU, mineC, mineA = (g.at[2 * z + y] for g in (r.GU, r.GC, r.GA))
+        r.IG[s] = folded(6, s)
+
+    mineU, mineC, mineA, mineB = (g.at[2 * z + y] for g in (r.GU, r.GC, r.GA, r.GB))
     def give(i, src, dst):
         pltpu.make_async_copy(src, dst, r.osem.at[i]).start()
 
@@ -1186,7 +1212,14 @@
         for j in range(nu):
             give(i, src.at[:, j], dst.at[:, 16 * j : 16 * j + 16])
 
-    backs = ((mineU, r.TU, r.OU, r.ou), (mineC, r.TC, r.OC, r.oc), (mineA, r.TA, r.OA, r.oa))
+    backs = (
+        (mineU, r.TU, r.OU, r.ou),
+        (mineC, r.TC, r.OC.at[0:ct], r.oc.at[0:ct]),
+        None,
+        None,
+        (mineB, r.TB, r.OC.at[ct:3], r.oc.at[ct:3]),
+    )
+    places_out = (0, 1, 2, None, 7)
 
     def lay(k, o, q, rows):
         if k == 0:
@@ -1202,51 +1235,82 @@
         got(tb.at[0:3], r.gtr.at[k])
         for d in (1, 2, 3):
             lay(k, o, t ^ d, tb[t ^ d])
-        give(k, o, far)
+        give(places_out[k], o, far)
 
     def given():
-        for i, (src, dst) in enumerate(((r.OU, r.ou), (r.OC, r.oc), (r.OA, r.oa), (r.OD, r.od), (r.NEW, r.new))):
+        for i, (src, dst) in ((0, (r.OU, r.ou)), (2, (r.OA, r.oa)), (3, (r.OD, r.od))):
             pltpu.make_async_copy(src, dst, r.osem.at[i]).wait()
-        for i, (src, dst) in ((5, (r.OR.at[0], r.out)), (6, (r.IG, r.ig))):
+        for i, (src, dst) in ((1, (r.OC.at[0:ct], r.oc.at[0:ct])), (7, (r.OC.at[ct:3], r.oc.at[ct:3]))):
+            pltpu.make_async_copy(src, dst, r.osem.at[i]).wait()
+        for i, (src, dst) in ((5, (r.OR.at[1], r.out)), (6, (r.IG, r.ig)), (4, (r.OR.at[0], r.om)), (8, (r.OR.at[2], r.ocm))):
             for j in range(nu):
                 pltpu.make_async_copy(src.at[:, j], dst.at[:, 16 * j : 16 * j + 16], r.osem.at[i]).wait()
 
     def small_out():
         got(r.os.at[0:3], r.gtr.at[3])
 
+    slots = L - nw
+    windows_of = [(q, max(R * q - slots, 0), R - max(slots - R * q, 0)) for q in range(4) if slots < R * (q + 1)]
+
     def new_send():
-        for d in (1, 2, 3):
-            remote(r.NEW.at[t], r.NEW.at[t], r.ts.at[4], r.tr.at[4], (b, t ^ d)).start()
-        left_all(r.NEW.at[0:3], r.ts.at[4])
+        for q, at, n in windows_of:
+            part = r.NEW.at[t, :, at : at + n]
+            if_(t != q, remote(part, part, r.ns.at[0], r.ns.at[1], (b, q)).start)
+
+    def new_sent():
+        for q, at, n in windows_of:
+            if_(t != q, lambda: got(r.NEW.at[0, :, at : at + n], r.ns.at[0]))
 
     def new_out():
-        got(r.NEW.at[0:3], r.tr.at[4])
-        give(4, r.NEW, r.new)
+        for q, at, n in windows_of:
+            if_(t == q, lambda: got(r.NEW.at[0:3, :, at : at + n], r.ns.at[1]))
+
+    def memories():
+        side = lax.broadcasted_iota(jnp.int32, (16, 1), 0)
+        for s in range(S):
+            for i in range(nu):
+                fresh = side + (R * t + 16 * i) < r.evicted[s]
+                r.OR[0, s, i] = jnp.where(fresh, r.CTX[s, 8 * nu + nu * t + i], r.MEMV[s, 16 * i : 16 * i + 16])
+                r.OR[2, s, i] = r.CTX[s, nu * t + i]
+        for q, at, n in windows_of:
+
+            @pl.when(t == q)
+            def _(at=at, n=n):
+                for i in range((R - n) // 16, nu):
+                    w = at + 16 * i - (R - n)
+                    for s in range(S):
+                        written = 3 * (side + w) + 3 <= r.evicted[s]
+                        for p in range(4):
+                            c = slice(p * Cw, (p + 1) * Cw)
+                            old = r.CTX[s, nu * t + i, :, c]
+                            r.OR[2, s, i, :, c] = jnp.where(written, r.NEW[p, s, w : w + 16], old)
 
     def drain():
         for n in parts:
-            all_sent(n)
+            if n != "U":
+                all_sent(n)
+        got(r.GA.at[:, 0:3], r.xs.at[0])
         for ref, sem in sends:
             got(ref, sem)
         act_sent()
+        new_sent()
         reduced_sent()
         for e, ref in enumerate((r.MIX, r.RES, r.DNP, r.ST, r.DMP, r.OR, r.IR)):
             got(ref.at[0:3], r.es.at[e])
         given()
 
-    def out_come():
-        got(r.OR, r.eo.at[0])
-
-    def in_come():
-        got(r.IR, r.eo.at[1])
-
+    here(r.wd, r.WD.at[b], 0)
+    here(r.mem, r.MEMV, 6)
+    for n in ("A", "C", "U"):
+        tier_own(n)
+    act_own()
     greet(G, True, True)
-    here(r.wd, r.WD.at[b], 0)
     tier_start("A")
     tier_start("C")
     small_start()
     tier_start("U")
     act_start(0, 1)
+    got(r.MEMV, r.lsem.at[6])
     memory_rows()
     act_start(2, 3, 4, 5, 6)
     got(r.WD.at[b], r.lsem.at[0])
@@ -1294,51 +1358,61 @@
     each(4, grad_down, {1: lambda: onward("C", 2)})
     onward("X", 2)
     y_wait("D")
-    each(S, back_feed, {0: lambda: onward("C", 3), 1: lambda: mid(0, 0), 2: lambda: onward("X", 3)})
-    fold_pass(2, S - 1, r.DNP, r.DNR)
+    each(S, back_feed, {0: lambda: onward("C", 3), 1: lambda: mid(0, 0), 2: lambda: onward("X", 3), 3: lambda: mid(0, 1)})
+    fold_pass(2, S - 1)
     compress()
     mid_c(0)
-    mid(0, 1)
     each(4, grad_up)
-    each(S, back_norm)
-    fold_pass(4, S - 1, r.DMP, r.DMR)
+    each(G, lambda i: to_y(2, turn(i)))
+    all_sent("U")
+    each(S, back_norm, {2: lambda: mid(0, 2)})
+    fold_pass(4, S - 1)
     mid_c(1)
-    mid(0, 2)
     grad_out()
-    each(S, back_attend, {1: lambda: mid_c(2)})
+    each(S, back_attend, {1: lambda: mid_c(2), 2: lambda: mid(1, 0)})
     small_y()
-    mid(1, 0)
-    each(4, grad_proj)
+    each(4, grad_proj, {1: lambda: mid(1, 1)})
+    proj_y(0)
+    mid(1, 2)
     each(S, out_rows)
-    mid(1, 1)
+    proj_y(1)
+    fold_pass(5, S - 1)
     each(S, input_rows)
+    proj_y(2)
+    fold_pass(6, S - 1)
+    cross_c()
     new_send()
-    mid(1, 2)
-    mid(3, 0)
-    cross_c()
+    mid(2, 0)
+    proj_y(3)
     fin(0, keep(r.OD))
     give(3, r.OD, r.od)
-    small_z()
-    mid(3, 1)
+    mid(2, 1)
+    mid(2, 2)
     fin(1, hold(mineU))
     tier_back(0, mineU, r.TU)
+    mid(3, 0)
+    small_z()
+    each(S, own_out)
+    rows_out(5, r.OR.at[1], r.out)
+    mid(3, 1)
+    fin(2, hold(mineB))
+    tier_back(4, mineB, r.TB)
+    small_tier()
+    new_out()
+    memories()
+    rows_out(4, r.OR.at[0], r.om)
+    rows_out(8, r.OR.at[2], r.ocm)
     mid(3, 2)
-    small_tier()
     fin_c(hold(mineC))
     tier_back(1, mineC, r.TC)
-    out_come()
-    each(S, own_out)
-    rows_out(5, r.OR.at[0], r.out)
-    in_come()
     each(S, own_input)
     rows_out(6, r.IG, r.ig)
-    new_out()
     tier_out(0)
+    tier_out(4)
+    small_out()
     tier_out(1)
-    small_out()
-    fin(3, hold(mineA))
-    tier_back(2, mineA, r.TA)
-    tier_out(2)
+    fin(3, across)
+    give(2, r.OA, r.oa)
     drain()
 
 def whole_layer(nb, ht, hd, arrays):
@@ -1348,12 +1422,14 @@
     G, Cw, Fw, L = nb // 2, M // 4, nb * rd, 64 * nu
     dma = pltpu.SemaphoreType.DMA
     V = lambda shape, dtype=bf16: pltpu.VMEM(shape, dtype)
+    ct = 1
     D4, A4, U4, C4 = (4, rd // 4, M), (4, rw, 4 * Cw), (4, rw, Fw), (4, rw, 3 * Cw)
     ins = arrays
     outs = dict(
         out=((S, R, M), bf16),
         ig=((S, R, M), f32),
-        new=((4, S * L // 3, Cw), bf16),
+        om=((S, R, M), bf16),
+        ocm=((S, R, M), bf16),
         od=((rd, M), f32),
         ou=((rw, 4 * Fw), f32),
         oc=((3, rw, M), f32),
@@ -1395,31 +1471,35 @@
         DC=V((S * L // 3, Cw)),
         GD=V((nb,) + D4),
         GU=V((nb,) + U4),
-        GC=V((nb,) + C4),
+        GC=V((nb, 4, rw, ct * Cw)),
+        GB=V((nb, 4, rw, (3 - ct) * Cw)),
         GA=V((nb,) + A4),
         YD=V((G,) + D4),
         YU=V((G,) + U4),
-        YC=V(C4),
+        YC=V((4, rw, ct * Cw)),
+        YB=V((G, 4, rw, (3 - ct) * Cw)),
         YA=V((G,) + A4),
         ZD=V((4,) + D4),
         ZU=V((4,) + U4),
-        ZC=V((2, 4) + C4),
+        ZC=V((2, 4, 4, rw, ct * Cw)),
+        ZB=V((4, 4, rw, (3 - ct) * Cw)),
         ZA=V((4,) + A4),
         YS=V((24, 128), f32),
         ZS=V((G, 24, 128), f32),
         TU=V(U4),
-        TC=V(C4),
-        TA=V(A4),
-        NEW=V((4, S * L // 3, Cw)),
+        TC=V((4, rw, ct * Cw)),
+        TB=V((4, rw, (3 - ct) * Cw)),
+        NEW=V((4, S, L // 3, Cw)),
         IG=V((S, nu, 16, M), f32),
         OD=V((rd, M), f32),
         OU=V((rw, 4 * Fw), f32),
         OC=V((3, rw, M), f32),
         OA=V((4, rw, M), f32),
-        osem=dma((7,)),
-        lsem=dma((6,)),
-        ts=dma((5,)),
-        tr=dma((5,)),
+        MEMV=V((S, R, M)),
+        osem=dma((9,)),
+        lsem=dma((7,)),
+        ts=dma((4,)),
+        tr=dma((4,)),
         zs=dma((6,)),
         zr=dma((2, 9, G - 1)),
         ys=dma((6,)),
@@ -1429,19 +1509,21 @@
         acf=dma((3,)),
         acx=dma((7,)),
         es=dma((7,)),
-        er=dma((5, S, 2)),
-        eo=dma((2,)),
-        gys=dma((4,)),
-        gyr=dma((4, G)),
-        gzs=dma((5,)),
-        gzr=dma((5, 3)),
+        er=dma((7, S, 2)),
+        ns=dma((2,)),
+        gys=dma((5,)),
+        gyr=dma((5, G)),
+        gzs=dma((6,)),
+        gzr=dma((6, 3)),
         ss=dma((2,)),
         sr=dma((2,)),
-        gts=dma((4,)),
-        gtr=dma((4,)),
+        xs=dma((1,)),
+        xr=dma((G,)),
+        gts=dma((5,)),
+        gtr=dma((5,)),
     )
     names = list(ins) + list(outs) + list(scratch)
-    near = dict(gain=VM, bias=VM, bdown=VM, bconv=VM, bup=VM, mem=VM, mask=VM, evicted=SM, slopes=SM)
+    near = dict(gain=VM, bias=VM, bdown=VM, bconv=VM, bup=VM, mask=VM, evicted=SM, slopes=SM)
     return pl.pallas_call(
         functools.partial(layer_kernel, names, (nb, nu, S, ht, hd, M, Cw, rw, rd, rs)),
         out_shape=[jax.ShapeDtypeStruct(s, d) for s, d in outs.values()],
@@ -1457,43 +1539,17 @@
 
 def finish_kernel(names, shape, *refs):
     r = Names(names, refs)
-    r.bufs = refs[len(names) :]
     nb, rs, rd, Fw, Cw, heads = shape
-    S, R, M = r.seg.shape
     b, t = lax.axis_index("batch"), lax.axis_index("tier")
     moves = [(r.out, r.o_out), (r.ig, r.o_ig), (r.od, r.o_od), (r.ou, r.o_ou), (r.oc, r.o_oc)]
     moves += [(r.oa.at[i], o) for i, o in enumerate((r.o_q, r.o_k, r.o_v, r.o_o))]
-    into, onto = [], []
-    for i, (src, dst) in enumerate(moves):
-        n = src.shape[0]
-        cut = 4 if n % 4 == 0 else 1
-        for j in range(cut):
-            rows = pl.ds(j * (n // cut), n // cut)
-            buf = r.bufs[i].at[rows]
-            into.append(pltpu.make_async_copy(src.at[rows], buf, r.sem.at[len(into)]))
-            onto.append(pltpu.make_async_copy(buf, dst.at[rows], r.sem.at[64 + len(onto)]))
+    moves += [(r.om, r.o_mem), (r.ocm, r.o_comp)]
+    bufs = refs[len(names) :]
+    into = [pltpu.make_async_copy(src, buf, r.sem.at[i]) for i, ((src, _), buf) in enumerate(zip(moves, bufs))]
+    n = len(moves)
+    onto = [pltpu.make_async_copy(buf, dst, r.sem.at[n + i]) for i, ((_, dst), buf) in enumerate(zip(moves, bufs))]
     for cp in into:
         cp.start()
-    nw = 4 * R // 3
-    slots = 4 * R - nw
-    place = lax.broadcasted_iota(jnp.int32, (R, 1), 0) + R * t
-    for s in range(S):
-        r.o_mem[s] = jnp.where(place < r.evicted[s], r.seg[s], r.mem[s])
-        r.o_comp[s] = r.comp[s]
-    for tier in range(4):
-        first = max(slots - R * tier, 0)
-        if first < R:
-
-            @pl.when(t == tier)
-            def _(tier=tier, first=first):
-                w = R * tier + first - slots
-                side = lax.broadcasted_iota(jnp.int32, (R - first, 1), 0)
-                for s in range(S):
-                    written = 3 * (side + w) + 3 <= r.evicted[s]
-                    for q in range(4):
-                        c = slice(q * Cw, (q + 1) * Cw)
-                        rows = r.new[q, s * nw + w : s * nw + w + R - first]
-                        r.o_comp[s, first:, c] = jnp.where(written, rows, r.comp[s, first:, c])
     spot = 4 * b + t
     block, inner = spot // (Cw // rs), lax.rem(spot, Cw // rs)
     half, group = inner // (128 // rs), lax.rem(inner, 128 // rs)
@@ -1515,15 +1571,15 @@
 
 
 def finish(nb, heads, arrays):
-    S, R, M = arrays["seg"].shape
+    S, R, M = arrays["out"].shape
     rw, rd, rs = arrays["oa"].shape[1], arrays["od"].shape[0], M // (4 * nb)
     Cw, Fw = M // 4, nb * rd
     rows, mat, vec = (S, R, M), (rw, M), (1, rs)
     outs = dict(
         o_out=(rows, bf16, ANY),
         o_ig=(rows, f32, ANY),
-        o_mem=(rows, bf16, VM),
-        o_comp=(rows, bf16, VM),
+        o_mem=(rows, bf16, ANY),
+        o_comp=(rows, bf16, ANY),
         o_q=(mat, f32, ANY),
         o_k=(mat, f32, ANY),
         o_v=(mat, f32, ANY),
@@ -1538,16 +1594,15 @@
         o_conv=(vec, f32, VM),
         o_slopes=((1, heads), f32, VM),
     )
-    moved = ("o_out", "o_ig", "o_od", "o_ou", "o_oc", "o_q", "o_k", "o_v", "o_o")
-    near = dict(seg=VM, mem=VM, comp=VM, new=VM, os=VM, evicted=SM)
+    moved = ("o_out", "o_ig", "o_od", "o_ou", "o_oc", "o_q", "o_k", "o_v", "o_o", "o_mem", "o_comp")
     return pl.pallas_call(
         functools.partial(
             finish_kernel, list(arrays) + list(outs) + ["sem"], (nb, rs, rd, Fw, Cw, heads)
         ),
         out_shape=[jax.ShapeDtypeStruct(s, d) for s, d, _ in outs.values()],
-        in_specs=[near.get(n, ANY) for n in arrays],
+        in_specs=[VM if n == "os" else ANY for n in arrays],
         out_specs=[o[2] for o in outs.values()],
-        scratch_shapes=[pltpu.SemaphoreType.DMA((128,))]
+        scratch_shapes=[pltpu.SemaphoreType.DMA((2 * len(moved),))]
         + [pltpu.VMEM(outs[n][0], outs[n][1]) for n in moved],
         compiler_params=pltpu.CompilerParams(vmem_limit_bytes=63 * 2**20),
         name="finish",
@@ -1579,7 +1634,7 @@
     S, R, M = segment.shape
     heads = slopes.shape[0]
     line = lambda v: v.reshape(1, -1)
-    names = ("out", "ig", "new", "od", "ou", "oc", "oa", "os")
+    names = ("out", "ig", "om", "ocm", "od", "ou", "oc", "oa", "os")
     made = whole_layer(
         nb,
         heads // 4,
@@ -1606,8 +1661,7 @@
             slopes=slopes,
         ),
     )
-    arrays = dict(zip(names, made), seg=segment, mem=memory, comp=compressed, evicted=evicted)
-    outs = finish(nb, heads, arrays)
+    outs = finish(nb, heads, dict(zip(names, made)))
     flat = (9, 11, 12, 13, 15, 16)
     return tuple(o.reshape(-1) if i in flat else o for i, o in enumerate(outs))
 

time: 192 us -> 177 us (0.922)
  Pallas kernels: 191 us -> 175 us
    pallas_call x1, Pallas kernels: 185 us -> 171 us  [whole_layer(): pl.pallas_call(functools.partial(layer_kernel, names, (nb, nu, S, ht, hd,...]
where the time goes in v4:
time: 177 us; the launch traced here: 176 us
  Pallas kernels  175 us (99%)
    pallas_call x1, Pallas kernels, whole_layer(): pl.pallas_call(functools.partial(layer_kernel, names, (nb, nu, S, ht, hd,...  171 us
    pallas_call x1, Pallas kernels, finish(): pl.pallas_call(functools.partial(finish_kernel, list(arrays) + list(outs)...  4.61 us

profile of v4, /device:TPU:11, one launch (start us, length us, event | category | flops | bytes accessed | tf_op | source)
XLA Modules:
  0.0 176.2 jit_solution(623715945866227893)
XLA Ops:
  0.7 170.8 %whole_layer.1 = (bf16[4,48,1024]{2,1,0:T(8,128)(2,1)}, f32[4,48,1024]{2,1,0:T(8,128)}, bf16[4,48,1024]{2,1,0:T(8,128)(2,1)}, bf16[4,48,1024]{2,1,0:T(8,128)(2,1...) custom-call(bf16[32,1024]{1,0:T(8,128)(2,1)} %refs_0_.1, ...), custom_call_target="tpu_custom_call" | custom-call | tf_op jit(solution)/shard_map/whole_layer/pallas_call | solution.py:1527
  171.4 4.6 %finish.1 = (bf16[4,48,1024]{2,1,0:T(8,128)(2,1)}, f32[4,48,1024]{2,1,0:T(8,128)}, bf16[4,48,1024]{2,1,0:T(8,128)(2,1)}, bf16[4,48,1024]{2,1,0:T(8,128)(2,1)}, f...) custom-call(bf16[4,48,1024]{2,1,0:T(8,128)(2,1)} %get-tuple-element., ...), custom_call_target="tpu_custom_call" | custom-call | tf_op jit(solution)/shard_map/finish/pallas_call | solution.py:1598

commit v5 on v4

--- a/solution.py
+++ b/solution.py
@@ -669,15 +669,15 @@
         col = ((1 - y) if n == "X" else y) if col is None else col
         return w.at[2 * zz + col, pl.ds(at, size)]
 
-    def hop(part, at, j, way):
+    def hop(part, at, zz, way):
         k = part[1]
         peer, past = (right, z < G - 1) if way == 0 else (left, z > 0)
-        return past, remote(at, at, r.zs.at[part[4]], r.zr.at[way, k, j], peer)
+        return past, remote(at, at, r.zs.at[part[4]], r.zr.at[k, zz - way], peer)
 
     def own_z(n):
         for part in parts[n]:
             for way in (0, 1):
-                past, cp = hop(part, chunk_of(n, part, z), 0, way)
+                past, cp = hop(part, chunk_of(n, part, z), z, way)
                 if_(past, cp.start)
 
     def own_y(n):
@@ -692,21 +692,27 @@
                     zz = z - j if way == 0 else z + j
                     step(part, j, way, zz, chunk_of(n, part, zz), zz >= 0 if way == 0 else zz < G)
 
-    def onward(n, *js):
+    def onward(n, *js, cross=True):
         def step(part, j, way, zz, at, there):
             k = part[1]
 
             def body():
-                got(at, r.zr.at[way, k, j - 1])
+                got(at, r.zr.at[k, zz - way])
                 if j < G - 1:
-                    past, cp = hop(part, at, j, way)
+                    past, cp = hop(part, at, zz, way)
                     if_(past, cp.start)
-                if n not in "CX":
+                if n not in "CX" and cross:
                     remote(at, at, r.ys.at[part[4]], r.yr.at[part[4]], ypeer).start()
 
             if_(there, body)
 
         arrivals(n, step, js or range(1, G))
+
+    def over(n, *js):
+        def step(part, j, way, zz, at, there):
+            if_(there, remote(at, at, r.ys.at[part[4]], r.yr.at[part[4]], ypeer).start)
+
+        arrivals(n, step, js)
 
     def all_sent(n):
         w, k = parts[n][0][0], parts[n][0][4]
@@ -720,20 +726,9 @@
         got(w.at[0 : 1 if n == "C" else G], r.yr.at[k])
 
     def small_start():
-        lane = lax.broadcasted_iota(jnp.int32, (8, 128), 1)
-        side = lax.broadcasted_iota(jnp.int32, (8, 128), 0)
-        spot = lax.rem(4 * b + t, Cw // rs)
-        half, group = spot // (128 // rs), lax.rem(spot, 128 // rs)
-        for q, v in enumerate((r.gain, r.bias, r.bdown, r.bconv)):
-            r.SMG[q : q + 1, :rs] = v[...].astype(f32)
-        r.SMG[4:5, :rd] = r.bup[...].astype(f32)
-        acc = jnp.zeros((8, 128), f32)
-        for q in range(4):
-            turned = pltpu.roll(jnp.broadcast_to(r.SMG[q : q + 1], (8, 128)), rs * group, 1)
-            mine = (side == 2 * q + half) & (lane >= rs * group) & (lane < rs * (group + 1))
-            acc = jnp.where(mine, turned, acc)
-        r.SM[b, t, 0:8] = acc
-        r.SM[b, t, 8:16] = jnp.broadcast_to(r.SMG[4:5], (8, 128))
+        r.SM[b, t] = jnp.zeros((8, 128), f32)
+        for q, v in enumerate((r.gain, r.bias, r.bdown, r.bconv, r.bup)):
+            r.SM[b, t, q : q + 1, : v.shape[1]] = v[...].astype(f32)
         tier_start("S")
 
     def memory_rows():
@@ -850,17 +845,16 @@
         spread_send(1, s, r.RES)
 
     def vectors():
-        for q in range(4):
-            block = r.SM[bq * q, 0, 0:8]
-            for bb in range(bq * q, bq * (q + 1)):
-                for tt in range(4):
-                    if bb != bq * q or tt:
-                        block = block + r.SM[bb, tt, 0:8]
-            for i in range(8):
-                at = q * Cw + 128 * (i % 2)
-                r.VV[i // 2 : i // 2 + 1, at : at + 128] = block[i : i + 1]
+        lane = lax.broadcasted_iota(jnp.int32, (8, 128), 1)
+        for at in range(0, M, 128):
+            block = jnp.zeros((8, 128), f32)
+            for i in range(128 // rs):
+                spot = at // rs + i
+                turned = pltpu.roll(r.SM[spot // 4, spot % 4], rs * i, 1)
+                block = jnp.where((lane >= rs * i) & (lane < rs * (i + 1)), turned, block)
+            r.VV[0:4, at : at + 128] = block[0:4]
         for bb in range(nb):
-            r.VV[4:5, bb * rd : (bb + 1) * rd] = r.SM[bb, t, 8:9, :rd]
+            r.VV[4:5, bb * rd : (bb + 1) * rd] = r.SM[bb, t, 4:5, :rd]
 
     def xhat_of(s, q):
         return (r.RES[q, s].astype(f32) - r.MU[s, :, :1]) * r.MU[s, :, 1:2]
@@ -1339,24 +1333,25 @@
     act_forward(0, 1, 2, 3, 4)
     act_wait(0)
     y_wait("A")
-    each(S, project, {0: lambda: onward("U", 2), 1: lambda: onward("D", 1)})
+    each(S, project, {0: lambda: onward("U", 2), 1: lambda: onward("D", 1, cross=False)})
     own_z("C")
+    each(S, attend, {1: lambda: onward("U", 3)})
+    over("D", 1)
+    spread_pass(0, 0, r.MIX)
+    each(S, residual, {1: lambda: onward("D", 2)})
     own_z("X")
-    each(S, attend, {1: lambda: onward("U", 3)})
-    spread_pass(0, 0, r.MIX)
-    each(S, residual)
-    onward("D", 2)
+    onward("C", 1)
     y_wait("S")
     vectors()
-    onward("C", 1)
     act_forward(5, 6)
+    onward("D", 3)
     y_wait("U")
     spread_pass(1, 0, r.RES)
-    each(S, feed, {1: lambda: onward("X", 1), 3: lambda: onward("D", 3)})
+    each(S, feed, {1: lambda: onward("X", 1)})
     act_wait(1)
     act_wait(2)
-    each(4, grad_down, {1: lambda: onward("C", 2)})
-    onward("X", 2)
+    onward("C", 2)
+    each(4, grad_down, {2: lambda: onward("X", 2)})
     y_wait("D")
     each(S, back_feed, {0: lambda: onward("C", 3), 1: lambda: mid(0, 0), 2: lambda: onward("X", 3), 3: lambda: mid(0, 1)})
     fold_pass(2, S - 1)
@@ -1367,22 +1362,23 @@
     all_sent("U")
     each(S, back_norm, {2: lambda: mid(0, 2)})
     fold_pass(4, S - 1)
-    mid_c(1)
     grad_out()
-    each(S, back_attend, {1: lambda: mid_c(2), 2: lambda: mid(1, 0)})
+    each(S, back_attend, {2: lambda: mid(1, 0)})
     small_y()
     each(4, grad_proj, {1: lambda: mid(1, 1)})
+    mid_c(1)
     proj_y(0)
     mid(1, 2)
     each(S, out_rows)
     proj_y(1)
+    mid_c(2)
     fold_pass(5, S - 1)
     each(S, input_rows)
     proj_y(2)
     fold_pass(6, S - 1)
-    cross_c()
     new_send()
     mid(2, 0)
+    cross_c()
     proj_y(3)
     fin(0, keep(r.OD))
     give(3, r.OD, r.od)
@@ -1397,7 +1393,6 @@
     mid(3, 1)
     fin(2, hold(mineB))
     tier_back(4, mineB, r.TB)
-    small_tier()
     new_out()
     memories()
     rows_out(4, r.OR.at[0], r.om)
@@ -1405,14 +1400,15 @@
     mid(3, 2)
     fin_c(hold(mineC))
     tier_back(1, mineC, r.TC)
+    small_tier()
     each(S, own_input)
     rows_out(6, r.IG, r.ig)
     tier_out(0)
     tier_out(4)
-    small_out()
     tier_out(1)
     fin(3, across)
     give(2, r.OA, r.oa)
+    small_out()
     drain()
 
 def whole_layer(nb, ht, hd, arrays):
@@ -1422,7 +1418,7 @@
     G, Cw, Fw, L = nb // 2, M // 4, nb * rd, 64 * nu
     dma = pltpu.SemaphoreType.DMA
     V = lambda shape, dtype=bf16: pltpu.VMEM(shape, dtype)
-    ct = 1
+    ct = 2
     D4, A4, U4, C4 = (4, rd // 4, M), (4, rw, 4 * Cw), (4, rw, Fw), (4, rw, 3 * Cw)
     ins = arrays
     outs = dict(
@@ -1441,7 +1437,7 @@
         WU=V((nb,) + U4),
         WC=V((nb,) + C4),
         WD=V((nb, rd, M)),
-        SM=V((nb, 4, 16, 128), f32),
+        SM=V((nb, 4, 8, 128), f32),
         CTX=V((S, 12 * nu, 16, M)),
         COT=V((S, 4 * nu, 16, M)),
         MK=V((S, 4, L // 12, 128), f32),
@@ -1501,7 +1497,7 @@
         ts=dma((4,)),
         tr=dma((4,)),
         zs=dma((6,)),
-        zr=dma((2, 9, G - 1)),
+        zr=dma((9, G - 1)),
         ys=dma((6,)),
         yr=dma((6,)),
         acs=dma((3,)),

time: 177 us -> 171 us (0.966)
  Pallas kernels: 175 us -> 170 us
    pallas_call x1, Pallas kernels: 171 us -> 166 us  [whole_layer(): pl.pallas_call(functools.partial(layer_kernel, names, (nb, nu, S, ht, hd,...]
where the time goes in v5:
time: 171 us
  Pallas kernels  170 us (99%)
    pallas_call x1, Pallas kernels, whole_layer(): pl.pallas_call(functools.partial(layer_kernel, names, (nb, nu, S, ht, hd,...  166 us
    pallas_call x1, Pallas kernels, finish(): pl.pallas_call(functools.partial(finish_kernel, list(arrays) + list(outs)...  4.61 us

profile of v5, /device:TPU:11, one launch (start us, length us, event | category | flops | bytes accessed | tf_op | source)
XLA Modules:
  0.0 171.1 jit_solution(98393171430487392)
XLA Ops:
  0.7 165.8 %whole_layer.1 = (bf16[4,48,1024]{2,1,0:T(8,128)(2,1)}, f32[4,48,1024]{2,1,0:T(8,128)}, bf16[4,48,1024]{2,1,0:T(8,128)(2,1)}, bf16[4,48,1024]{2,1,0:T(8,128)(2,1...) custom-call(bf16[32,1024]{1,0:T(8,128)(2,1)} %refs_0_.1, ...), custom_call_target="tpu_custom_call" | custom-call | tf_op jit(solution)/shard_map/whole_layer/pallas_call | solution.py:1523
  166.5 4.6 %finish.1 = (bf16[4,48,1024]{2,1,0:T(8,128)(2,1)}, f32[4,48,1024]{2,1,0:T(8,128)}, bf16[4,48,1024]{2,1,0:T(8,128)(2,1)}, bf16[4,48,1024]{2,1,0:T(8,128)(2,1)}, f...) custom-call(bf16[4,48,1024]{2,1,0:T(8,128)(2,1)} %get-tuple-element., ...), custom_call_target="tpu_custom_call" | custom-call | tf_op jit(solution)/shard_map/finish/pallas_call | solution.py:1594

commit v6 on v5

--- a/solution.py
+++ b/solution.py
@@ -540,7 +540,7 @@
     r = Names(names, refs)
     nb, nu, S, ht, hd, M, Cw, rw, rd, rs = shape
     R = 16 * nu
-    ct = r.OC.shape[0] - r.GB.shape[-1] // Cw
+    Hw = Cw // 2
     G, bq = nb // 2, nb // 4
     L = 16 * 4 * nu
     C3 = 3 * L
@@ -626,7 +626,10 @@
     wide = lambda at, size: pl.ds(pl.multiple_of(at, 128), size)
     mats = (r.w_query, r.w_key, r.w_value, r.w_output)
     whole = {"S": r.SM, "A": r.WA, "U": r.WU, "C": r.WC}
-    index = {"S": 0, "A": 1, "U": 2, "C": 3}
+    index = {"S": 0, "A": 1, "U": 2, "C": 3, "H": 7}
+
+    def tiers(n, at):
+        return r.WCX.at[at] if n == "H" else whole[n].at[b, at]
 
     def cuts(n, q):
         if n == "S":
@@ -637,7 +640,10 @@
             return [
                 (r.w_up.at[:, wide((4 * i + q) * rd, rd)], r.WU.at[b, t, :, i * rd : (i + 1) * rd]) for i in range(nb)
             ]
-        return [(r.w_conv.at[i, :, wide(Cw * q, Cw)], r.WC.at[b, t, :, i * Cw : (i + 1) * Cw]) for i in range(3)]
+        half, to = (y, r.WC.at[b]) if n == "C" else (1 - y, r.WCX)
+        return [
+            (r.w_conv.at[i, :, wide(Cw * q + Hw * half, Hw)], to.at[t, :, i * Hw : (i + 1) * Hw]) for i in range(3)
+        ]
 
     def tier_own(n):
         for src, dst in cuts(n, t):
@@ -648,26 +654,45 @@
         for d in (1, 2, 3):
             for src, dst in cuts(n, t ^ d):
                 remote(src, dst, r.ts.at[i], r.tr.at[i], (b, t ^ d)).start()
-        left_all(whole[n].at[b, 0:3], r.ts.at[i])
+        left_all(tiers(n, slice(0, 3)), r.ts.at[i])
 
     def tier_wait(n):
         i = index[n]
         if n != "S":
-            got(whole[n].at[b, t], r.lsem.at[i])
-        got(whole[n].at[b, 0:3], r.tr.at[i])
+            got(tiers(n, t), r.lsem.at[i])
+        got(tiers(n, slice(0, 3)), r.tr.at[i])
 
     def if_(cond, body):
         pl.when(cond)(body)
 
+    def at_ends(body):
+        return lambda: if_(ends, body)
+
+    def inside(body):
+        return lambda: if_(~ends, body)
+
+    def both(*bodies):
+        def run():
+            for body in bodies:
+                body()
+
+        return run
+
     right, left = (2 * z + 2 + y, t), (2 * z - 2 + y, t)
     parts = {"S": [(r.SM, 0, 0, 4, 0)], "C": [(r.WC, 1, 0, 4, 1)], "X": [(r.WC, 2, 0, 4, 2)]}
-    for i, (n, w, size) in enumerate((("A", r.WA, 2), ("U", r.WU, 2), ("D", r.WD, rd // 2))):
-        parts[n] = [(w, 3 + 2 * i + h, h * size, size, 3 + i) for h in (0, 1)]
+    for i, (n, w) in enumerate((("A", r.WA), ("U", r.WU))):
+        parts[n] = [(w, 3 + 2 * i + h, h * 2, 2, 3 + i) for h in (0, 1)]
+    for i, (n, at) in enumerate((("D", 0), ("E", rd // 2), ("F", rd // 2))):
+        parts[n] = [(r.WD, 7 + i, at, rd // 2, 5 + i)]
 
     def chunk_of(n, part, zz, col=None):
         w, k, at, size, _ = part
-        col = ((1 - y) if n == "X" else y) if col is None else col
+        col = ((1 - y) if n in "XF" else y) if col is None else col
         return w.at[2 * zz + col, pl.ds(at, size)]
+
+    def chunks(n, count):
+        w, _, at, size, _ = parts[n][0]
+        return w.at[0:count, at : at + size * len(parts[n])]
 
     def hop(part, at, zz, way):
         k = part[1]
@@ -683,7 +708,7 @@
     def own_y(n):
         for part in parts[n]:
             at, k = chunk_of(n, part, z), part[4]
-            remote(at, at, r.ys.at[k], r.yr.at[k], ypeer).start()
+            remote(r.WCX if n == "C" else at, at, r.ys.at[k], r.yr.at[k], ypeer).start()
 
     def arrivals(n, step, js):
         for j in js:
@@ -701,7 +726,7 @@
                 if j < G - 1:
                     past, cp = hop(part, at, zz, way)
                     if_(past, cp.start)
-                if n not in "CX" and cross:
+                if n not in "CXEF" and cross:
                     remote(at, at, r.ys.at[part[4]], r.yr.at[part[4]], ypeer).start()
 
             if_(there, body)
@@ -715,15 +740,14 @@
         arrivals(n, step, js)
 
     def all_sent(n):
-        w, k = parts[n][0][0], parts[n][0][4]
-        if_(ends, lambda: got(w.at[0:1], r.zs.at[k]))
-        if_(~ends, lambda: got(w.at[0:5], r.zs.at[k]))
-        if n != "X":
-            got(w.at[0 : 1 if n == "C" else G], r.ys.at[k])
+        k = parts[n][0][4]
+        if_(ends, lambda: got(chunks(n, 1), r.zs.at[k]))
+        if_(~ends, lambda: got(chunks(n, 5), r.zs.at[k]))
+        if n not in "XF":
+            got(chunks(n, 1 if n in "CE" else G), r.ys.at[k])
 
     def y_wait(n):
-        w, k = parts[n][0][0], parts[n][0][4]
-        got(w.at[0 : 1 if n == "C" else G], r.yr.at[k])
+        got(chunks(n, 1 if n in "CE" else G), r.yr.at[parts[n][0][4]])
 
     def small_start():
         r.SM[b, t] = jnp.zeros((8, 128), f32)
@@ -743,7 +767,9 @@
             square = lambda axis: lax.broadcasted_iota(jnp.int32, (R // 3, R // 3), axis)
             line = jnp.broadcast_to(r.mask[s : s + 1].astype(f32), (R // 3, R // 3))
             col = jnp.sum(jnp.where(square(0) == square(1), line, 0.0), axis=1, keepdims=True)
-            r.MK[s, t] = jnp.broadcast_to(col, (R // 3, 128))
+            spot = lax.broadcasted_iota(jnp.int32, (R // 3, 128), 0) + (R // 3) * t
+            lane = lax.broadcasted_iota(jnp.int32, (R // 3, 128), 1)
+            r.MK[s, t] = jnp.where((lane < 64) | (3 * spot + 3 <= r.evicted[s]), col, 0.0)
 
     def rows_of(src, buf, first):
         at = lambda q: buf.at[:, pl.ds(first + nu * q, nu)]
@@ -752,6 +778,17 @@
 
     def held(at):
         return [(at(t), at(t))], at, False
+
+    def memory_y():
+        for i in range(3):
+            remote(r.CTX.at[:, 4 * nu + 4 * i + t], r.MEMX.at[:, 4 * i + t], r.ms.at[0], r.ms.at[1], ypeer).start()
+        remote(r.MK.at[:, t], r.MKX.at[:, t], r.ms.at[2], r.ms.at[3], ypeer).start()
+        left_all(r.MEMX.at[:, 0:3], r.ms.at[0])
+        left_all(r.MKX.at[:, 0], r.ms.at[2])
+
+    def memory_come():
+        got(r.MEMX.at[:, 0:3], r.ms.at[1])
+        got(r.MKX.at[:, 0], r.ms.at[3])
 
     pieces = [
         rows_of(r.seg, r.CTX, 8 * nu),
@@ -761,10 +798,14 @@
         held(lambda q: r.CTX.at[:, 4 * nu + 8 + q]),
         rows_of(r.cot, r.COT, 0),
         held(lambda q: r.MK.at[:, q]),
+        held(lambda q: r.MEMX.at[:, q]),
+        held(lambda q: r.MEMX.at[:, 4 + q]),
+        held(lambda q: r.MEMX.at[:, 8 + q]),
+        held(lambda q: r.MKX.at[:, q]),
     ]
 
-    group = lambda i: 0 if i < 5 else i - 4
-    grouped = [(r.CTX, 3 * nu), (r.COT, nu), (r.MK, 1)]
+    group = lambda i: 0 if i < 5 else (1, 2, 3, 3, 3, 4)[i - 5]
+    grouped = [(r.CTX, 3 * nu), (r.COT, nu), (r.MK, 1), (r.MEMX, 3), (r.MKX, 1)]
 
     def act_own():
         for i, (cut, at, far) in enumerate(pieces):
@@ -885,7 +926,7 @@
         inner = jnp.where(z == 1, low, G - 1 - low)
         return jnp.where(z == 0, G - 1 - j, jnp.where(z == G - 1, j, inner))
 
-    grads = [(r.GD, r.YD, r.ZD), (r.GU, r.YU, r.ZU), (r.GB, r.YB, r.ZB), (r.WU, r.YA, r.ZA)]
+    grads = {0: (r.GD, r.YD, r.ZD), 1: (r.GU, r.YU, r.ZU), 3: (r.WU, r.YA, r.ZA)}
 
     def to_y(k, zz):
         g, yb, zb = grads[k]
@@ -910,6 +951,8 @@
         to = jnp.where(ends, mate, o)
         slot = jnp.where(o == mate, 2, jnp.where(ends, lax.rem(o, 2), 3))
         remote(at, zb.at[slot], r.gzs.at[sem], r.gzr.at[sem, jnp.minimum(slot, 2)], (2 * to + y, t)).start()
+
+    straight = ()
 
     def mid(k, *steps):
         g, yb, zb = grads[k]
@@ -918,7 +961,10 @@
             at = yb.at[o]
             got(at, r.gyr.at[k, o])
             plus(at, g.at[2 * o + y])
-            pass_on(i, at, zb, o, k)
+            if k in straight:
+                remote(at, zb.at[z], r.gzs.at[k], r.gzr.at[k, 2], (2 * o + y, t)).start()
+            else:
+                pass_on(i, at, zb, o, k)
 
     def mid_c(*steps):
         for i in steps or range(G - 1):
@@ -927,12 +973,14 @@
                 pass_on(i, r.GC.at[2 * o + col], r.ZC.at[c], o, 4 + c)
 
     def arrived(zb, sem):
-        got(zb.at[2:4], r.gzr.at[sem, 2])
-
-    def summed(at, zb, more, store):
+        n = 3 if sem in straight else 2
+        got(zb.at[4 - n : 4], r.gzr.at[sem, 2])
+        return [zb.at[lax.rem(z + d, G)] for d in range(1, G)] if n == 3 else [zb.at[2], zb.at[3]]
+
+    def summed(at, more, store):
         def total(i):
             acc = at[i].astype(f32)
-            for o in [zb.at[2], zb.at[3]] + more:
+            for o in more:
                 acc = acc + o[i].astype(f32)
             store(i, acc)
 
@@ -942,26 +990,26 @@
         g, yb, zb = grads[k]
         at = yb.at[z]
         got(at, r.gyr.at[k, z])
-        arrived(zb, k)
-        summed(at, zb, [g.at[2 * z + y]], store)
+        summed(at, arrived(zb, k) + [g.at[2 * z + y]], store)
 
     def cross_c():
-        arrived(r.ZC.at[0], 4)
+        come = arrived(r.ZC.at[0], 4)
         other = r.GC.at[2 * z + 1 - y]
 
         def store(i, acc):
             other[i] = acc.astype(bf16)
 
-        summed(other, r.ZC.at[0], [], store)
+        summed(other, come, store)
         remote(other, r.YC, r.gys.at[4], r.gyr.at[4, 0], ypeer).start()
 
     def fin_c(store):
+        summed(r.GC.at[2 * z + y], arrived(r.ZC.at[1], 5), store)
+
+    def crossed_c():
         got(r.YC, r.gyr.at[4, 0])
-        arrived(r.ZC.at[1], 5)
-        summed(r.GC.at[2 * z + y], r.ZC.at[1], [r.YC], store)
 
     def reduced_sent():
-        for k, (g, yb, zb) in enumerate(grads):
+        for k, (g, yb, zb) in grads.items():
             got(g.at[0:G], r.gys.at[k])
             got(g.at[0:3], r.gzs.at[k])
         got(r.YC, r.gys.at[4])
@@ -1056,6 +1104,12 @@
         for q in range(4):
             g = dot_tn(r.MIX[q].reshape(S * L, Cw), r.DB[...].reshape(S * L, Cw))
             r.GA[bq * q : bq * (q + 1), :, :, 3 * Cw :] = g.astype(bf16).reshape(bq, 4, rw, Cw)
+        by_tier(slice(None), slice(3 * Cw, 4 * Cw), r.xs.at[1], r.xr.at[G])
+
+    def by_tier(rows, c, sent, come):
+        for d in (1, 2, 3):
+            remote(r.GA.at[rows, t ^ d, :, c], r.WU.at[rows, t, :, c], sent, come, (b, t ^ d)).start()
+        r.WU[rows, t, :, c] = r.GA[rows, t, :, c]
 
     def out_rows(s):
         for q in range(4):
@@ -1068,32 +1122,36 @@
         fold_late(5, s)
 
 
-    def windows(k):
-        return r.CTX[:, 4 * nu + 4 * k : 4 * nu + 4 * (k + 1)].reshape(S * nw, M)
+    hc = wide(t * Cw + Hw * y, Hw)
+
+    def windows(k, g):
+        buf, at = (r.MEMX, 4 * k) if g else (r.CTX, 4 * nu + 4 * k)
+        return buf.at[:, at : at + 4]
 
     def compress():
-        conv = r.VV[3:4, tc]
-        pooled = 0.0
+        sums = jnp.zeros((1, Hw), f32)
+        for g in (0, 1):
+            conv = r.VV[3:4, hc]
+            pooled = 0.0
+            for k in range(3):
+                wk = r.WC[:, :, :, k * Hw : (k + 1) * Hw].reshape(M, Hw)
+                conv = conv + jnp.dot(windows(k, g)[...].reshape(S * nw, M), wk, preferred_element_type=f32)
+                pooled = pooled + windows(k, g)[:, :, :, hc].reshape(S * nw, Hw).astype(f32)
+            marks = (r.MKX if g else r.MK)[...].reshape(S * nw, 128)
+            fresh = (marks[:, :1] * conv).astype(bf16).reshape(S, nw, Hw)
+            if g:
+                r.NEWX[...] = fresh
+            else:
+                r.NEW[t, :, :, wide(Hw * y, Hw)] = fresh
+            d_conv = marks[:, 64:65] * (conv - pooled * (1.0 / 3.0))
+            sums = sums + jnp.sum(d_conv, axis=0, keepdims=True)
+            r.DC[g] = d_conv.astype(bf16)
+        r.SMG[pl.ds(Fw // 128 + 3 * (Cw // 128) + y, 1)] = sums
+        remote(r.NEWX, r.NEW.at[t, :, :, wide(Hw * y, Hw)], r.ns.at[2], r.ns.at[3], ypeer).start()
+        left_all(r.NEWX, r.ns.at[2])
         for k in range(3):
-            wk = r.WC[:, :, :, k * Cw : (k + 1) * Cw].reshape(M, Cw)
-            conv = conv + jnp.dot(windows(k), wk, preferred_element_type=f32)
-            pooled = pooled + r.CTX[:, 4 * nu + 4 * k : 4 * nu + 4 * (k + 1), :, tc].reshape(S * nw, Cw).astype(f32)
-        mask = r.MK[...].reshape(S * nw, 128)[:, :1]
-        done = 3 * lax.broadcasted_iota(jnp.int32, (nw, 128), 0) + 3
-        live = jnp.concatenate(
-            [(done <= r.evicted[s]).astype(f32)[:, :1] for s in range(S)], axis=0
-        ) * mask
-        r.NEW[t] = (mask * conv).astype(bf16).reshape(S, nw, Cw)
-        d_conv = live * (conv - pooled * (1.0 / 3.0))
-        total = jnp.sum(d_conv, axis=0, keepdims=True)
-        for k in range(Cw // 128):
-            at = Fw // 128 + 3 * (Cw // 128) + k
-            r.SMG[at : at + 1] = total[:, 128 * k : 128 * (k + 1)]
-        r.DC[...] = d_conv.astype(bf16)
-        for k in range(3):
-            g = dot_tn(windows(k), r.DC[...])
-            far, at = (r.GC, k) if k < ct else (r.GB, k - ct)
-            far[:, :, :, at * Cw : (at + 1) * Cw] = g.astype(bf16).reshape(nb, 4, rw, Cw)
+            grad = sum(dot_tn(windows(k, g)[...].reshape(S * nw, M), r.DC[g]) for g in (0, 1))
+            r.GC[:, :, :, k * Hw : (k + 1) * Hw] = grad.astype(bf16).reshape(nb, 4, rw, Hw)
 
     slope_row = Fw // 128 + 4 * (Cw // 128)
 
@@ -1129,14 +1187,14 @@
         rows = pl.ds(j * bq, bq)
         r.GA[rows, :, :, :Cw] = gq.astype(bf16).reshape(bq, 4, rw, Cw)
         r.GA[rows, :, :, Cw : 3 * Cw] = gkv.astype(bf16).reshape(bq, 4, rw, 2 * Cw)
-        for d in (1, 2, 3):
-            remote(r.GA.at[rows, t ^ d], r.WU.at[rows, t], r.xs.at[0], r.xr.at[j], (b, t ^ d)).start()
-        r.WU[rows, t] = r.GA[rows, t]
+        by_tier(rows, slice(0, 3 * Cw), r.xs.at[0], r.xr.at[j])
 
     def proj_y(*steps):
         for i in steps:
             j = turn(i)
-            got(r.WU.at[pl.ds(j * bq, bq), 0:3], r.xr.at[j])
+            if i == 0:
+                got(r.WU.at[:, 0:3, :, 3 * Cw :], r.xr.at[G])
+            got(r.WU.at[pl.ds(j * bq, bq), 0:3, :, : 3 * Cw], r.xr.at[j])
             to_y(3, j)
 
     def own_out(s):
@@ -1198,7 +1256,7 @@
     def own_input(s):
         r.IG[s] = folded(6, s)
 
-    mineU, mineC, mineA, mineB = (g.at[2 * z + y] for g in (r.GU, r.GC, r.GA, r.GB))
+    mineU, mineC = (g.at[2 * z + y] for g in (r.GU, r.GC))
     def give(i, src, dst):
         pltpu.make_async_copy(src, dst, r.osem.at[i]).start()
 
@@ -1206,35 +1264,26 @@
         for j in range(nu):
             give(i, src.at[:, j], dst.at[:, 16 * j : 16 * j + 16])
 
-    backs = (
-        (mineU, r.TU, r.OU, r.ou),
-        (mineC, r.TC, r.OC.at[0:ct], r.oc.at[0:ct]),
-        None,
-        None,
-        (mineB, r.TB, r.OC.at[ct:3], r.oc.at[ct:3]),
-    )
-    places_out = (0, 1, 2, None, 7)
-
-    def lay(k, o, q, rows):
+    backs = {0: (mineU, r.TU), 1: (mineC, r.TC), 4: (r.YC, r.TB)}
+
+    def lay(k, q, rows):
         if k == 0:
             for i in range(nb):
-                o[:, wide((4 * i + q) * rd, rd)] = rows[:, i * rd : (i + 1) * rd].astype(f32)
+                r.OU[:, wide((4 * i + q) * rd, rd)] = rows[:, i * rd : (i + 1) * rd].astype(f32)
         else:
-            for i in range(o.shape[0]):
-                o[i, :, wide(q * Cw, Cw)] = rows[:, i * Cw : (i + 1) * Cw].astype(f32)
+            half = y if k == 1 else 1 - y
+            for i in range(3):
+                r.OC[i, :, wide(q * Cw + Hw * half, Hw)] = rows[:, i * Hw : (i + 1) * Hw].astype(f32)
 
     def tier_out(k):
-        m, tb, o, far = backs[k]
-        lay(k, o, t, m[t])
+        m, tb = backs[k]
+        lay(k, t, m[t])
         got(tb.at[0:3], r.gtr.at[k])
         for d in (1, 2, 3):
-            lay(k, o, t ^ d, tb[t ^ d])
-        give(places_out[k], o, far)
+            lay(k, t ^ d, tb[t ^ d])
 
     def given():
-        for i, (src, dst) in ((0, (r.OU, r.ou)), (2, (r.OA, r.oa)), (3, (r.OD, r.od))):
-            pltpu.make_async_copy(src, dst, r.osem.at[i]).wait()
-        for i, (src, dst) in ((1, (r.OC.at[0:ct], r.oc.at[0:ct])), (7, (r.OC.at[ct:3], r.oc.at[ct:3]))):
+        for i, (src, dst) in ((0, (r.OU, r.ou)), (1, (r.OC, r.oc)), (2, (r.OA, r.oa)), (3, (r.OD, r.od))):
             pltpu.make_async_copy(src, dst, r.osem.at[i]).wait()
         for i, (src, dst) in ((5, (r.OR.at[1], r.out)), (6, (r.IG, r.ig)), (4, (r.OR.at[0], r.om)), (8, (r.OR.at[2], r.ocm))):
             for j in range(nu):
@@ -1247,6 +1296,7 @@
     windows_of = [(q, max(R * q - slots, 0), R - max(slots - R * q, 0)) for q in range(4) if slots < R * (q + 1)]
 
     def new_send():
+        got(r.NEWX, r.ns.at[3])
         for q, at, n in windows_of:
             part = r.NEW.at[t, :, at : at + n]
             if_(t != q, remote(part, part, r.ns.at[0], r.ns.at[1], (b, q)).start)
@@ -1283,7 +1333,8 @@
         for n in parts:
             if n != "U":
                 all_sent(n)
-        got(r.GA.at[:, 0:3], r.xs.at[0])
+        got(r.GA.at[:, 0:3, :, : 3 * Cw], r.xs.at[0])
+        got(r.GA.at[:, 0:3, :, 3 * Cw :], r.xs.at[1])
         for ref, sem in sends:
             got(ref, sem)
         act_sent()
@@ -1295,25 +1346,28 @@
 
     here(r.wd, r.WD.at[b], 0)
     here(r.mem, r.MEMV, 6)
-    for n in ("A", "C", "U"):
+    for n in "ACHU":
         tier_own(n)
     act_own()
     greet(G, True, True)
     tier_start("A")
-    tier_start("C")
+    tier_start("H")
     small_start()
     tier_start("U")
+    tier_start("C")
     act_start(0, 1)
+    got(r.WD.at[b], r.lsem.at[0])
+    own_z("D")
+    own_z("E")
+    own_y("E")
+    own_y("D")
     got(r.MEMV, r.lsem.at[6])
     memory_rows()
     act_start(2, 3, 4, 5, 6)
-    got(r.WD.at[b], r.lsem.at[0])
-    own_z("D")
-    own_y("D")
     tier_wait("A")
     own_z("A")
     own_y("A")
-    tier_wait("C")
+    tier_wait("H")
     own_y("C")
     tier_wait("S")
     own_z("S")
@@ -1325,87 +1379,111 @@
     onward("S", 2)
     tier_wait("U")
     own_z("U")
+    y_wait("E")
+    own_z("F")
     onward("A", 3)
     own_y("U")
     onward("S", 3)
-    y_wait("C")
     onward("U", 1)
     act_forward(0, 1, 2, 3, 4)
     act_wait(0)
     y_wait("A")
     each(S, project, {0: lambda: onward("U", 2), 1: lambda: onward("D", 1, cross=False)})
+    onward("E", 1)
+    tier_wait("C")
+    y_wait("C")
+    each(S, attend, {1: lambda: onward("U", 3)})
+    memory_y()
+    over("D", 1)
+    onward("F", 1)
+    onward("D", 2)
     own_z("C")
-    each(S, attend, {1: lambda: onward("U", 3)})
-    over("D", 1)
+    own_z("X")
     spread_pass(0, 0, r.MIX)
-    each(S, residual, {1: lambda: onward("D", 2)})
-    own_z("X")
+    each(S, residual, {1: lambda: onward("E", 2)})
+    onward("F", 2)
+    onward("D", 3)
     onward("C", 1)
     y_wait("S")
     vectors()
     act_forward(5, 6)
-    onward("D", 3)
     y_wait("U")
     spread_pass(1, 0, r.RES)
-    each(S, feed, {1: lambda: onward("X", 1)})
+    each(S, feed, {0: lambda: onward("X", 1), 2: lambda: onward("E", 3)})
+    memory_come()
+    act_start(7, 8, 9, 10)
+    onward("F", 3)
     act_wait(1)
     act_wait(2)
     onward("C", 2)
     each(4, grad_down, {2: lambda: onward("X", 2)})
     y_wait("D")
-    each(S, back_feed, {0: lambda: onward("C", 3), 1: lambda: mid(0, 0), 2: lambda: onward("X", 3), 3: lambda: mid(0, 1)})
+    all_sent("U")
+    each(
+        S,
+        back_feed,
+        {
+            0: lambda: onward("C", 3),
+            1: lambda: mid(0, 0),
+            2: both(lambda: onward("X", 3), lambda: act_forward(7, 8, 9, 10)),
+            3: at_ends(lambda: mid(0, 1)),
+        },
+    )
+    act_wait(3)
+    act_wait(4)
+    compress()
     fold_pass(2, S - 1)
-    compress()
+    inside(lambda: mid(0, 1))()
+    each(S, out_rows)
     mid_c(0)
     each(4, grad_up)
-    each(G, lambda i: to_y(2, turn(i)))
-    all_sent("U")
-    each(S, back_norm, {2: lambda: mid(0, 2)})
+    mid(0, 2)
+    fold_pass(5, S - 1)
+    each(S, back_norm)
     fold_pass(4, S - 1)
     grad_out()
+    mid_c(1)
     each(S, back_attend, {2: lambda: mid(1, 0)})
+    mid_c(2)
     small_y()
-    each(4, grad_proj, {1: lambda: mid(1, 1)})
-    mid_c(1)
+    new_send()
+    each(4, grad_proj, {1: at_ends(lambda: mid(1, 1))})
+    inside(lambda: mid(1, 1))()
+    at_ends(lambda: mid(1, 2))()
     proj_y(0)
-    mid(1, 2)
-    each(S, out_rows)
+    each(S, input_rows)
     proj_y(1)
-    mid_c(2)
-    fold_pass(5, S - 1)
-    each(S, input_rows)
+    cross_c()
+    fold_pass(6, S - 1)
+    small_z()
+    inside(lambda: mid(1, 2))()
     proj_y(2)
-    fold_pass(6, S - 1)
-    new_send()
-    mid(2, 0)
-    cross_c()
-    proj_y(3)
+    fin_c(hold(mineC))
+    tier_back(1, mineC, r.TC)
     fin(0, keep(r.OD))
     give(3, r.OD, r.od)
-    mid(2, 1)
-    mid(2, 2)
+    mid(3, 0)
+    proj_y(3)
     fin(1, hold(mineU))
     tier_back(0, mineU, r.TU)
-    mid(3, 0)
-    small_z()
+    crossed_c()
+    tier_back(4, r.YC, r.TB)
     each(S, own_out)
     rows_out(5, r.OR.at[1], r.out)
-    mid(3, 1)
-    fin(2, hold(mineB))
-    tier_back(4, mineB, r.TB)
     new_out()
     memories()
     rows_out(4, r.OR.at[0], r.om)
     rows_out(8, r.OR.at[2], r.ocm)
+    mid(3, 1)
+    small_tier()
     mid(3, 2)
-    fin_c(hold(mineC))
-    tier_back(1, mineC, r.TC)
-    small_tier()
     each(S, own_input)
     rows_out(6, r.IG, r.ig)
+    tier_out(1)
+    tier_out(4)
+    give(1, r.OC, r.oc)
     tier_out(0)
-    tier_out(4)
-    tier_out(1)
+    give(0, r.OU, r.ou)
     fin(3, across)
     give(2, r.OA, r.oa)
     small_out()
@@ -1418,8 +1496,7 @@
     G, Cw, Fw, L = nb // 2, M // 4, nb * rd, 64 * nu
     dma = pltpu.SemaphoreType.DMA
     V = lambda shape, dtype=bf16: pltpu.VMEM(shape, dtype)
-    ct = 2
-    D4, A4, U4, C4 = (4, rd // 4, M), (4, rw, 4 * Cw), (4, rw, Fw), (4, rw, 3 * Cw)
+    D4, A4, U4, C4 = (4, rd // 4, M), (4, rw, 4 * Cw), (4, rw, Fw), (4, rw, 3 * Cw // 2)
     ins = arrays
     outs = dict(
         out=((S, R, M), bf16),
@@ -1436,6 +1513,10 @@
         WA=V((nb,) + A4),
         WU=V((nb,) + U4),
         WC=V((nb,) + C4),
+        WCX=V(C4),
+        MEMX=V((S, 12, 16, M)),
+        MKX=V((S, 4, L // 12, 128), f32),
+        NEWX=V((S, L // 3, Cw // 2)),
         WD=V((nb, rd, M)),
         SM=V((nb, 4, 8, 128), f32),
         CTX=V((S, 12 * nu, 16, M)),
@@ -1464,27 +1545,24 @@
         OP=V((S, 4 * nu, 16, M)),
         OR=V((3, S, nu, 16, M)),
         IR=V((3, S, nu, 16, M)),
-        DC=V((S * L // 3, Cw)),
+        DC=V((2, S * L // 3, Cw // 2)),
         GD=V((nb,) + D4),
         GU=V((nb,) + U4),
-        GC=V((nb, 4, rw, ct * Cw)),
-        GB=V((nb, 4, rw, (3 - ct) * Cw)),
+        GC=V((nb,) + C4),
         GA=V((nb,) + A4),
         YD=V((G,) + D4),
         YU=V((G,) + U4),
-        YC=V((4, rw, ct * Cw)),
-        YB=V((G, 4, rw, (3 - ct) * Cw)),
+        YC=V(C4),
         YA=V((G,) + A4),
         ZD=V((4,) + D4),
         ZU=V((4,) + U4),
-        ZC=V((2, 4, 4, rw, ct * Cw)),
-        ZB=V((4, 4, rw, (3 - ct) * Cw)),
+        ZC=V((2, 4) + C4),
         ZA=V((4,) + A4),
         YS=V((24, 128), f32),
         ZS=V((G, 24, 128), f32),
         TU=V(U4),
-        TC=V((4, rw, ct * Cw)),
-        TB=V((4, rw, (3 - ct) * Cw)),
+        TC=V(C4),
+        TB=V(C4),
         NEW=V((4, S, L // 3, Cw)),
         IG=V((S, nu, 16, M), f32),
         OD=V((rd, M), f32),
@@ -1493,28 +1571,29 @@
         OA=V((4, rw, M), f32),
         MEMV=V((S, R, M)),
         osem=dma((9,)),
-        lsem=dma((7,)),
-        ts=dma((4,)),
-        tr=dma((4,)),
-        zs=dma((6,)),
-        zr=dma((9, G - 1)),
-        ys=dma((6,)),
-        yr=dma((6,)),
-        acs=dma((3,)),
-        acc=dma((3,)),
-        acf=dma((3,)),
-        acx=dma((7,)),
+        lsem=dma((8,)),
+        ts=dma((8,)),
+        tr=dma((8,)),
+        zs=dma((8,)),
+        zr=dma((10, G - 1)),
+        ys=dma((8,)),
+        yr=dma((8,)),
+        ms=dma((4,)),
+        acs=dma((5,)),
+        acc=dma((5,)),
+        acf=dma((5,)),
+        acx=dma((11,)),
         es=dma((7,)),
         er=dma((7, S, 2)),
-        ns=dma((2,)),
+        ns=dma((4,)),
         gys=dma((5,)),
         gyr=dma((5, G)),
         gzs=dma((6,)),
         gzr=dma((6, 3)),
         ss=dma((2,)),
         sr=dma((2,)),
-        xs=dma((1,)),
-        xr=dma((G,)),
+        xs=dma((2,)),
+        xr=dma((G + 1,)),
         gts=dma((5,)),
         gtr=dma((5,)),
     )

time: 171 us -> 165 us (0.965)
  Pallas kernels: 170 us -> 163 us
    pallas_call x1, Pallas kernels: 166 us -> 158 us  [whole_layer(): pl.pallas_call(functools.partial(layer_kernel, names, (nb, nu, S, ht, hd,...]
where the time goes in v6:
time: 165 us; the launch traced here: 164 us
  Pallas kernels  163 us (99%)
    pallas_call x1, Pallas kernels, whole_layer(): pl.pallas_call(functools.partial(layer_kernel, names, (nb, nu, S, ht, hd,...  158 us
    pallas_call x1, Pallas kernels, finish(): pl.pallas_call(functools.partial(finish_kernel, list(arrays) + list(outs)...  4.61 us

profile of v6, /device:TPU:11, one launch (start us, length us, event | category | flops | bytes accessed | tf_op | source)
XLA Modules:
  0.0 163.5 jit_solution(18117622948305620187)
XLA Ops:
  0.7 158.1 %whole_layer.1 = (bf16[4,48,1024]{2,1,0:T(8,128)(2,1)}, f32[4,48,1024]{2,1,0:T(8,128)}, bf16[4,48,1024]{2,1,0:T(8,128)(2,1)}, bf16[4,48,1024]{2,1,0:T(8,128)(2,1...) custom-call(bf16[32,1024]{1,0:T(8,128)(2,1)} %refs_0_.1, ...), custom_call_target="tpu_custom_call" | custom-call | tf_op jit(solution)/shard_map/whole_layer/pallas_call | solution.py:1602
  158.7 4.6 %finish.1 = (bf16[4,48,1024]{2,1,0:T(8,128)(2,1)}, f32[4,48,1024]{2,1,0:T(8,128)}, bf16[4,48,1024]{2,1,0:T(8,128)(2,1)}, bf16[4,48,1024]{2,1,0:T(8,128)(2,1)}, f...) custom-call(bf16[4,48,1024]{2,1,0:T(8,128)(2,1)} %get-tuple-element., ...), custom_call_target="tpu_custom_call" | custom-call | tf_op jit(solution)/shard_map/finish/pallas_call | solution.py:1673

commit v7 on v6

--- a/solution.py
+++ b/solution.py
@@ -541,6 +541,7 @@
     nb, nu, S, ht, hd, M, Cw, rw, rd, rs = shape
     R = 16 * nu
     Hw = Cw // 2
+    nd = r.YD.shape[1]
     G, bq = nb // 2, nb // 4
     L = 16 * 4 * nu
     C3 = 3 * L
@@ -626,7 +627,7 @@
     wide = lambda at, size: pl.ds(pl.multiple_of(at, 128), size)
     mats = (r.w_query, r.w_key, r.w_value, r.w_output)
     whole = {"S": r.SM, "A": r.WA, "U": r.WU, "C": r.WC}
-    index = {"S": 0, "A": 1, "U": 2, "C": 3, "H": 7}
+    index = {"S": 0, "A": 1, "U": 2, "C": 3, "H": 4}
 
     def tiers(n, at):
         return r.WCX.at[at] if n == "H" else whole[n].at[b, at]
@@ -811,7 +812,7 @@
         for i, (cut, at, far) in enumerate(pieces):
             if far:
                 for src, dst in cut:
-                    here(src, dst, 4 + group(i))
+                    here(src, dst, 5 + group(i))
 
     def act_start(*which):
         for i in which:
@@ -832,7 +833,7 @@
         got(buf.at[:, 0:n], r.acc.at[g])
         got(buf.at[:, 0:n], r.acf.at[g])
         if g < 2:
-            got(buf.at[:, 0 : n if g else 2 * nu], r.lsem.at[4 + g])
+            got(buf.at[:, 0 : n if g else 2 * nu], r.lsem.at[5 + g])
 
     def act_sent():
         for g, (buf, n) in enumerate(grouped):
@@ -926,11 +927,19 @@
         inner = jnp.where(z == 1, low, G - 1 - low)
         return jnp.where(z == 0, G - 1 - j, jnp.where(z == G - 1, j, inner))
 
-    grads = {0: (r.GD, r.YD, r.ZD), 1: (r.GU, r.YU, r.ZU), 3: (r.WU, r.YA, r.ZA)}
+    grads = {0: (r.GD, r.YD, r.ZD), 1: (r.GU, r.YU, r.ZU), 2: (r.GA, r.YO, r.ZO), 3: (r.WU, r.YA, r.ZA)}
+
+    def block(k, b_):
+        g = grads[k][0]
+        if k == 0:
+            return g.at[b_, 0:nd]
+        if k == 1:
+            return g.at[b_]
+        return g.at[b_, :, :, 3 * Cw :] if k == 2 else g.at[b_, :, :, : 3 * Cw]
 
     def to_y(k, zz):
         g, yb, zb = grads[k]
-        remote(g.at[2 * zz + (1 - y)], yb.at[zz], r.gys.at[k], r.gyr.at[k, zz], ypeer).start()
+        remote(block(k, 2 * zz + (1 - y)), yb.at[zz], r.gys.at[k], r.gyr.at[k, zz], ypeer).start()
 
     def plus(into, *others):
         def add(i):
@@ -952,30 +961,36 @@
         slot = jnp.where(o == mate, 2, jnp.where(ends, lax.rem(o, 2), 3))
         remote(at, zb.at[slot], r.gzs.at[sem], r.gzr.at[sem, jnp.minimum(slot, 2)], (2 * to + y, t)).start()
 
-    straight = ()
-
     def mid(k, *steps):
         g, yb, zb = grads[k]
         for i in steps or range(G - 1):
             o = turn(i)
             at = yb.at[o]
             got(at, r.gyr.at[k, o])
-            plus(at, g.at[2 * o + y])
-            if k in straight:
-                remote(at, zb.at[z], r.gzs.at[k], r.gzr.at[k, 2], (2 * o + y, t)).start()
-            else:
-                pass_on(i, at, zb, o, k)
-
-    def mid_c(*steps):
+            plus(at, block(k, 2 * o + y))
+            pass_on(i, at, zb, o, k)
+
+    def part_c(b_):
+        return r.GC.at[b_]
+
+    def part_e(b_):
+        return r.GD.at[b_, nd:4]
+
+    def along(part, zb, sem, steps):
         for i in steps or range(G - 1):
             o = turn(i)
             for c, col in enumerate((1 - y, y)):
-                pass_on(i, r.GC.at[2 * o + col], r.ZC.at[c], o, 4 + c)
+                pass_on(i, part(2 * o + col), zb.at[c], o, sem + c)
+
+    def mid_c(*steps):
+        along(part_c, r.ZC, 4, steps)
+
+    def mid_e(*steps):
+        along(part_e, r.ZE, 6, steps)
 
     def arrived(zb, sem):
-        n = 3 if sem in straight else 2
-        got(zb.at[4 - n : 4], r.gzr.at[sem, 2])
-        return [zb.at[lax.rem(z + d, G)] for d in range(1, G)] if n == 3 else [zb.at[2], zb.at[3]]
+        got(zb.at[2:4], r.gzr.at[sem, 2])
+        return [zb.at[2], zb.at[3]]
 
     def summed(at, more, store):
         def total(i):
@@ -984,23 +999,36 @@
                 acc = acc + o[i].astype(f32)
             store(i, acc)
 
-        each(4, total)
+        each(at.shape[0], total)
 
     def fin(k, store):
         g, yb, zb = grads[k]
         at = yb.at[z]
         got(at, r.gyr.at[k, z])
-        summed(at, arrived(zb, k) + [g.at[2 * z + y]], store)
+        summed(at, arrived(zb, k) + [block(k, 2 * z + y)], store)
+
+    def cross(part, zb, sem, to, i):
+        other = part(2 * z + 1 - y)
+
+        def store(j, acc):
+            other[j] = acc.astype(bf16)
+
+        summed(other, arrived(zb.at[0], sem), store)
+        remote(other, to, r.gys.at[i], r.gyr.at[i, 0], ypeer).start()
 
     def cross_c():
-        come = arrived(r.ZC.at[0], 4)
-        other = r.GC.at[2 * z + 1 - y]
-
-        def store(i, acc):
-            other[i] = acc.astype(bf16)
-
-        summed(other, come, store)
-        remote(other, r.YC, r.gys.at[4], r.gyr.at[4, 0], ypeer).start()
+        cross(part_c, r.ZC, 4, r.YC, 4)
+
+    def cross_e():
+        cross(part_e, r.ZE, 6, r.YE, 5)
+
+    def fin_e():
+        got(r.YE, r.gyr.at[5, 0])
+
+        def store(j, acc):
+            r.OD[pl.ds((nd + j) * (rd // 4), rd // 4)] = acc
+
+        summed(part_e(2 * z + y), arrived(r.ZE.at[1], 7) + [r.YE], store)
 
     def fin_c(store):
         summed(r.GC.at[2 * z + y], arrived(r.ZC.at[1], 5), store)
@@ -1010,11 +1038,13 @@
 
     def reduced_sent():
         for k, (g, yb, zb) in grads.items():
-            got(g.at[0:G], r.gys.at[k])
-            got(g.at[0:3], r.gzs.at[k])
+            got(block(k, slice(0, G)), r.gys.at[k])
+            got(block(k, slice(0, 3)), r.gzs.at[k])
         got(r.YC, r.gys.at[4])
+        got(r.YE, r.gys.at[5])
         for sem in (4, 5):
             got(r.GC.at[0:3], r.gzs.at[sem])
+            got(r.GD.at[0:3, nd:4], r.gzs.at[sem + 2])
 
     fb = Fw // 4
 
@@ -1104,7 +1134,7 @@
         for q in range(4):
             g = dot_tn(r.MIX[q].reshape(S * L, Cw), r.DB[...].reshape(S * L, Cw))
             r.GA[bq * q : bq * (q + 1), :, :, 3 * Cw :] = g.astype(bf16).reshape(bq, 4, rw, Cw)
-        by_tier(slice(None), slice(3 * Cw, 4 * Cw), r.xs.at[1], r.xr.at[G])
+        each(G, lambda i: to_y(2, turn(i)))
 
     def by_tier(rows, c, sent, come):
         for d in (1, 2, 3):
@@ -1119,7 +1149,6 @@
             o = o + mine * (r.RT[s] + r.VV[2:3, c])
             r.OP[s, :, :, c] = o.astype(bf16).reshape(4 * nu, 16, Cw)
         fold_send(5, s)
-        fold_late(5, s)
 
 
     hc = wide(t * Cw + Hw * y, Hw)
@@ -1192,8 +1221,6 @@
     def proj_y(*steps):
         for i in steps:
             j = turn(i)
-            if i == 0:
-                got(r.WU.at[:, 0:3, :, 3 * Cw :], r.xr.at[G])
             got(r.WU.at[pl.ds(j * bq, bq), 0:3, :, : 3 * Cw], r.xr.at[j])
             to_y(3, j)
 
@@ -1218,7 +1245,7 @@
         return store
 
     def across(q, acc):
-        for i in range(4):
+        for i in range(3):
             r.OA[i, :, wide(q * Cw, Cw)] = acc[:, i * Cw : (i + 1) * Cw]
 
     def hold(m):
@@ -1256,7 +1283,7 @@
     def own_input(s):
         r.IG[s] = folded(6, s)
 
-    mineU, mineC = (g.at[2 * z + y] for g in (r.GU, r.GC))
+    mineU, mineC, mineO = r.GU.at[2 * z + y], r.GC.at[2 * z + y], r.GA.at[2 * z + y, :, :, 3 * Cw :]
     def give(i, src, dst):
         pltpu.make_async_copy(src, dst, r.osem.at[i]).start()
 
@@ -1264,12 +1291,14 @@
         for j in range(nu):
             give(i, src.at[:, j], dst.at[:, 16 * j : 16 * j + 16])
 
-    backs = {0: (mineU, r.TU), 1: (mineC, r.TC), 4: (r.YC, r.TB)}
+    backs = {0: (mineU, r.TU), 1: (mineC, r.TC), 2: (mineO, r.TO), 4: (r.YC, r.TB)}
 
     def lay(k, q, rows):
         if k == 0:
             for i in range(nb):
                 r.OU[:, wide((4 * i + q) * rd, rd)] = rows[:, i * rd : (i + 1) * rd].astype(f32)
+        elif k == 2:
+            r.OA[3, :, wide(q * Cw, Cw)] = rows.astype(f32)
         else:
             half = y if k == 1 else 1 - y
             for i in range(3):
@@ -1334,7 +1363,6 @@
             if n != "U":
                 all_sent(n)
         got(r.GA.at[:, 0:3, :, : 3 * Cw], r.xs.at[0])
-        got(r.GA.at[:, 0:3, :, 3 * Cw :], r.xs.at[1])
         for ref, sem in sends:
             got(ref, sem)
         act_sent()
@@ -1345,7 +1373,7 @@
         given()
 
     here(r.wd, r.WD.at[b], 0)
-    here(r.mem, r.MEMV, 6)
+    here(r.mem, r.MEMV, 7)
     for n in "ACHU":
         tier_own(n)
     act_own()
@@ -1361,7 +1389,7 @@
     own_z("E")
     own_y("E")
     own_y("D")
-    got(r.MEMV, r.lsem.at[6])
+    got(r.MEMV, r.lsem.at[7])
     memory_rows()
     act_start(2, 3, 4, 5, 6)
     tier_wait("A")
@@ -1415,8 +1443,11 @@
     onward("F", 3)
     act_wait(1)
     act_wait(2)
+    each(4, grad_down)
+    mid_e(0)
+    at_ends(both(lambda: mid_e(1), lambda: mid_e(2)))()
     onward("C", 2)
-    each(4, grad_down, {2: lambda: onward("X", 2)})
+    onward("X", 2)
     y_wait("D")
     all_sent("U")
     each(
@@ -1424,29 +1455,33 @@
         back_feed,
         {
             0: lambda: onward("C", 3),
-            1: lambda: mid(0, 0),
+            1: both(inside(lambda: mid_e(1)), lambda: mid(0, 0)),
             2: both(lambda: onward("X", 3), lambda: act_forward(7, 8, 9, 10)),
             3: at_ends(lambda: mid(0, 1)),
         },
     )
+    fold_pass(2, S - 1)
+    each(2, out_rows)
+    inside(both(lambda: mid_e(2), lambda: mid(0, 1)))()
+    fold_pass(5, 0)
+    fold_pass(5, 1)
     act_wait(3)
     act_wait(4)
     compress()
-    fold_pass(2, S - 1)
-    inside(lambda: mid(0, 1))()
-    each(S, out_rows)
     mid_c(0)
     each(4, grad_up)
     mid(0, 2)
-    fold_pass(5, S - 1)
     each(S, back_norm)
     fold_pass(4, S - 1)
     grad_out()
+    each(S - 2, lambda s: out_rows(s + 2))
+    cross_e()
     mid_c(1)
-    each(S, back_attend, {2: lambda: mid(1, 0)})
+    fold_pass(5, 2)
+    fold_pass(5, 3)
+    each(S, back_attend, {0: lambda: mid(1, 0)})
     mid_c(2)
     small_y()
-    new_send()
     each(4, grad_proj, {1: at_ends(lambda: mid(1, 1))})
     inside(lambda: mid(1, 1))()
     at_ends(lambda: mid(1, 2))()
@@ -1455,35 +1490,43 @@
     proj_y(1)
     cross_c()
     fold_pass(6, S - 1)
+    at_ends(lambda: mid(2, 0, 1))()
     small_z()
     inside(lambda: mid(1, 2))()
     proj_y(2)
+    at_ends(both(lambda: mid(2, 2), lambda: mid(3, 0)))()
+    inside(lambda: mid(2, 0, 1, 2))()
     fin_c(hold(mineC))
     tier_back(1, mineC, r.TC)
-    fin(0, keep(r.OD))
-    give(3, r.OD, r.od)
-    mid(3, 0)
     proj_y(3)
+    new_send()
+    inside(lambda: mid(3, 0))()
     fin(1, hold(mineU))
     tier_back(0, mineU, r.TU)
+    mid(3, 1)
+    fin(0, keep(r.OD))
+    fin_e()
+    give(3, r.OD, r.od)
+    fin(2, hold(mineO))
+    tier_back(2, mineO, r.TO)
+    mid(3, 2)
     crossed_c()
     tier_back(4, r.YC, r.TB)
+    small_tier()
     each(S, own_out)
     rows_out(5, r.OR.at[1], r.out)
     new_out()
     memories()
     rows_out(4, r.OR.at[0], r.om)
     rows_out(8, r.OR.at[2], r.ocm)
-    mid(3, 1)
-    small_tier()
-    mid(3, 2)
     each(S, own_input)
     rows_out(6, r.IG, r.ig)
     tier_out(1)
-    tier_out(4)
-    give(1, r.OC, r.oc)
     tier_out(0)
     give(0, r.OU, r.ou)
+    tier_out(4)
+    tier_out(2)
+    give(1, r.OC, r.oc)
     fin(3, across)
     give(2, r.OA, r.oa)
     small_out()
@@ -1496,6 +1539,7 @@
     G, Cw, Fw, L = nb // 2, M // 4, nb * rd, 64 * nu
     dma = pltpu.SemaphoreType.DMA
     V = lambda shape, dtype=bf16: pltpu.VMEM(shape, dtype)
+    nd = 3
     D4, A4, U4, C4 = (4, rd // 4, M), (4, rw, 4 * Cw), (4, rw, Fw), (4, rw, 3 * Cw // 2)
     ins = arrays
     outs = dict(
@@ -1550,17 +1594,22 @@
         GU=V((nb,) + U4),
         GC=V((nb,) + C4),
         GA=V((nb,) + A4),
-        YD=V((G,) + D4),
+        YD=V((G, nd) + D4[1:]),
+        YE=V((4 - nd,) + D4[1:]),
         YU=V((G,) + U4),
         YC=V(C4),
-        YA=V((G,) + A4),
-        ZD=V((4,) + D4),
+        YO=V((G, 4, rw, Cw)),
+        YA=V((G, 4, rw, 3 * Cw)),
+        ZD=V((4, nd) + D4[1:]),
+        ZE=V((2, 4, 4 - nd) + D4[1:]),
         ZU=V((4,) + U4),
         ZC=V((2, 4) + C4),
-        ZA=V((4,) + A4),
+        ZO=V((4, 4, rw, Cw)),
+        ZA=V((4, 4, rw, 3 * Cw)),
         YS=V((24, 128), f32),
         ZS=V((G, 24, 128), f32),
         TU=V(U4),
+        TO=V((4, rw, Cw)),
         TC=V(C4),
         TB=V(C4),
         NEW=V((4, S, L // 3, Cw)),
@@ -1572,8 +1621,8 @@
         MEMV=V((S, R, M)),
         osem=dma((9,)),
         lsem=dma((8,)),
-        ts=dma((8,)),
-        tr=dma((8,)),
+        ts=dma((5,)),
+        tr=dma((5,)),
         zs=dma((8,)),
         zr=dma((10, G - 1)),
         ys=dma((8,)),
@@ -1586,14 +1635,14 @@
         es=dma((7,)),
         er=dma((7, S, 2)),
         ns=dma((4,)),
-        gys=dma((5,)),
-        gyr=dma((5, G)),
-        gzs=dma((6,)),
-        gzr=dma((6, 3)),
+        gys=dma((6,)),
+        gyr=dma((6, G)),
+        gzs=dma((8,)),
+        gzr=dma((8, 3)),
         ss=dma((2,)),
         sr=dma((2,)),
-        xs=dma((2,)),
-        xr=dma((G + 1,)),
+        xs=dma((1,)),
+        xr=dma((G,)),
         gts=dma((5,)),
         gtr=dma((5,)),
     )
@@ -1616,33 +1665,41 @@
     r = Names(names, refs)
     nb, rs, rd, Fw, Cw, heads = shape
     b, t = lax.axis_index("batch"), lax.axis_index("tier")
-    moves = [(r.out, r.o_out), (r.ig, r.o_ig), (r.od, r.o_od), (r.ou, r.o_ou), (r.oc, r.o_oc)]
-    moves += [(r.oa.at[i], o) for i, o in enumerate((r.o_q, r.o_k, r.o_v, r.o_o))]
-    moves += [(r.om, r.o_mem), (r.ocm, r.o_comp)]
+    squares = (r.o_q, r.o_k, r.o_v, r.o_o)
+    moves = [(r.out, r.o_out), (r.ig, r.o_ig), (r.od, r.o_od), (r.ou, r.o_ou), (r.oc, r.o_oc), (r.om, r.o_mem), (r.ocm, r.o_comp)]
+    n = len(moves)
     bufs = refs[len(names) :]
+    small = pltpu.make_async_copy(r.os, r.osv, r.sem.at[n])
+    small.start()
     into = [pltpu.make_async_copy(src, buf, r.sem.at[i]) for i, ((src, _), buf) in enumerate(zip(moves, bufs))]
-    n = len(moves)
-    onto = [pltpu.make_async_copy(buf, dst, r.sem.at[n + i]) for i, ((_, dst), buf) in enumerate(zip(moves, bufs))]
+    into.append(pltpu.make_async_copy(r.oa, bufs[n], r.sem.at[n + 1]))
+    onto = [
+        [pltpu.make_async_copy(buf, dst, r.sem.at[n + 2 + i])] for i, ((_, dst), buf) in enumerate(zip(moves, bufs))
+    ]
+    onto.append([pltpu.make_async_copy(bufs[n].at[i], o, r.sem.at[2 * n + 2 + i]) for i, o in enumerate(squares)])
     for cp in into:
         cp.start()
+    small.wait()
     spot = 4 * b + t
     block, inner = spot // (Cw // rs), lax.rem(spot, Cw // rs)
     half, group = inner // (128 // rs), lax.rem(inner, 128 // rs)
     for i, o in enumerate((r.o_down, r.o_gain, r.o_bias, r.o_conv)):
-        row = r.os[block, pl.ds(Fw // 128 + (Cw // 128) * i + half, 1), :]
+        row = r.osv[block, pl.ds(Fw // 128 + (Cw // 128) * i + half, 1), :]
         turned = pltpu.roll(jnp.broadcast_to(row, (8, 128)), lax.rem(128 - rs * group, 128), 1)
         o[...] = turned[0:1, :rs]
-    r.o_up[...] = r.os[t, pl.ds(b, 1), :rd]
+    r.o_up[...] = r.osv[t, pl.ds(b, 1), :rd]
     at = Fw // 128 + 4 * (Cw // 128)
-    total = r.os[0, at : at + 1]
+    total = r.osv[0, at : at + 1]
     for q in range(1, 4):
-        total = total + r.os[q, at : at + 1]
+        total = total + r.osv[q, at : at + 1]
     r.o_slopes[...] = total[:, :heads]
     for cp, then in zip(into, onto):
         cp.wait()
-        then.start()
-    for cp in onto:
-        cp.wait()
+        for c in then:
+            c.start()
+    for then in onto:
+        for c in then:
+            c.wait()
 
 
 def finish(nb, heads, arrays):
@@ -1669,16 +1726,17 @@
         o_conv=(vec, f32, VM),
         o_slopes=((1, heads), f32, VM),
     )
-    moved = ("o_out", "o_ig", "o_od", "o_ou", "o_oc", "o_q", "o_k", "o_v", "o_o", "o_mem", "o_comp")
+    moved = ("out", "ig", "od", "ou", "oc", "om", "ocm", "oa")
+    n = len(moved) - 1
     return pl.pallas_call(
         functools.partial(
-            finish_kernel, list(arrays) + list(outs) + ["sem"], (nb, rs, rd, Fw, Cw, heads)
+            finish_kernel, list(arrays) + list(outs) + ["sem", "osv"], (nb, rs, rd, Fw, Cw, heads)
         ),
         out_shape=[jax.ShapeDtypeStruct(s, d) for s, d, _ in outs.values()],
-        in_specs=[VM if n == "os" else ANY for n in arrays],
+        in_specs=[ANY] * len(arrays),
         out_specs=[o[2] for o in outs.values()],
-        scratch_shapes=[pltpu.SemaphoreType.DMA((2 * len(moved),))]
-        + [pltpu.VMEM(outs[n][0], outs[n][1]) for n in moved],
+        scratch_shapes=[pltpu.SemaphoreType.DMA((2 * n + 6,)), pltpu.VMEM(arrays["os"].shape, f32)]
+        + [pltpu.VMEM(arrays[i].shape, arrays[i].dtype) for i in moved],
         compiler_params=pltpu.CompilerParams(vmem_limit_bytes=63 * 2**20),
         name="finish",
     )(*arrays.values())

time: 165 us -> 157 us (0.952)
  Pallas kernels: 163 us -> 155 us
    pallas_call x1, Pallas kernels: 158 us -> 151 us  [whole_layer(): pl.pallas_call(functools.partial(layer_kernel, names, (nb, nu, S, ht, hd,...]
where the time goes in v7:
time: 157 us; the launch traced here: 156 us
  Pallas kernels  155 us (99%)
    pallas_call x1, Pallas kernels, whole_layer(): pl.pallas_call(functools.partial(layer_kernel, names, (nb, nu, S, ht, hd,...  151 us
    pallas_call x1, Pallas kernels, finish(): pl.pallas_call(functools.partial(finish_kernel, list(arrays) + list(outs)...  3.86 us

profile of v7, /device:TPU:11, one launch (start us, length us, event | category | flops | bytes accessed | tf_op | source)
XLA Modules:
  0.0 155.5 jit_solution(10032868829325410873)
XLA Ops:
  0.7 150.8 %whole_layer.1 = (bf16[4,48,1024]{2,1,0:T(8,128)(2,1)}, f32[4,48,1024]{2,1,0:T(8,128)}, bf16[4,48,1024]{2,1,0:T(8,128)(2,1)}, bf16[4,48,1024]{2,1,0:T(8,128)(2,1...) custom-call(bf16[32,1024]{1,0:T(8,128)(2,1)} %refs_0_.1, ...), custom_call_target="tpu_custom_call" | custom-call | tf_op jit(solution)/shard_map/whole_layer/pallas_call | solution.py:1651
  151.5 3.9 %finish.1 = (bf16[4,48,1024]{2,1,0:T(8,128)(2,1)}, f32[4,48,1024]{2,1,0:T(8,128)}, bf16[4,48,1024]{2,1,0:T(8,128)(2,1)}, bf16[4,48,1024]{2,1,0:T(8,128)(2,1)}, f...) custom-call(bf16[4,48,1024]{2,1,0:T(8,128)(2,1)} %get-tuple-element., ...), custom_call_target="tpu_custom_call" | custom-call | tf_op jit(solution)/shard_map/finish/pallas_call | solution.py:1731

commit v8 on v7

--- a/solution.py
+++ b/solution.py
@@ -683,8 +683,11 @@
     parts = {"S": [(r.SM, 0, 0, 4, 0)], "C": [(r.WC, 1, 0, 4, 1)], "X": [(r.WC, 2, 0, 4, 2)]}
     for i, (n, w) in enumerate((("A", r.WA), ("U", r.WU))):
         parts[n] = [(w, 3 + 2 * i + h, h * 2, 2, 3 + i) for h in (0, 1)]
-    for i, (n, at) in enumerate((("D", 0), ("E", rd // 2), ("F", rd // 2))):
-        parts[n] = [(r.WD, 7 + i, at, rd // 2, 5 + i)]
+    first = rd // 4
+    rest = (rd - first) // 2
+    parts["D"] = [(r.WD, 7, 0, first, 5)]
+    for i, n in enumerate("EF"):
+        parts[n] = [(r.WD, 8 + 2 * i + h, first + h * rest, rest, 6 + i) for h in (0, 1)]
 
     def chunk_of(n, part, zz, col=None):
         w, k, at, size, _ = part
@@ -1417,46 +1420,48 @@
     act_wait(0)
     y_wait("A")
     each(S, project, {0: lambda: onward("U", 2), 1: lambda: onward("D", 1, cross=False)})
-    onward("E", 1)
+    inside(lambda: onward("E", 1))()
+    inside(lambda: onward("F", 1))()
     tier_wait("C")
     y_wait("C")
-    each(S, attend, {1: lambda: onward("U", 3)})
+    each(S, attend)
+    onward("U", 3)
     memory_y()
     over("D", 1)
-    onward("F", 1)
     onward("D", 2)
     own_z("C")
     own_z("X")
     spread_pass(0, 0, r.MIX)
-    each(S, residual, {1: lambda: onward("E", 2)})
-    onward("F", 2)
-    onward("D", 3)
-    onward("C", 1)
+    each(S, residual)
+    inside(lambda: onward("E", 2))()
+    inside(lambda: onward("F", 2))()
     y_wait("S")
     vectors()
     act_forward(5, 6)
+    onward("D", 3)
     y_wait("U")
     spread_pass(1, 0, r.RES)
-    each(S, feed, {0: lambda: onward("X", 1), 2: lambda: onward("E", 3)})
+    each(S, feed, {0: inside(lambda: onward("C", 1)), 1: inside(lambda: onward("E", 3)), 2: inside(lambda: onward("X", 1))})
     memory_come()
     act_start(7, 8, 9, 10)
-    onward("F", 3)
     act_wait(1)
     act_wait(2)
     each(4, grad_down)
     mid_e(0)
     at_ends(both(lambda: mid_e(1), lambda: mid_e(2)))()
-    onward("C", 2)
-    onward("X", 2)
+    inside(lambda: onward("F", 3))()
+    inside(lambda: onward("C", 2))()
+    inside(lambda: onward("X", 2))()
+    at_ends(both(lambda: onward("E"), lambda: onward("F")))()
     y_wait("D")
     all_sent("U")
     each(
         S,
         back_feed,
         {
-            0: lambda: onward("C", 3),
+            0: inside(lambda: onward("C", 3)),
             1: both(inside(lambda: mid_e(1)), lambda: mid(0, 0)),
-            2: both(lambda: onward("X", 3), lambda: act_forward(7, 8, 9, 10)),
+            2: both(inside(lambda: onward("X", 3)), lambda: act_forward(7, 8, 9, 10)),
             3: at_ends(lambda: mid(0, 1)),
         },
     )
@@ -1467,6 +1472,7 @@
     fold_pass(5, 1)
     act_wait(3)
     act_wait(4)
+    at_ends(both(lambda: onward("C"), lambda: onward("X")))()
     compress()
     mid_c(0)
     each(4, grad_up)
@@ -1491,11 +1497,11 @@
     cross_c()
     fold_pass(6, S - 1)
     at_ends(lambda: mid(2, 0, 1))()
-    small_z()
     inside(lambda: mid(1, 2))()
     proj_y(2)
     at_ends(both(lambda: mid(2, 2), lambda: mid(3, 0)))()
     inside(lambda: mid(2, 0, 1, 2))()
+    small_z()
     fin_c(hold(mineC))
     tier_back(1, mineC, r.TC)
     proj_y(3)
@@ -1624,7 +1630,7 @@
         ts=dma((5,)),
         tr=dma((5,)),
         zs=dma((8,)),
-        zr=dma((10, G - 1)),
+        zr=dma((12, G - 1)),
         ys=dma((8,)),
         yr=dma((8,)),
         ms=dma((4,)),

time: 157 us -> 155 us (0.987)
  Pallas kernels: 155 us -> 151 us
    pallas_call x1, Pallas kernels: 151 us -> 147 us  [whole_layer(): pl.pallas_call(functools.partial(layer_kernel, names, (nb, nu, S, ht, hd,...]
where the time goes in v8:
time: 155 us; the launch traced here: 152 us
  Pallas kernels  151 us (97%)
    pallas_call x1, Pallas kernels, whole_layer(): pl.pallas_call(functools.partial(layer_kernel, names, (nb, nu, S, ht, hd,...  147 us
    pallas_call x1, Pallas kernels, finish(): pl.pallas_call(functools.partial(finish_kernel, list(arrays) + list(outs)...  3.86 us

profile of v8, /device:TPU:11, one launch (start us, length us, event | category | flops | bytes accessed | tf_op | source)
XLA Modules:
  0.0 152.0 jit_solution(5802356693278327480)
XLA Ops:
  0.7 147.3 %whole_layer.1 = (bf16[4,48,1024]{2,1,0:T(8,128)(2,1)}, f32[4,48,1024]{2,1,0:T(8,128)}, bf16[4,48,1024]{2,1,0:T(8,128)(2,1)}, bf16[4,48,1024]{2,1,0:T(8,128)(2,1...) custom-call(bf16[32,1024]{1,0:T(8,128)(2,1)} %refs_0_.1, ...), custom_call_target="tpu_custom_call" | custom-call | tf_op jit(solution)/shard_map/whole_layer/pallas_call | solution.py:1657
  148.0 3.9 %finish.1 = (bf16[4,48,1024]{2,1,0:T(8,128)(2,1)}, f32[4,48,1024]{2,1,0:T(8,128)}, bf16[4,48,1024]{2,1,0:T(8,128)(2,1)}, bf16[4,48,1024]{2,1,0:T(8,128)(2,1)}, f...) custom-call(bf16[4,48,1024]{2,1,0:T(8,128)(2,1)} %get-tuple-element., ...), custom_call_target="tpu_custom_call" | custom-call | tf_op jit(solution)/shard_map/finish/pallas_call | solution.py:1737

commit v9 on v8

--- a/solution.py
+++ b/solution.py
@@ -1278,10 +1278,10 @@
         acc = r.ZS[0]
         for zz in range(1, G):
             acc = acc + r.ZS[zz]
-        r.os[t] = acc
+        r.OS[t] = acc
         for d in (1, 2, 3):
-            remote(r.os.at[t], r.os.at[t], r.gts.at[3], r.gtr.at[3], (b, t ^ d)).start()
-        left_all(r.os.at[0:3], r.gts.at[3])
+            remote(r.OS.at[t], r.OS.at[t], r.gts.at[3], r.gtr.at[3], (b, t ^ d)).start()
+        left_all(r.OS.at[0:3], r.gts.at[3])
 
     def own_input(s):
         r.IG[s] = folded(6, s)
@@ -1315,14 +1315,15 @@
             lay(k, t ^ d, tb[t ^ d])
 
     def given():
-        for i, (src, dst) in ((0, (r.OU, r.ou)), (1, (r.OC, r.oc)), (2, (r.OA, r.oa)), (3, (r.OD, r.od))):
+        for i, (src, dst) in ((0, (r.OU, r.ou)), (1, (r.OC, r.oc)), (2, (r.OA, r.oa)), (3, (r.OD, r.od)), (7, (r.OS, r.os))):
             pltpu.make_async_copy(src, dst, r.osem.at[i]).wait()
         for i, (src, dst) in ((5, (r.OR.at[1], r.out)), (6, (r.IG, r.ig)), (4, (r.OR.at[0], r.om)), (8, (r.OR.at[2], r.ocm))):
             for j in range(nu):
                 pltpu.make_async_copy(src.at[:, j], dst.at[:, 16 * j : 16 * j + 16], r.osem.at[i]).wait()
 
     def small_out():
-        got(r.os.at[0:3], r.gtr.at[3])
+        got(r.OS.at[0:3], r.gtr.at[3])
+        give(7, r.OS, r.os)
 
     slots = L - nw
     windows_of = [(q, max(R * q - slots, 0), R - max(slots - R * q, 0)) for q in range(4) if slots < R * (q + 1)]
@@ -1370,10 +1371,8 @@
             got(ref, sem)
         act_sent()
         new_sent()
-        reduced_sent()
         for e, ref in enumerate((r.MIX, r.RES, r.DNP, r.ST, r.DMP, r.OR, r.IR)):
             got(ref.at[0:3], r.es.at[e])
-        given()
 
     here(r.wd, r.WD.at[b], 0)
     here(r.mem, r.MEMV, 7)
@@ -1467,26 +1466,30 @@
     )
     fold_pass(2, S - 1)
     each(2, out_rows)
-    inside(both(lambda: mid_e(2), lambda: mid(0, 1)))()
+    each(4, grad_up)
     fold_pass(5, 0)
     fold_pass(5, 1)
+    inside(both(lambda: mid_e(2), lambda: mid(0, 1)))()
+    at_ends(lambda: mid(0, 2))()
     act_wait(3)
     act_wait(4)
     at_ends(both(lambda: onward("C"), lambda: onward("X")))()
     compress()
+    inside(lambda: mid(0, 2))()
     mid_c(0)
-    each(4, grad_up)
-    mid(0, 2)
+    at_ends(lambda: mid_c(1))()
     each(S, back_norm)
     fold_pass(4, S - 1)
     grad_out()
     each(S - 2, lambda s: out_rows(s + 2))
     cross_e()
-    mid_c(1)
+    inside(lambda: mid_c(1))()
     fold_pass(5, 2)
     fold_pass(5, 3)
-    each(S, back_attend, {0: lambda: mid(1, 0)})
-    mid_c(2)
+    mid(1, 0)
+    at_ends(lambda: mid_c(2))()
+    each(S, back_attend)
+    inside(lambda: mid_c(2))()
     small_y()
     each(4, grad_proj, {1: at_ends(lambda: mid(1, 1))})
     inside(lambda: mid(1, 1))()
@@ -1510,14 +1513,14 @@
     fin(1, hold(mineU))
     tier_back(0, mineU, r.TU)
     mid(3, 1)
+    crossed_c()
+    tier_back(4, r.YC, r.TB)
     fin(0, keep(r.OD))
     fin_e()
     give(3, r.OD, r.od)
     fin(2, hold(mineO))
     tier_back(2, mineO, r.TO)
     mid(3, 2)
-    crossed_c()
-    tier_back(4, r.YC, r.TB)
     small_tier()
     each(S, own_out)
     rows_out(5, r.OR.at[1], r.out)
@@ -1533,10 +1536,12 @@
     tier_out(4)
     tier_out(2)
     give(1, r.OC, r.oc)
+    small_out()
+    drain()
     fin(3, across)
     give(2, r.OA, r.oa)
-    small_out()
-    drain()
+    reduced_sent()
+    given()
 
 def whole_layer(nb, ht, hd, arrays):
     S, R, M = arrays["seg"].shape
@@ -1624,6 +1629,7 @@
         OU=V((rw, 4 * Fw), f32),
         OC=V((3, rw, M), f32),
         OA=V((4, rw, M), f32),
+        OS=V((4, 24, 128), f32),
         MEMV=V((S, R, M)),
         osem=dma((9,)),
         lsem=dma((8,)),
@@ -1658,7 +1664,7 @@
         functools.partial(layer_kernel, names, (nb, nu, S, ht, hd, M, Cw, rw, rd, rs)),
         out_shape=[jax.ShapeDtypeStruct(s, d) for s, d in outs.values()],
         in_specs=[near.get(n, ANY) for n in ins],
-        out_specs=[VM if n == "os" else ANY for n in outs],
+        out_specs=[ANY] * len(outs),
         scratch_shapes=list(scratch.values()),
         compiler_params=pltpu.CompilerParams(
             collective_id=9, has_side_effects=True, vmem_limit_bytes=63 * 2**20
@@ -1689,16 +1695,21 @@
     spot = 4 * b + t
     block, inner = spot // (Cw // rs), lax.rem(spot, Cw // rs)
     half, group = inner // (128 // rs), lax.rem(inner, 128 // rs)
-    for i, o in enumerate((r.o_down, r.o_gain, r.o_bias, r.o_conv)):
+    for i in range(4):
         row = r.osv[block, pl.ds(Fw // 128 + (Cw // 128) * i + half, 1), :]
         turned = pltpu.roll(jnp.broadcast_to(row, (8, 128)), lax.rem(128 - rs * group, 128), 1)
-        o[...] = turned[0:1, :rs]
-    r.o_up[...] = r.osv[t, pl.ds(b, 1), :rd]
+        r.vecs[i : i + 1, :] = turned[0:1, :rs]
+    r.ups[...] = r.osv[t, pl.ds(b, 1), :rd]
     at = Fw // 128 + 4 * (Cw // 128)
     total = r.osv[0, at : at + 1]
     for q in range(1, 4):
         total = total + r.osv[q, at : at + 1]
-    r.o_slopes[...] = total[:, :heads]
+    r.slope[...] = total[:, :heads]
+    lines = [(r.vecs.at[i : i + 1], o) for i, o in enumerate((r.o_down, r.o_gain, r.o_bias, r.o_conv))]
+    lines += [(r.ups, r.o_up), (r.slope, r.o_slopes)]
+    onto.append([pltpu.make_async_copy(src, dst, r.sem.at[2 * n + 6 + i]) for i, (src, dst) in enumerate(lines)])
+    for c in onto[-1]:
+        c.start()
     for cp, then in zip(into, onto):
         cp.wait()
         for c in then:
@@ -1723,25 +1734,31 @@
         o_v=(mat, f32, ANY),
         o_o=(mat, f32, ANY),
         o_ou=((rw, 4 * Fw), f32, ANY),
-        o_up=((1, rd), f32, VM),
+        o_up=((1, rd), f32, ANY),
         o_od=((rd, M), f32, ANY),
-        o_down=(vec, f32, VM),
-        o_gain=(vec, f32, VM),
-        o_bias=(vec, f32, VM),
+        o_down=(vec, f32, ANY),
+        o_gain=(vec, f32, ANY),
+        o_bias=(vec, f32, ANY),
         o_oc=((3, rw, M), f32, ANY),
-        o_conv=(vec, f32, VM),
-        o_slopes=((1, heads), f32, VM),
+        o_conv=(vec, f32, ANY),
+        o_slopes=((1, heads), f32, ANY),
     )
     moved = ("out", "ig", "od", "ou", "oc", "om", "ocm", "oa")
     n = len(moved) - 1
     return pl.pallas_call(
         functools.partial(
-            finish_kernel, list(arrays) + list(outs) + ["sem", "osv"], (nb, rs, rd, Fw, Cw, heads)
+            finish_kernel, list(arrays) + list(outs) + ["sem", "osv", "vecs", "ups", "slope"], (nb, rs, rd, Fw, Cw, heads)
         ),
         out_shape=[jax.ShapeDtypeStruct(s, d) for s, d, _ in outs.values()],
         in_specs=[ANY] * len(arrays),
         out_specs=[o[2] for o in outs.values()],
-        scratch_shapes=[pltpu.SemaphoreType.DMA((2 * n + 6,)), pltpu.VMEM(arrays["os"].shape, f32)]
+        scratch_shapes=[
+            pltpu.SemaphoreType.DMA((2 * n + 12,)),
+            pltpu.VMEM(arrays["os"].shape, f32),
+            pltpu.VMEM((4, rs), f32),
+            pltpu.VMEM((1, rd), f32),
+            pltpu.VMEM((1, heads), f32),
+        ]
         + [pltpu.VMEM(arrays[i].shape, arrays[i].dtype) for i in moved],
         compiler_params=pltpu.CompilerParams(vmem_limit_bytes=63 * 2**20),
         name="finish",

time: 155 us -> 151 us (0.974); the launches traced: 152 us -> 151 us
  no operation moved by 1% of the time
where the time goes in v9:
time: 151 us
  Pallas kernels  150 us (99%)
    pallas_call x1, Pallas kernels, whole_layer(): pl.pallas_call(functools.partial(layer_kernel, names, (nb, nu, S, ht, hd,...  146 us
    pallas_call x1, Pallas kernels, finish(): pl.pallas_call(functools.partial(finish_kernel, list(arrays) + list(outs)...  3.42 us

profile of v9, /device:TPU:11, one launch (start us, length us, event | category | flops | bytes accessed | tf_op | source)
XLA Modules:
  0.0 150.7 jit_solution(1620825839468159252)
XLA Ops:
  0.7 146.4 %whole_layer.1 = (bf16[4,48,1024]{2,1,0:T(8,128)(2,1)}, f32[4,48,1024]{2,1,0:T(8,128)}, bf16[4,48,1024]{2,1,0:T(8,128)(2,1)}, bf16[4,48,1024]{2,1,0:T(8,128)(2,1...) custom-call(bf16[32,1024]{1,0:T(8,128)(2,1)} %refs_0_.1, ...), custom_call_target="tpu_custom_call" | custom-call | tf_op jit(solution)/shard_map/whole_layer/pallas_call | solution.py:1663
  147.1 3.4 %finish.1 = (bf16[4,48,1024]{2,1,0:T(8,128)(2,1)}, f32[4,48,1024]{2,1,0:T(8,128)}, bf16[4,48,1024]{2,1,0:T(8,128)(2,1)}, bf16[4,48,1024]{2,1,0:T(8,128)(2,1)}, f...) custom-call(bf16[4,48,1024]{2,1,0:T(8,128)(2,1)} %get-tuple-element., ...), custom_call_target="tpu_custom_call" | custom-call | tf_op jit(solution)/shard_map/finish/pallas_call | solution.py:1748

commit v10 on v9

--- a/solution.py
+++ b/solution.py
@@ -680,7 +680,7 @@
         return run
 
     right, left = (2 * z + 2 + y, t), (2 * z - 2 + y, t)
-    parts = {"S": [(r.SM, 0, 0, 4, 0)], "C": [(r.WC, 1, 0, 4, 1)], "X": [(r.WC, 2, 0, 4, 2)]}
+    parts = {"S": [(r.SM, 0, t, 1, 0)], "C": [(r.WC, 1, 0, 4, 1)], "X": [(r.WC, 2, 0, 4, 2)]}
     for i, (n, w) in enumerate((("A", r.WA), ("U", r.WU))):
         parts[n] = [(w, 3 + 2 * i + h, h * 2, 2, 3 + i) for h in (0, 1)]
     first = rd // 4
@@ -696,7 +696,7 @@
 
     def chunks(n, count):
         w, _, at, size, _ = parts[n][0]
-        return w.at[0:count, at : at + size * len(parts[n])]
+        return w.at[0:count, pl.ds(at, size * len(parts[n]))]
 
     def hop(part, at, zz, way):
         k = part[1]
@@ -757,7 +757,14 @@
         r.SM[b, t] = jnp.zeros((8, 128), f32)
         for q, v in enumerate((r.gain, r.bias, r.bdown, r.bconv, r.bup)):
             r.SM[b, t, q : q + 1, : v.shape[1]] = v[...].astype(f32)
-        tier_start("S")
+
+    def small_spread():
+        for d in (1, 2, 3):
+            remote(r.SM.at[:, t], r.SM.at[:, t], r.ts.at[0], r.tr.at[0], (b, t ^ d)).start()
+        left_all(r.SM.at[:, 0:3], r.ts.at[0])
+
+    def small_come():
+        got(r.SM.at[:, 0:3], r.tr.at[0])
 
     def memory_rows():
         W = R // 3
@@ -1384,7 +1391,6 @@
     tier_start("H")
     small_start()
     tier_start("U")
-    tier_start("C")
     act_start(0, 1)
     got(r.WD.at[b], r.lsem.at[0])
     own_z("D")
@@ -1393,13 +1399,14 @@
     own_y("D")
     got(r.MEMV, r.lsem.at[7])
     memory_rows()
-    act_start(2, 3, 4, 5, 6)
+    act_start(2, 3, 4)
+    tier_start("C")
+    act_start(5, 6)
     tier_wait("A")
     own_z("A")
     own_y("A")
     tier_wait("H")
     own_y("C")
-    tier_wait("S")
     own_z("S")
     own_y("S")
     table()
@@ -1418,11 +1425,14 @@
     act_forward(0, 1, 2, 3, 4)
     act_wait(0)
     y_wait("A")
-    each(S, project, {0: lambda: onward("U", 2), 1: lambda: onward("D", 1, cross=False)})
+    each(S, project, {0: inside(lambda: onward("U", 2)), 1: inside(lambda: onward("D", 1, cross=False))})
+    at_ends(both(lambda: onward("U", 2), lambda: onward("D", 1, cross=False)))()
     inside(lambda: onward("E", 1))()
     inside(lambda: onward("F", 1))()
     tier_wait("C")
     y_wait("C")
+    y_wait("S")
+    small_spread()
     each(S, attend)
     onward("U", 3)
     memory_y()
@@ -1434,7 +1444,7 @@
     each(S, residual)
     inside(lambda: onward("E", 2))()
     inside(lambda: onward("F", 2))()
-    y_wait("S")
+    small_come()
     vectors()
     act_forward(5, 6)
     onward("D", 3)
@@ -1445,9 +1455,11 @@
     act_start(7, 8, 9, 10)
     act_wait(1)
     act_wait(2)
-    each(4, grad_down)
-    mid_e(0)
-    at_ends(both(lambda: mid_e(1), lambda: mid_e(2)))()
+    each(
+        4,
+        grad_down,
+        {0: lambda: mid_e(0), 1: at_ends(lambda: mid_e(1)), 2: at_ends(lambda: mid_e(2))},
+    )
     inside(lambda: onward("F", 3))()
     inside(lambda: onward("C", 2))()
     inside(lambda: onward("X", 2))()

time: 151 us -> 150 us (level)
  Pallas kernels: 150 us -> 148 us
    pallas_call x1, Pallas kernels: 146 us -> 144 us  [whole_layer(): pl.pallas_call(functools.partial(layer_kernel, names, (nb, nu, S, ht, hd,...]
where the time goes in v10:
time: 150 us; the launch traced here: 149 us
  Pallas kernels  148 us (99%)
    pallas_call x1, Pallas kernels, whole_layer(): pl.pallas_call(functools.partial(layer_kernel, names, (nb, nu, S, ht, hd,...  144 us
    pallas_call x1, Pallas kernels, finish(): pl.pallas_call(functools.partial(finish_kernel, list(arrays) + list(outs)...  3.42 us

profile of v10, /device:TPU:11, one launch (start us, length us, event | category | flops | bytes accessed | tf_op | source)
XLA Modules:
  0.0 148.6 jit_solution(2361962971951402327)
XLA Ops:
  0.7 144.4 %whole_layer.1 = (bf16[4,48,1024]{2,1,0:T(8,128)(2,1)}, f32[4,48,1024]{2,1,0:T(8,128)}, bf16[4,48,1024]{2,1,0:T(8,128)(2,1)}, bf16[4,48,1024]{2,1,0:T(8,128)(2,1...) custom-call(bf16[32,1024]{1,0:T(8,128)(2,1)} %refs_0_.1, ...), custom_call_target="tpu_custom_call" | custom-call | tf_op jit(solution)/shard_map/whole_layer/pallas_call | solution.py:1675
  145.1 3.4 %finish.1 = (bf16[4,48,1024]{2,1,0:T(8,128)(2,1)}, f32[4,48,1024]{2,1,0:T(8,128)}, bf16[4,48,1024]{2,1,0:T(8,128)(2,1)}, bf16[4,48,1024]{2,1,0:T(8,128)(2,1)}, f...) custom-call(bf16[4,48,1024]{2,1,0:T(8,128)(2,1)} %get-tuple-element., ...), custom_call_target="tpu_custom_call" | custom-call | tf_op jit(solution)/shard_map/finish/pallas_call | solution.py:1760
